TPU v7x, 32 devices: a whole 2x2x4 slice. The times are simulated.
32 devices in a mesh: rep: 4 (over y, x), fsdp: 4 (over z), seq: 2 (over core).
Axes of the slice: x: 2, y: 2, z: 4, core: 2. Of those that a mesh axis runs over, the one named last changes fastest.
Arguments:
- block_input: bfloat16 [4096, 1024], P(('rep', 'fsdp', 'seq')), may hold values from -6 to 6
- ln1_gain: bfloat16 [1024], P('fsdp'), may hold values from 0.5 to 1.5
- ln1_shift: bfloat16 [1024], P('fsdp'), may hold values from -1 to 1
- qkv_weight: bfloat16 [1024, 3072], P('fsdp'), may hold values from -0.1875 to 0.1875
- qv_bias: bfloat16 [2048], P('fsdp'), may hold values from -1 to 1
- proj_weight: bfloat16 [1024, 1024], P('fsdp'), may hold values from -0.75 to 0.75
- proj_bias: bfloat16 [1024], P('fsdp'), may hold values from -1 to 1
- ln2_gain: bfloat16 [1024], P('fsdp'), may hold values from 0.5 to 1.5
- ln2_shift: bfloat16 [1024], P('fsdp'), may hold values from -1 to 1
- fc_weight: bfloat16 [4096, 1024], P('fsdp'), may hold values from -0.1875 to 0.1875
- fc_bias: bfloat16 [4096], P('fsdp'), may hold values from -1 to 1
- out_weight: bfloat16 [4096, 1024], P('fsdp'), may hold values from -0.09375 to 0.09375
- out_bias: bfloat16 [1024], P('fsdp'), may hold values from -1 to 1
- cotangent: bfloat16 [4096, 1024], P(('rep', 'fsdp', 'seq')), may hold values from -6 to 6
Outputs:
- block_output: bfloat16 [4096, 1024], P(('rep', 'fsdp', 'seq'))
- input_grad: float32 [4096, 1024], P(('rep', 'fsdp', 'seq'))
- ln1_gain_grad: float32 [1024], P('fsdp')
- ln1_shift_grad: float32 [1024], P('fsdp')
- qkv_weight_grad: float32 [1024, 3072], P('fsdp')
- qv_bias_grad: float32 [2048], P('fsdp')
- proj_weight_grad: float32 [1024, 1024], P('fsdp')
- proj_bias_grad: float32 [1024], P('fsdp')
- ln2_gain_grad: float32 [1024], P('fsdp')
- ln2_shift_grad: float32 [1024], P('fsdp')
- fc_weight_grad: float32 [4096, 1024], P('fsdp')
- fc_bias_grad: float32 [4096], P('fsdp')
- out_weight_grad: float32 [4096, 1024], P('fsdp')
- out_bias_grad: float32 [1024], P('fsdp')
All inputs are finite; a program needn't handle non-finite values.
Results may differ from a plain program's by a relative error of at most 0.019.
Values may be sent and summed in bfloat16 or wider, within the bound.
No kernel may reach another device: no remote copies, remote signals or barrier semaphores. Data moves between devices by JAX's collectives and lax.ppermute only.
A program may use at most 192 MiB of HBM per device.

v0:
```python
import math

import jax
import jax.numpy as jnp
from jax import lax
from jax.experimental import pallas as pl
from jax.experimental.pallas import tpu as pltpu
from jax.sharding import PartitionSpec as P

HEADS = 16
HEAD_DIM = 64

norm_eps = 1e-05
masked_value = -1e30
f32 = jnp.float32
bf16 = jnp.bfloat16

REPS, SHARDS, CORES = 4, 4, 2
LANE, ROWS, WIDTH, SHARD, TRIPLE, HIDDEN = 128, 128, 1024, 256, 384, 1024
SCALE = HEAD_DIM ** (-0.5)


def normalise(values):
    centre = jnp.mean(values, -1, keepdims=True)
    offsets = values - centre
    spread = jnp.mean(offsets * offsets, -1, keepdims=True)
    scale = lax.rsqrt(spread + norm_eps)
    return offsets * scale, scale


def norm_pull(unit, scale, gain, grad):
    inner = grad * gain
    first = jnp.mean(inner, -1, keepdims=True)
    second = jnp.mean(inner * unit, -1, keepdims=True)
    return scale * (inner - first - unit * second), jnp.sum(grad * unit, 0), jnp.sum(grad, 0)


def gelu_and_slope(values):
    rate = 0.7978845608028654
    squared = values * values
    bent = jnp.tanh(rate * (values + 0.044715 * values * squared))
    half = 0.5 * (1.0 + bent)
    slope = half + 0.5 * values * (1.0 - bent * bent) * (rate * (1.0 + 3.0 * 0.044715 * squared))
    return values * half, slope


def contract(left, right, left_axis, right_axis):
    return lax.dot_general(
        left, right, (((left_axis,), (right_axis,)), ((), ())), preferred_element_type=f32
    )


def swap(value, axis, size, offset):
    return lax.ppermute(value, axis, [(i, i ^ offset) for i in range(size)])


def pick(array, index, axis):
    return lax.dynamic_index_in_dim(array, index, axis, keepdims=False)


def place(pieces, positions):
    stacked = jnp.zeros((len(pieces),) + pieces[0].shape, pieces[0].dtype)
    for piece, position in zip(pieces, positions):
        stacked = lax.dynamic_update_index_in_dim(stacked, piece, position, 0)
    return stacked


def lanes(start, size):
    return pl.ds(pl.multiple_of(start, LANE), size)


def vmem_call(kernel, outs, args, hbm=(), scratch=(), flops=0):
    moved = sum(a.size * a.dtype.itemsize for a in args)
    moved += sum(math.prod(s) * jnp.dtype(t).itemsize for s, t in outs)
    whole = pl.BlockSpec(memory_space=pltpu.VMEM)
    return pl.pallas_call(
        kernel,
        out_shape=[jax.ShapeDtypeStruct(s, t) for s, t in outs],
        in_specs=[
            pl.BlockSpec(memory_space=pl.ANY) if i in hbm else whole for i in range(len(args))
        ],
        out_specs=[whole] * len(outs),
        scratch_shapes=list(scratch),
        compiler_params=pltpu.CompilerParams(vmem_limit_bytes=40 * 1024 * 1024),
        cost_estimate=pl.CostEstimate(flops=flops, bytes_accessed=moved, transcendentals=0),
    )(*args)


def mesh_place():
    return lax.axis_index("rep"), lax.axis_index("fsdp"), lax.axis_index("seq")


def total(refs, read):
    return (read(refs[0]) + read(refs[1])) + (read(refs[2]) + read(refs[3]))


def pack_kernel(qkv, vectors, packed, sems):
    rep, _, core = mesh_place()
    copies = [
        pltpu.make_async_copy(
            qkv.at[:, lanes(t * WIDTH + (rep * CORES + core) * LANE, LANE)],
            packed.at[pl.ds(0, SHARD), pl.ds(t * LANE, LANE)],
            sems.at[t],
        )
        for t in range(3)
    ]
    for copy in copies:
        copy.start()
    packed[SHARD:, :] = vectors[...]
    for copy in copies:
        copy.wait()


def unit_kernel(x0, x1, x2, x3, cot, fc, out, unit, scale, cot_copy, ff, sems):
    rep, _, core = mesh_place()
    piece = pl.ds(pl.multiple_of((rep * CORES + core) * LANE, LANE), LANE)
    copies = [
        pltpu.make_async_copy(fc.at[piece, :], ff.at[0], sems.at[0]),
        pltpu.make_async_copy(out.at[piece, :], ff.at[1], sems.at[1]),
        pltpu.make_async_copy(cot, cot_copy, sems.at[2]),
    ]
    for copy in copies:
        copy.start()
    for k, x in enumerate((x0, x1, x2, x3)):
        unit[k * ROWS : (k + 1) * ROWS, :], spread = normalise(x[...].astype(f32))
        if k == 0:
            scale[...] = jnp.broadcast_to(spread, (ROWS, LANE))
    for copy in copies:
        copy.wait()


def qkv_kernel(
    unit, p0, p1, p2, p3, f0, f1, f2, f3, qkv, kv_send, normed, weight, vectors, biases
):
    rep, shard, core = mesh_place()
    for k, (own, far) in enumerate(((p0, f0), (p1, f1), (p2, f2), (p3, f3))):
        at = pl.ds(pl.multiple_of((shard ^ k) * SHARD, SHARD), SHARD)
        weight[at, 0:TRIPLE] = own[0:SHARD, :]
        weight[at, TRIPLE : 2 * TRIPLE] = far[0:SHARD, :]
        vectors[:, at] = own[SHARD:, 0:SHARD].astype(f32)
    for p in range(CORES):
        for t, at in ((0, 0), (2, 2)):
            start = (at + rep // 2) * SHARD + (core ^ p) * LANE
            even, odd = vectors[2:3, lanes(start, LANE)], vectors[3:4, lanes(start, LANE)]
            biases[:, pl.ds(p * TRIPLE + t * LANE, LANE)] = jnp.broadcast_to(
                jnp.where(rep % 2 == 0, even, odd), (8, LANE)
            )
        biases[:, pl.ds(p * TRIPLE + LANE, LANE)] = jnp.zeros((8, LANE), f32)

    @pl.loop(0, 2)
    def _(block):
        at = pl.ds(pl.multiple_of(block * 2 * ROWS, 2 * ROWS), 2 * ROWS)
        values = (unit[at, :] * vectors[0:1, :] + vectors[1:2, :]).astype(bf16)
        normed[at, :] = values
        mixed = jnp.dot(values, weight[...], preferred_element_type=f32) + biases[0:1, :]
        mixed = mixed.astype(bf16)
        qkv[at, :] = mixed
        kv_send[at, 0 : 2 * LANE] = mixed[:, TRIPLE + LANE : 2 * TRIPLE]
        kv_send[at, 2 * LANE : 4 * LANE] = mixed[:, LANE:TRIPLE]


def dot_rows(left, right):
    return contract(left, right, 1, 1)


def head_probs(query, key_own, key_far, causal, far_seen):
    own = jnp.where(causal, dot_rows(query, key_own) * SCALE, masked_value)
    far = jnp.where(far_seen, dot_rows(query, key_far) * SCALE, masked_value)
    peak = jnp.maximum(jnp.max(own, -1, keepdims=True), jnp.max(far, -1, keepdims=True))
    own, far = jnp.exp(own - peak), jnp.exp(far - peak)
    share = 1.0 / (jnp.sum(own, -1, keepdims=True) + jnp.sum(far, -1, keepdims=True))
    return own * share, far * share


def head_masks(core):
    causal = lax.broadcasted_iota(jnp.int32, (ROWS, ROWS), 1) <= lax.broadcasted_iota(
        jnp.int32, (ROWS, ROWS), 0
    )
    far_seen = (lax.broadcasted_iota(jnp.int32, (ROWS, ROWS), 0) * 0 + core) == 1
    first = lax.broadcasted_iota(jnp.int32, (ROWS, LANE), 1) < HEAD_DIM
    return causal, far_seen, first


def attend_kernel(qkv, far, attended):
    core = lax.axis_index("seq")
    causal, far_seen, first = head_masks(core)

    @pl.loop(0, REPS)
    def _(sequence):
        at = pl.ds(pl.multiple_of(sequence * ROWS, ROWS), ROWS)
        for p in range(CORES):
            base = p * TRIPLE
            query = qkv[at, base : base + LANE]
            key_own = qkv[at, base + LANE : base + 2 * LANE]
            value_own = qkv[at, base + 2 * LANE : base + 3 * LANE]
            key_far = far[at, 2 * p * LANE : (2 * p + 1) * LANE]
            value_far = far[at, (2 * p + 1) * LANE : (2 * p + 2) * LANE]
            heads = []
            for mask in (first, ~first):
                masked = jnp.where(mask, query, jnp.zeros_like(query))
                own, other = head_probs(masked, key_own, key_far, causal, far_seen)
                heads.append(
                    jnp.dot(own.astype(bf16), value_own, preferred_element_type=f32)
                    + jnp.dot(other.astype(bf16), value_far, preferred_element_type=f32)
                )
            attended[at, p * LANE : (p + 1) * LANE] = jnp.where(first, *heads).astype(bf16)


def branch_kernel(a0, a1, a2, a3, x, proj, vectors, middle, unit, scale, normed, joined):
    rep, _, core = mesh_place()
    for k, a in enumerate((a0, a1, a2, a3)):
        for p in range(CORES):
            at = lanes(((rep ^ k) * CORES + (core ^ p)) * LANE, LANE)
            joined[:, at] = a[:, p * LANE : (p + 1) * LANE]
    branch = jnp.dot(joined[...], proj[...], preferred_element_type=f32)
    values = x[...].astype(f32) + branch + vectors[4:5, :]
    middle[...] = values
    norm, spread = normalise(values)
    unit[...] = norm
    scale[...] = jnp.broadcast_to(spread, (ROWS, LANE))
    normed[...] = (norm * vectors[5:6, :] + vectors[6:7, :]).astype(bf16)


def hidden_kernel(*refs):
    h, c, own, far = refs[0:4], refs[4:8], refs[8:12], refs[12:16]
    vectors, back, hidden, pre_grad, fc, out, h_all, c_all, bias = refs[16:]
    _, shard, core = mesh_place()
    for j, ff in enumerate((own, far)):
        for k in range(SHARDS):
            at = pl.ds((j * SHARDS + k) * LANE, LANE)
            fc[at, :] = ff[k][0]
            out[at, :] = ff[k][1]
            start = (shard ^ k) * SHARD + (core ^ j) * LANE
            bias[:, at] = jnp.broadcast_to(vectors[8:9, lanes(start, LANE)], (8, LANE))
    for k in range(REPS):
        at = pl.ds(k * ROWS, ROWS)
        h_all[at, :] = h[k][...]
        c_all[at, :] = c[k][...]

    @pl.loop(0, 2)
    def _(block):
        at = pl.ds(pl.multiple_of(block * 2 * ROWS, 2 * ROWS), 2 * ROWS)
        for n in range(HIDDEN // 256):
            tile = pl.ds(n * 256, 256)
            preact = dot_rows(h_all[at, :], fc[tile, :]) + bias[0:1, tile]
            value, slope = gelu_and_slope(preact)
            hidden[at, tile] = value.astype(bf16)
            grad = dot_rows(c_all[at, :], out[tile, :])
            pre_grad[at, tile] = (grad * slope).astype(bf16)
        back[at, :] = jnp.dot(pre_grad[at, :], fc[...], preferred_element_type=f32).astype(bf16)


def weights_kernel(hidden, pre_grad, h_all, c_all, out, output, own, far, sums):
    @pl.loop(0, 2)
    def _(block):
        at = pl.ds(pl.multiple_of(block * 2 * ROWS, 2 * ROWS), 2 * ROWS)
        output[at, :] = jnp.dot(hidden[at, :], out[...], preferred_element_type=f32).astype(bf16)

    sums[...] = jnp.broadcast_to(
        jnp.sum(pre_grad[...].astype(f32), 0, keepdims=True), sums.shape
    )
    for j, grads in enumerate((own, far)):
        for k in range(0, SHARDS, 2):
            tile = pl.ds((j * SHARDS + k) * LANE, 2 * LANE)
            for i, (left, right) in enumerate(((pre_grad, h_all), (hidden, c_all))):
                grad = contract(left[:, tile], right[...], 0, 0).astype(bf16)
                grads[k, i] = grad[0:LANE]
                grads[k + 1, i] = grad[LANE:]


def middle_kernel(
    g0, g1, g2, g3, unit, scale, vectors, cot, proj, middle_grad, o0, o1, o2, o3, sums, low, back
):
    rep, _, core = mesh_place()
    grad = total((g0, g1, g2, g3), lambda g: g[...].astype(f32))
    part, gain, shift = norm_pull(unit[...], scale[:, 0:1], vectors[5:6, :], grad)
    cots = cot[...].astype(f32)
    values = cots + part
    middle_grad[...] = values
    branch = values.astype(bf16)
    low[...] = branch
    back[...] = dot_rows(branch, proj[...]).astype(bf16)
    rows = [jnp.sum(branch.astype(f32), 0), gain, shift, jnp.sum(cots, 0)]
    for i, row in enumerate(rows):
        sums[i : i + 1, :] = row[None]
    sums[4:8, :] = jnp.zeros((4, WIDTH), f32)
    for k, o in enumerate((o0, o1, o2, o3)):
        for p in range(CORES):
            at = lanes(((rep ^ k) * CORES + (core ^ p)) * LANE, LANE)
            o[:, p * LANE : (p + 1) * LANE] = back[:, at]
        o[:, SHARD : 2 * SHARD] = low[:, lanes((rep ^ k) * SHARD, SHARD)]


def proj_grad_kernel(attended, b0, b1, b2, b3, grads, cols):
    rep, _, core = mesh_place()
    for k, b in enumerate((b0, b1, b2, b3)):
        cols[k * ROWS : (k + 1) * ROWS, :] = b[:, SHARD : 2 * SHARD]
    for a in range(REPS):
        blocks = [
            cols[pl.ds(pl.multiple_of((a ^ j ^ rep) * ROWS, ROWS), ROWS), :] for j in range(REPS)
        ]
        grad = contract(attended[a], jnp.concatenate(blocks, 0), 0, 0).astype(bf16)
        for p in range(CORES):
            for j in range(CORES):
                start = (a * CORES + j) * SHARD + (core ^ p) * LANE
                grads[pl.ds(pl.multiple_of(start, LANE), LANE), :] = grad[
                    p * LANE : (p + 1) * LANE, j * LANE : (j + 1) * LANE
                ]


def attend_back_kernel(qkv, far, b0, b1, b2, b3, query_grad, own_grad, far_grad, grads):
    core = lax.axis_index("seq")
    causal, far_seen, first = head_masks(core)
    for k, b in enumerate((b0, b1, b2, b3)):
        grads[k * ROWS : (k + 1) * ROWS, :] = b[:, 0 : 2 * LANE]

    @pl.loop(0, REPS)
    def _(sequence):
        at = pl.ds(pl.multiple_of(sequence * ROWS, ROWS), ROWS)
        for p in range(CORES):
            base = p * TRIPLE
            query = qkv[at, base : base + LANE]
            key_own = qkv[at, base + LANE : base + 2 * LANE]
            value_own = qkv[at, base + 2 * LANE : base + 3 * LANE]
            key_far = far[at, 2 * p * LANE : (2 * p + 1) * LANE]
            value_far = far[at, (2 * p + 1) * LANE : (2 * p + 2) * LANE]
            grad = grads[at, p * LANE : (p + 1) * LANE]
            queries, sums = [], [0.0] * 4
            for mask in (first, ~first):
                masked = jnp.where(mask, query, jnp.zeros_like(query))
                back = jnp.where(mask, grad, jnp.zeros_like(grad))
                own, other = head_probs(masked, key_own, key_far, causal, far_seen)
                own_back, other_back = dot_rows(back, value_own), dot_rows(back, value_far)
                row = jnp.sum(own * own_back, -1, keepdims=True) + jnp.sum(
                    other * other_back, -1, keepdims=True
                )
                own_score = (own * (own_back - row)).astype(bf16)
                other_score = (other * (other_back - row)).astype(bf16)
                queries.append(
                    jnp.dot(own_score, key_own, preferred_element_type=f32)
                    + jnp.dot(other_score, key_far, preferred_element_type=f32)
                )
                parts = [
                    contract(own_score, masked, 0, 0) * SCALE,
                    contract(own.astype(bf16), back, 0, 0),
                    contract(other_score, masked, 0, 0) * SCALE,
                    contract(other.astype(bf16), back, 0, 0),
                ]
                sums = [a + b for a, b in zip(sums, parts)]
            query_grad[at, p * LANE : (p + 1) * LANE] = (
                jnp.where(first, *queries) * SCALE
            ).astype(bf16)
            own_at = slice(2 * p * LANE, (2 * p + 1) * LANE)
            own_grad[at, own_at] = sums[0]
            own_grad[at, (2 * p + 1) * LANE : (2 * p + 2) * LANE] = sums[1]
            q = 1 - p
            far_grad[at, 2 * q * LANE : (2 * q + 1) * LANE] = sums[2].astype(bf16)
            far_grad[at, (2 * q + 1) * LANE : (2 * q + 2) * LANE] = sums[3].astype(bf16)


def qkv_back_kernel(
    query_grad, own_grad, far_grad, weight, normed, unit, ff_sums, mid_sums, own, far, joined, small, mixed, sums
):
    rep, shard, core = mesh_place()
    for p in range(CORES):
        base = p * TRIPLE
        mixed[:, base : base + LANE] = query_grad[:, p * LANE : (p + 1) * LANE]
        at = slice(2 * p * LANE, (2 * p + 2) * LANE)
        mixed[:, base + LANE : base + 3 * LANE] = (
            own_grad[:, at] + far_grad[:, at].astype(f32)
        ).astype(bf16)
    for k in range(SHARDS):
        at = lanes((shard ^ k) * SHARD, SHARD)
        grad = contract(normed[:, at], mixed[...], 0, 0).astype(bf16)
        own[k] = grad[:, 0:TRIPLE]
        far[k] = grad[:, TRIPLE:]
    gain = jnp.zeros((1, WIDTH), f32)
    shift = jnp.zeros((1, WIDTH), f32)
    for k in range(REPS):
        at = pl.ds(k * ROWS, ROWS)
        back = dot_rows(mixed[at, :], weight[...])
        joined[at, :] = back.astype(bf16)
        gain = gain + jnp.sum(back * unit[at, :], 0, keepdims=True)
        shift = shift + jnp.sum(back, 0, keepdims=True)
    sums[0:1, :] = gain
    sums[1:2, :] = shift
    mixed_sums = jnp.sum(mixed[...].astype(f32), 0, keepdims=True)
    for p in range(CORES):
        for i in range(2):
            start = i * SHARD + (core ^ p) * LANE
            sums[2:3, lanes(start, LANE)] = mixed_sums[
                :, p * TRIPLE + 2 * i * LANE : p * TRIPLE + (2 * i + 1) * LANE
            ]
    for k in range(SHARDS):
        small[k] = jnp.zeros(small.shape[1:], f32)
        at = lanes((shard ^ k) * SHARD, SHARD)
        small[k, 0:1, 0:SHARD] = sums[0:1, at]
        small[k, 1:2, 0:SHARD] = sums[1:2, at]
        queries = jnp.where((shard ^ k) == rep // 2, sums[2:3, 0:SHARD], 0.0)
        values = jnp.where((shard ^ k) == 2 + rep // 2, sums[2:3, SHARD : 2 * SHARD], 0.0)
        small[k, 2:3, 0:SHARD] = jnp.where(rep % 2 == 0, queries + values, 0.0)
        small[k, 3:4, 0:SHARD] = jnp.where(rep % 2 == 1, queries + values, 0.0)
        for i in range(4):
            small[k, 4 + i : 5 + i, 0:SHARD] = mid_sums[i : i + 1, at]
        for j in range(CORES):
            part = ff_sums[:, (j * SHARDS + k) * LANE : (j * SHARDS + k + 1) * LANE]
            row = lax.broadcasted_iota(jnp.int32, part.shape, 0)
            small[k, 8:16, lanes((core ^ j) * LANE, LANE)] = jnp.where(row == rep, part, 0.0)


def tail_kernel(own, far, small, o0, o1, o2, o3):
    for k, o in enumerate((o0, o1, o2, o3)):
        o[0:SHARD, :] = (own[k].astype(f32) + far[k].astype(f32)).astype(bf16)
        o[SHARD:, :] = small[k].astype(bf16)


def gather_tail_kernel(p0, p1, p2, p3, proj, o):
    o[:, 0:TRIPLE] = total((p0, p1, p2, p3), lambda p: p[...].astype(f32)).astype(bf16)
    o[0:SHARD, TRIPLE:] = proj[...]
    o[SHARD:, TRIPLE:] = jnp.zeros((o.shape[0] - SHARD, LANE), bf16)


def input_kernel(j0, j1, j2, j3, r0, r1, r2, r3, unit, scale, vectors, middle_grad, middle, block, grad):
    back = total((j0, j1, j2, j3), lambda g: g[...].astype(f32))
    output = total((r0, r1, r2, r3), lambda g: g[...].astype(f32))
    block[...] = (middle[...] + output + vectors[7:8, :]).astype(bf16)
    part, _, _ = norm_pull(unit[0:ROWS, :], scale[:, 0:1], vectors[0:1, :], back)
    grad[...] = middle_grad[...] + part


def final_kernel(p0, p1, p2, p3, f0, f1, f2, f3, qkv, proj, small):
    rep, _, core = mesh_place()
    for k, pair in enumerate(((p0, f0), (p1, f1), (p2, f2), (p3, f3))):
        for j, piece in enumerate(pair):
            start = ((rep ^ k) * CORES + (core ^ j)) * LANE
            for t in range(3):
                qkv[:, lanes(t * WIDTH + start, LANE)] = piece[
                    0:SHARD, t * LANE : (t + 1) * LANE
                ].astype(f32)
            proj[:, lanes(start, LANE)] = piece[0:SHARD, TRIPLE:].astype(f32)

    def read(pair):
        return pair[0][SHARD:, 0:SHARD].astype(f32) + pair[1][SHARD:, 0:SHARD].astype(f32)

    small[...] = total(((p0, f0), (p1, f1), (p2, f2), (p3, f3)), read)


def spread_kernel(p0, p1, p2, p3, f0, f1, f2, f3, fc, out):
    rep, _, core = mesh_place()
    for k, pair in enumerate(((p0, f0), (p1, f1), (p2, f2), (p3, f3))):
        for j, piece in enumerate(pair):
            at = pl.ds(pl.multiple_of(((rep ^ k) * CORES + (core ^ j)) * LANE, LANE), LANE)
            fc[at, :] = piece[0].astype(f32)
            out[at, :] = piece[1].astype(f32)


def add_kernel(own, far, o0, o1, o2, o3):
    for k, o in enumerate((o0, o1, o2, o3)):
        o[...] = (own[k].astype(f32) + far[k].astype(f32)).astype(bf16)


def sum_kernel(p0, p1, p2, p3, o):
    o[...] = total((p0, p1, p2, p3), lambda p: p[...].astype(f32)).astype(bf16)


def tiled_body(
    block_input,
    ln1_gain,
    ln1_shift,
    qkv_weight,
    qv_bias,
    proj_weight,
    proj_bias,
    ln2_gain,
    ln2_shift,
    fc_weight,
    fc_bias,
    out_weight,
    out_bias,
    cotangent,
):
    rep, _, core = mesh_place()

    def over_rep(pieces):
        return [swap(p, "rep", REPS, k) if k else p for k, p in enumerate(pieces)]

    def over_shards(pieces):
        return [swap(p, "fsdp", SHARDS, k) if k else p for k, p in enumerate(pieces)]

    def over_cores(value):
        return swap(value, "seq", CORES, 1)

    all_rows = REPS * ROWS
    fc_bias_part = pick(fc_bias.reshape(REPS, -1), rep, 0)
    vectors = [
        ln1_gain,
        ln1_shift,
        qv_bias[:SHARD],
        qv_bias[SHARD:],
        proj_bias,
        ln2_gain,
        ln2_shift,
        out_bias,
        fc_bias_part,
    ]
    vectors = jnp.stack(vectors + [jnp.zeros_like(ln1_gain)] * (16 - len(vectors)))
    vectors = jnp.pad(vectors, ((0, 0), (0, TRIPLE - SHARD)))
    (packed,) = vmem_call(
        pack_kernel,
        [((SHARD + 16, TRIPLE), bf16)],
        [qkv_weight, vectors],
        hbm=(0,),
        scratch=[pltpu.SemaphoreType.DMA((3,))],
    )
    own_packed = over_shards([packed] * SHARDS)
    far_packed = [over_cores(p) for p in own_packed]
    inputs = over_rep([block_input] * REPS)

    proj_part = pick(proj_weight.reshape(REPS * CORES, -1, WIDTH), rep * CORES + core, 0)
    proj_full = lax.all_gather(proj_part, "fsdp", axis=0)
    proj_full = lax.all_gather(proj_full, ("rep", "seq"), axis=1)
    proj_full = proj_full.reshape(WIDTH, WIDTH)

    unit_one, scale_one, own_cot, ff = vmem_call(
        unit_kernel,
        [
            ((all_rows, WIDTH), f32),
            ((ROWS, LANE), f32),
            ((ROWS, WIDTH), bf16),
            ((2, LANE, WIDTH), bf16),
        ],
        inputs + [cotangent, fc_weight, out_weight],
        hbm=(4, 5, 6),
        scratch=[pltpu.SemaphoreType.DMA((3,))],
    )
    cots = over_rep([own_cot] * REPS)
    own_ff = over_shards([ff] * SHARDS)
    far_ff = [over_cores(f) for f in own_ff]

    qkv, kv_send, normed_one, qkv_mine, vectors = vmem_call(
        qkv_kernel,
        [
            ((all_rows, 2 * TRIPLE), bf16),
            ((all_rows, 4 * LANE), bf16),
            ((all_rows, WIDTH), bf16),
            ((WIDTH, 2 * TRIPLE), bf16),
            ((16, WIDTH), f32),
        ],
        [unit_one] + own_packed + far_packed,
        scratch=[pltpu.VMEM((8, 2 * TRIPLE), f32)],
        flops=2 * all_rows * WIDTH * 2 * TRIPLE,
    )
    kv_far = over_cores(kv_send)
    (attended,) = vmem_call(
        attend_kernel,
        [((all_rows, SHARD), bf16)],
        [qkv, kv_far],
        flops=4 * all_rows * 2 * ROWS * SHARD,
    )
    mine = over_rep([attended[k * ROWS : (k + 1) * ROWS] for k in range(REPS)])
    middle, unit_two, scale_two, normed_two = vmem_call(
        branch_kernel,
        [
            ((ROWS, WIDTH), f32),
            ((ROWS, WIDTH), f32),
            ((ROWS, LANE), f32),
            ((ROWS, WIDTH), bf16),
        ],
        mine + [block_input, proj_full, vectors],
        scratch=[pltpu.VMEM((ROWS, WIDTH), bf16)],
        flops=2 * ROWS * WIDTH * WIDTH,
    )
    normed_two = over_rep([normed_two] * REPS)
    attended_all = lax.all_gather(attended, "rep", axis=0)

    back, hidden, pre_grad, _, out_mine, h_all, c_all, _ = vmem_call(
        hidden_kernel,
        [
            ((all_rows, WIDTH), bf16),
            ((all_rows, HIDDEN), bf16),
            ((all_rows, HIDDEN), bf16),
            ((HIDDEN, WIDTH), bf16),
            ((HIDDEN, WIDTH), bf16),
            ((all_rows, WIDTH), bf16),
            ((all_rows, WIDTH), bf16),
            ((8, HIDDEN), f32),
        ],
        normed_two + cots + own_ff + far_ff + [vectors],
        flops=6 * all_rows * WIDTH * HIDDEN,
    )
    back = over_rep([back[k * ROWS : (k + 1) * ROWS] for k in range(REPS)])
    output, ff_own, ff_far, ff_sums = vmem_call(
        weights_kernel,
        [
            ((all_rows, WIDTH), bf16),
            ((SHARDS, 2, LANE, WIDTH), bf16),
            ((SHARDS, 2, LANE, WIDTH), bf16),
            ((8, HIDDEN), f32),
        ],
        [hidden, pre_grad, h_all, c_all, out_mine],
        flops=6 * all_rows * WIDTH * HIDDEN,
    )
    piece = ((2, LANE, WIDTH), bf16)
    ff_pieces = vmem_call(add_kernel, [piece] * SHARDS, [ff_own, over_cores(ff_far)])
    (ff_piece,) = vmem_call(sum_kernel, [piece], over_shards(ff_pieces))
    ff_pieces = over_rep([ff_piece] * REPS)
    fc_grads, out_grads = vmem_call(
        spread_kernel,
        [((2 * REPS * LANE, WIDTH), f32)] * 2,
        ff_pieces + [over_cores(p) for p in ff_pieces],
    )

    middle_grad, o0, o1, o2, o3, mid_sums = vmem_call(
        middle_kernel,
        [((ROWS, WIDTH), f32)] + [((ROWS, 2 * SHARD), bf16)] * REPS + [((8, WIDTH), f32)],
        back + [unit_two, scale_two, vectors, cotangent, proj_full],
        scratch=[pltpu.VMEM((ROWS, WIDTH), bf16)] * 2,
        flops=2 * ROWS * WIDTH * WIDTH,
    )
    pairs = over_rep([o0, o1, o2, o3])
    query_grad, own_grad, far_grad = vmem_call(
        attend_back_kernel,
        [
            ((all_rows, SHARD), bf16),
            ((all_rows, 4 * LANE), f32),
            ((all_rows, 4 * LANE), bf16),
        ],
        [qkv, kv_far] + pairs,
        scratch=[pltpu.VMEM((all_rows, SHARD), bf16)],
        flops=10 * all_rows * 2 * ROWS * SHARD,
    )
    (proj_grads,) = vmem_call(
        proj_grad_kernel,
        [((WIDTH * CORES, LANE), bf16)],
        [attended_all] + pairs,
        scratch=[pltpu.VMEM((all_rows, SHARD), bf16)],
        flops=2 * all_rows * WIDTH * SHARD,
    )
    proj_grads = lax.psum_scatter(proj_grads, ("fsdp", "seq"), scatter_dimension=0, tiled=True)

    qkv_own, qkv_far, joined, small = vmem_call(
        qkv_back_kernel,
        [
            ((SHARDS, SHARD, TRIPLE), bf16),
            ((SHARDS, SHARD, TRIPLE), bf16),
            ((all_rows, WIDTH), bf16),
            ((SHARDS, 16, TRIPLE), f32),
        ],
        [query_grad, own_grad, over_cores(far_grad), qkv_mine, normed_one, unit_one, ff_sums, mid_sums],
        scratch=[pltpu.VMEM((all_rows, 2 * TRIPLE), bf16), pltpu.VMEM((8, WIDTH), f32)],
        flops=4 * all_rows * WIDTH * 2 * TRIPLE,
    )
    tail = vmem_call(
        tail_kernel,
        [((SHARD + 16, TRIPLE), bf16)] * SHARDS,
        [qkv_own, over_cores(qkv_far), small],
    )
    (tail,) = vmem_call(
        gather_tail_kernel,
        [((SHARD + 16, TRIPLE + LANE), bf16)],
        over_shards(tail) + [proj_grads],
    )
    tail = over_rep([tail] * REPS)
    qkv_grads, proj_grads, small = vmem_call(
        final_kernel,
        [((SHARD, 3 * WIDTH), f32), ((SHARD, WIDTH), f32), ((16, SHARD), f32)],
        tail + [over_cores(t) for t in tail],
    )
    joined = over_rep([joined[k * ROWS : (k + 1) * ROWS] for k in range(REPS)])
    output = over_rep([output[k * ROWS : (k + 1) * ROWS] for k in range(REPS)])
    block_output, input_grad = vmem_call(
        input_kernel,
        [((ROWS, WIDTH), bf16), ((ROWS, WIDTH), f32)],
        joined + output + [unit_one, scale_one, vectors, middle_grad, middle],
    )
    return (
        block_output,
        input_grad,
        small[0],
        small[1],
        qkv_grads,
        small[2:4].reshape(-1),
        proj_grads,
        small[4],
        small[5],
        small[6],
        fc_grads,
        small[8:12].reshape(-1),
        out_grads,
        small[7],
    )


def make_body(reps, shards, cores):
    def rep_swap(value, offset):
        return swap(value, "rep", reps, offset) if offset else value

    def shard_swap(value, offset):
        return swap(value, "fsdp", shards, offset) if offset else value

    def core_swap(value):
        return swap(value, "seq", cores, 1)

    def plane_gather(value):
        return [rep_swap(value, k) for k in range(reps)]

    def plane_exchange(pieces):
        return [rep_swap(piece, k) for k, piece in enumerate(pieces)]

    def pair_sum(pieces):
        while len(pieces) > 1:
            pieces = [pieces[i] + pieces[i + 1] for i in range(0, len(pieces), 2)]
        return pieces[0]

    def own_scatter(parts):
        core = lax.axis_index("seq")
        shard = lax.axis_index("fsdp")
        kept = pick(parts, core, 1).astype(f32)
        kept = (kept + core_swap(pick(parts, 1 - core, 1)).astype(f32)).astype(bf16)
        pieces = [shard_swap(pick(kept, shard ^ k, 0), k).astype(f32) for k in range(shards)]
        return pair_sum(pieces).astype(bf16)

    def place_both(pieces):
        core = lax.axis_index("seq")
        rep = lax.axis_index("rep")
        held = jnp.zeros((reps, cores) + pieces[0].shape, pieces[0].dtype)
        zeros = (0,) * pieces[0].ndim
        for k, piece in enumerate(pieces):
            held = lax.dynamic_update_slice(held, piece[None, None], (rep ^ k, core) + zeros)
            far = core_swap(piece)
            held = lax.dynamic_update_slice(held, far[None, None], (rep ^ k, 1 - core) + zeros)
        return held

    def body(
        block_input,
        ln1_gain,
        ln1_shift,
        qkv_weight,
        qv_bias,
        proj_weight,
        proj_bias,
        ln2_gain,
        ln2_shift,
        fc_weight,
        fc_bias,
        out_weight,
        out_bias,
        cotangent,
    ):
        rows, width = block_input.shape
        shard_width = width // shards
        part = width // (reps * cores)
        rep_width = part * cores
        hidden_part = fc_weight.shape[0] // (reps * cores)
        head_scale = HEAD_DIM ** (-0.5)
        rep = lax.axis_index("rep")
        shard = lax.axis_index("fsdp")
        core = lax.axis_index("seq")
        rep_at = [rep ^ k for k in range(reps)]
        shard_at = [shard ^ k for k in range(shards)]

        columns = qkv_weight.reshape(shard_width, 3, reps, cores, part)
        columns = pick(pick(columns, rep, 2), core, 2).reshape(shard_width, 3 * part)
        fc_bias_part = pick(fc_bias.reshape(reps, -1), rep, 0)
        vectors = [
            ln1_gain,
            ln1_shift,
            qv_bias[:shard_width],
            qv_bias[shard_width:],
            proj_bias,
            ln2_gain,
            ln2_shift,
            out_bias,
            fc_bias_part,
        ]
        vectors = [jnp.pad(v, (0, 3 * part - v.shape[0])) for v in vectors]
        vectors = jnp.stack(vectors + [jnp.zeros_like(vectors[0])] * (16 - len(vectors)))
        packed = jnp.concatenate([columns, vectors], 0)
        packed, own_rows = lax.optimization_barrier((packed, block_input))
        packed = place([shard_swap(packed, k) for k in range(shards)], shard_at)
        inputs_all = jnp.concatenate(plane_gather(own_rows), 0)
        columns = packed[:, :shard_width].reshape(width, 3 * part)
        vectors = packed[:, shard_width:, :].astype(f32)

        def vector(index, size):
            return vectors[:, index, :size].reshape(-1)

        gain_one, shift_one = vector(0, shard_width), vector(1, shard_width)
        qv_full = jnp.stack([vectors[:, 2, :shard_width], vectors[:, 3, :shard_width]], 1)
        qv_full = qv_full.reshape(2, reps, cores * part)
        proj_bias_full = vector(4, shard_width)
        gain_two, shift_two = vector(5, shard_width), vector(6, shard_width)
        out_bias_full = vector(7, shard_width)
        fc_bias_mine = vector(8, fc_bias_part.shape[0])
        qkv_mine = place([columns, core_swap(columns)], [core, 1 - core])
        qkv_mine = jnp.transpose(qkv_mine, (1, 0, 2)).reshape(width, cores * 3 * part)

        proj_part = pick(proj_weight.reshape(reps * cores, -1, width), rep * cores + core, 0)
        proj_full = lax.all_gather(proj_part, ("rep", "fsdp", "seq"), axis=0)
        proj_full = proj_full.reshape((reps, shards, cores) + proj_part.shape)
        proj_full = jnp.transpose(proj_full, (1, 0, 2, 3, 4)).reshape(width, width)

        fc_part = pick(fc_weight.reshape(reps * cores, hidden_part, width), rep * cores + core, 0)
        out_part = pick(out_weight.reshape(reps * cores, hidden_part, width), rep * cores + core, 0)
        both_part = jnp.stack([fc_part, out_part])
        both_part, packed = lax.optimization_barrier((both_part, packed))
        both = place([shard_swap(both_part, k) for k in range(shards)], shard_at)
        both = place([both, core_swap(both)], [core, 1 - core])
        fc_mine = jnp.transpose(both[:, :, 0], (1, 0, 2, 3)).reshape(-1, width)
        out_mine = jnp.transpose(both[:, :, 1], (1, 0, 2, 3)).reshape(-1, width)

        own_cot, inputs_all = lax.optimization_barrier((cotangent, inputs_all))
        cot_all = jnp.concatenate(plane_gather(own_cot), 0)

        unit_one, scale_one = normalise(inputs_all.astype(f32))
        normed_all = (unit_one * gain_one + shift_one).astype(bf16)
        mixed = jnp.dot(normed_all, qkv_mine, preferred_element_type=f32)
        mixed = mixed.reshape(reps, rows, cores, 3, part)
        qv_mine = pick(qv_full, rep, 1).reshape(2, cores, part)
        heads = (reps, rows, rep_width // HEAD_DIM, HEAD_DIM)
        queries = (mixed[:, :, :, 0] + qv_mine[0]).astype(bf16).reshape(heads)
        keys = mixed[:, :, :, 1].astype(bf16).reshape(heads)
        values = (mixed[:, :, :, 2] + qv_mine[1]).astype(bf16).reshape(heads)
        far_pair = core_swap(jnp.stack([keys, values]))
        keys_both = jnp.concatenate([keys, far_pair[0]], 1)
        values_both = jnp.concatenate([values, far_pair[1]], 1)

        row_pos = lax.broadcasted_iota(jnp.int32, (rows, 2 * rows), 0)
        col_pos = lax.broadcasted_iota(jnp.int32, (rows, 2 * rows), 1)
        allowed = jnp.where(col_pos < rows, col_pos <= row_pos, core == 1)
        scores = jnp.einsum("sqhd,skhd->shqk", queries, keys_both, preferred_element_type=f32)
        scores = jnp.where(allowed, scores * head_scale, masked_value)
        peak = jnp.max(scores, -1, keepdims=True)
        powers = jnp.exp(scores - peak)
        probs = powers / jnp.sum(powers, -1, keepdims=True)
        probs_low = probs.astype(bf16)
        attended = jnp.einsum("shqk,skhd->sqhd", probs_low, values_both, preferred_element_type=f32)
        attended_low = attended.astype(bf16).reshape(reps, rows, rep_width)
        mine = place(plane_exchange([attended_low[k] for k in range(reps)]), rep_at)
        mine = jnp.transpose(mine, (1, 0, 2)).reshape(rows, width)
        middle = (
            block_input.astype(f32)
            + jnp.dot(mine, proj_full, preferred_element_type=f32)
            + proj_bias_full
        )
        unit_two, scale_two = normalise(middle)
        normed_two = (unit_two * gain_two + shift_two).astype(bf16)
        normed_two_all = jnp.concatenate(plane_gather(normed_two), 0)

        attended_all = place([attended_low[k] for k in range(reps)], rep_at)
        attended_all = lax.all_gather(attended_all.reshape(reps * rows, rep_width), "rep", axis=0)
        attended_all = jnp.transpose(attended_all, (1, 0, 2)).reshape(reps * rows, width)

        hidden_grad = contract(cot_all, out_mine, 1, 1)
        preact = contract(normed_two_all, fc_mine, 1, 1) + fc_bias_mine
        hidden, slope = gelu_and_slope(preact)
        hidden_low = hidden.astype(bf16)
        pre_grad = (hidden_grad * slope).astype(bf16)
        normed_grad = jnp.dot(pre_grad, fc_mine, preferred_element_type=f32).astype(bf16)
        normed_grad = normed_grad.reshape(reps, rows, width)
        normed_grad = plane_exchange([normed_grad[k] for k in range(reps)])
        normed_grad = pair_sum([v.astype(f32) for v in normed_grad])
        output = jnp.dot(hidden_low, out_mine, preferred_element_type=f32).astype(bf16)
        output, normed_grad = lax.optimization_barrier((output, normed_grad))
        output = output.reshape(reps, rows, width)
        output = plane_exchange([output[k] for k in range(reps)])
        output = pair_sum([v.astype(f32) for v in output])
        block_output = (middle + output + out_bias_full).astype(bf16)

        out_grads = contract(hidden_low, cot_all, 0, 0).astype(bf16)
        out_grads = lax.psum_scatter(out_grads, ("fsdp", "seq"), scatter_dimension=0, tiled=True)
        fc_grads = contract(pre_grad, normed_two_all, 0, 0).astype(bf16)
        fc_grads = own_scatter(fc_grads.reshape(shards, cores, hidden_part, width))
        ff_grads = plane_gather(jnp.stack([fc_grads, out_grads]))
        ff_grads = place_both(ff_grads)
        fc_grads = ff_grads[:, :, 0].reshape(-1, width).astype(f32)
        out_grads = ff_grads[:, :, 1].reshape(-1, width).astype(f32)

        middle_part, gain_two_grads, shift_two_grads = norm_pull(
            unit_two, scale_two, gain_two, normed_grad
        )
        middle_grad = cotangent.astype(f32) + middle_part
        branch_grad = middle_grad.astype(bf16)
        attended_grad = contract(branch_grad, proj_full, 1, 1).astype(bf16)
        pair = [v.reshape(rows, reps, rep_width) for v in (attended_grad, branch_grad)]
        pair = jnp.concatenate(pair, 2)
        pair = plane_exchange([pick(pair, i, 1) for i in rep_at])
        attended_grad = jnp.stack([v[:, :rep_width] for v in pair]).reshape(heads)
        branch_cols = place([v[:, rep_width:] for v in pair], rep_at).reshape(-1, rep_width)
        proj_grads = contract(attended_all, branch_cols, 0, 0).astype(bf16)
        proj_grads = proj_grads.reshape(shards, shard_width, cores, part)
        proj_grads = jnp.transpose(proj_grads, (0, 2, 1, 3)).reshape(-1, part)
        proj_grads = lax.psum_scatter(proj_grads, ("fsdp", "seq"), scatter_dimension=0, tiled=True)
        proj_grads = lax.all_gather(proj_grads, ("rep", "seq"), axis=0)
        proj_grads = jnp.transpose(proj_grads, (1, 0, 2)).reshape(shard_width, width).astype(f32)

        prob_grad = jnp.einsum("sqhd,skhd->shqk", attended_grad, values_both, preferred_element_type=f32)
        row_total = jnp.sum(probs * prob_grad, -1, keepdims=True)
        score_low = (probs * (prob_grad - row_total)).astype(bf16)
        query_grad = (
            jnp.einsum("shqk,skhd->sqhd", score_low, keys_both, preferred_element_type=f32)
            * head_scale
        )
        key_grad = (
            jnp.einsum("shqk,sqhd->skhd", score_low, queries, preferred_element_type=f32)
            * head_scale
        )
        value_grad = jnp.einsum("shqk,sqhd->skhd", probs_low, attended_grad, preferred_element_type=f32)
        far_grads = core_swap(jnp.stack([key_grad[:, rows:], value_grad[:, rows:]]).astype(bf16))
        key_grad = key_grad[:, :rows] + far_grads[0].astype(f32)
        value_grad = value_grad[:, :rows] + far_grads[1].astype(f32)
        mixed_grad = jnp.stack(
            [
                g.astype(bf16).reshape(reps * rows, cores, part)
                for g in (query_grad, key_grad, value_grad)
            ],
            2,
        ).reshape(reps * rows, cores * 3 * part)
        qkv_grads = contract(normed_all, mixed_grad, 0, 0).astype(bf16)
        normed_one_grad = contract(mixed_grad, qkv_mine, 1, 1)
        joined = normed_one_grad.astype(bf16).reshape(reps, rows, width)
        joined = plane_exchange([joined[k] for k in range(reps)])
        joined = pair_sum([v.astype(f32) for v in joined])
        input_part = norm_pull(unit_one[:rows], scale_one[:rows], gain_one, joined)[0]
        input_grad = middle_grad + input_part

        gain_one_grads = jnp.sum(normed_one_grad * unit_one, 0)
        shift_one_grads = jnp.sum(normed_one_grad, 0)
        mixed_sums = jnp.sum(mixed_grad.astype(f32), 0).reshape(cores, 3, part)
        qv_sums = jnp.stack([mixed_sums[:, 0].reshape(-1), mixed_sums[:, 2].reshape(-1)])
        qv_sums = lax.dynamic_update_index_in_dim(
            jnp.zeros((2, reps, rep_width), f32), qv_sums, rep, 1
        )
        fc_sums = jnp.sum(pre_grad.astype(f32), 0).reshape(shards, -1)
        fc_sums = lax.dynamic_update_index_in_dim(
            jnp.zeros((shards, reps, fc_sums.shape[1]), f32), fc_sums, rep, 1
        )
        small = [
            gain_one_grads,
            shift_one_grads,
            qv_sums,
            jnp.sum(branch_grad.astype(f32), 0),
            gain_two_grads,
            shift_two_grads,
            jnp.sum(cotangent.astype(f32), 0),
            fc_sums,
        ]
        small = jnp.concatenate([v.reshape(shards, -1) for v in small], 1).astype(bf16)
        small_size = small.shape[1]
        small_rows = -(-small_size // (16 * 3 * part)) * 16
        small = jnp.pad(small, ((0, 0), (0, small_rows * 3 * part - small_size)))
        small = small.reshape(shards, small_rows, 3 * part)

        qkv_grads = qkv_grads.reshape(shards, shard_width, cores, 3 * part)
        tail = pick(qkv_grads, core, 2).astype(f32)
        tail = (tail + core_swap(pick(qkv_grads, 1 - core, 2)).astype(f32)).astype(bf16)
        tail = jnp.concatenate([tail, small], 1)
        tail = [shard_swap(pick(tail, i, 0), k).astype(f32) for k, i in enumerate(shard_at)]
        tail = place_both(plane_gather(pair_sum(tail).astype(bf16)))
        qkv_grads = tail[:, :, :shard_width].reshape(reps * cores, shard_width, 3, part)
        qkv_grads = jnp.transpose(qkv_grads, (1, 2, 0, 3)).reshape(shard_width, 3 * width)
        qkv_grads = qkv_grads.astype(f32)
        small = jnp.sum(tail[:, :, shard_width:].astype(f32), (0, 1)).reshape(-1)
        sizes = [1, 1, 2, 1, 1, 1, 1]
        ends = [0]
        for size in sizes:
            ends.append(ends[-1] + size * shard_width)
        one = [small[a:b] for a, b in zip(ends[:-1], ends[1:])] + [small[ends[-1] : small_size]]
        return (
            block_output,
            input_grad,
            one[0],
            one[1],
            qkv_grads,
            one[2],
            proj_grads,
            one[3],
            one[4],
            one[5],
            fc_grads,
            one[7],
            out_grads,
            one[6],
        )

    return body


def solution(mesh):
    line, block = P("fsdp"), P("fsdp", None)
    tokens = P(("rep", "fsdp", "seq"), None)
    in_specs = (
        tokens,
        line,
        line,
        block,
        line,
        block,
        line,
        line,
        line,
        block,
        line,
        block,
        line,
        tokens,
    )
    out_specs = (
        tokens,
        tokens,
        line,
        line,
        block,
        line,
        block,
        line,
        line,
        line,
        block,
        line,
        block,
        line,
    )
    sizes = mesh.shape["rep"], mesh.shape["fsdp"], mesh.shape["seq"]
    general = make_body(*sizes)

    def body(*args):
        tiled = sizes == (REPS, SHARDS, CORES) and args[0].shape == (ROWS, WIDTH)
        return tiled_body(*args) if tiled else general(*args)

    return jax.shard_map(body, mesh=mesh, in_specs=in_specs, out_specs=out_specs, check_vma=False)
```

profile of v0, /device:TPU:9, one launch (start us, length us, event | category | flops | bytes accessed | tf_op | source)
XLA Modules:
  0.0 326.3 jit_solution(4581223872038834109)
XLA Ops:
  9.1 11.9 %all_gather.16 = bf16[4,32,1024]{2,1,0:T(8,128)(2,1)} all-gather(bf16[1,32,1024]{2,1,0:T(8,128)(2,1)S(1)} %constant_dynamic-slice_fusion), channel_id=1, replica_groups=mesh['rep'=4,'fsdp'=4,'seq'=2] {'fsdp'}, dimensions={0}, use_global_device_ids=true | all-gather | bytes 327680 | tf_op jit(solution)/shard_map/all_gather | solution.py:520
  33.2 3.1 collective-permute-start.2
  36.3 3.2 collective-permute-done.4.p2
  39.6 9.8 %collective-permute-start.6 = (bf16[272,384]{1,0:T(8,128)(2,1)S(1)}, bf16[272,384]{1,0:T(8,128)(2,1)S(1)}, u32[]{:S(2)}, u32[]{:S(2)}) collective-permute-start(bf16[272,384]{1,0:T(8,128)(2,1)S(1)} %shard_map.246.p0), channel_id=1, source_target_pairs={{0,1},{1,0},{2,3},{3,2},{4,5},{5,4},{6,7},{7,6},{8,9},{9,8},{10,11... | collective-permute-start | bytes 626696 | tf_op jit(solution)/shard_map/ppermute | solution.py:54
  49.4 3.4 %collective-permute-start.7 = (bf16[272,384]{1,0:T(8,128)(2,1)S(1)}, bf16[272,384]{1,0:T(8,128)(2,1)S(1)}, u32[]{:S(2)}, u32[]{:S(2)}) collective-permute-start(bf16[272,384]{1,0:T(8,128)(2,1)S(1)} %collective-permute-done.3.p1), channel_id=1, source_target_pairs={{0,1},{1,0},{2,3},{3,2},{4,5},{5,4},{6,7},{7,6},{8,9},{9,8},{10,11... | collective-permute-start | bytes 626696 | tf_op jit(solution)/shard_map/ppermute | solution.py:54
  64.9 6.9 %shard_map.248 = bf16[512,256]{1,0:T(8,128)(2,1)} custom-call(bf16[512,768]{1,0:T(8,128)(2,1)S(1)} %get-tuple-element.66.qkv, bf16[512,512]{1,0:T(8,128)(2,1)S(1)} %collective-permute-done.10.far), custom_call_target="tpu_custom_call" | custom-call | flops 134217728 | bytes 1572864 | tf_op jit(solution)/shard_map/pallas_call | solution.py:76
  73.7 9.9 %collective-permute-done.20.refs_9_ = bf16[2,128,1024]{2,1,0:T(8,128)(2,1)} collective-permute-done((bf16[2,128,1024]{2,1,0:T(8,128)(2,1)}, bf16[2,128,1024]{2,1,0:T(8,128)(2,1)}, u32[]{:S(2)}, u32[]{:S(2)}) %collective-permute-start.20) | collective-permute-done | bytes 524320 | tf_op jit(solution)/shard_map/ppermute | solution.py:54
  87.3 22.4 %collective-permute-done.22.refs_11_ = bf16[2,128,1024]{2,1,0:T(8,128)(2,1)} collective-permute-done((bf16[2,128,1024]{2,1,0:T(8,128)(2,1)}, bf16[2,128,1024]{2,1,0:T(8,128)(2,1)}, u32[]{:S(2)}, u32[]{:S(2)}) %collective-permute-start.22) | collective-permute-done | bytes 524320 | tf_op jit(solution)/shard_map/ppermute | solution.py:54
  129.6 5.3 %collective-permute-done.14.refs_1_ = bf16[128,1024]{1,0:T(8,128)(2,1)} collective-permute-done((bf16[128,1024]{1,0:T(8,128)(2,1)}, bf16[128,1024]{1,0:T(8,128)(2,1)}, u32[]{:S(2)}, u32[]{:S(2)}) %collective-permute-start.14) | collective-permute-done | bytes 262176 | tf_op jit(solution)/shard_map/ppermute | solution.py:54
  134.9 7.1 %collective-permute-done.16.refs_3_ = bf16[128,1024]{1,0:T(8,128)(2,1)} collective-permute-done((bf16[128,1024]{1,0:T(8,128)(2,1)}, bf16[128,1024]{1,0:T(8,128)(2,1)}, u32[]{:S(2)}, u32[]{:S(2)}) %collective-permute-start.16) | collective-permute-done | bytes 262176 | tf_op jit(solution)/shard_map/ppermute | solution.py:54
  142.0 7.9 %shard_map.250 = (bf16[512,1024]{1,0:T(8,128)(2,1)S(1)}, bf16[512,1024]{1,0:T(8,128)(2,1)S(1)}, bf16[512,1024]{1,0:T(8,128)(2,1)S(1)}, bf16[1024,1024]{1,0:T(8,1...) custom-call(bf16[128,1024]{1,0:T(8,128)(2,1)} %get-tuple-element.69., ...), custom_call_target="tpu_custom_call" | custom-call | flops 3221225472 | bytes 15826944 | tf_op jit(solution)/shard_map/pallas_call | solution.py:76
  153.4 5.2 %shard_map.253 = (bf16[512,1024]{1,0:T(8,128)(2,1)S(1)}, bf16[4,2,128,1024]{3,2,1,0:T(8,128)(2,1)S(1)}, bf16[4,2,128,1024]{3,2,1,0:T(8,128)(2,1)}, f32[8,1024]{1,0:T(8,128)S(1)}) custom-call(bf16[512,1024]{1,0:T(8,128)(2,1)S(1)} %get-tuple-element.84.hidden, bf16[512,1024]{1,0:T(8,128)(2,1)S(1)} %get-tuple-element.85.pre_grad, ...), custom_call_target="tpu_custom_call" | custom-call | flops 3221225472 | bytes 11567104 | tf_op jit(solution)/shard_map/pallas_call | solution.py:76
  161.0 6.7 %collective-permute-done.29.g3 = bf16[128,1024]{1,0:T(8,128)(2,1)S(1)} collective-permute-done((bf16[128,1024]{1,0:T(8,128)(2,1)S(1)}, bf16[128,1024]{1,0:T(8,128)(2,1)S(1)}, u32[]{:S(2)}, u32[]{:S(2)}) %collective-permute-start.29) | collective-permute-done | bytes 262176 | tf_op jit(solution)/shard_map/ppermute | solution.py:54
  175.3 9.2 %shard_map.252 = (bf16[512,256]{1,0:T(8,128)(2,1)S(1)}, f32[512,512]{1,0:T(8,128)S(1)}, bf16[512,512]{1,0:T(8,128)(2,1)S(1)}) custom-call(bf16[512,768]{1,0:T(8,128)(2,1)S(1)} %get-tuple-element.66.qkv, bf16[512,512]{1,0:T(8,128)(2,1)S(1)} %collective-permute-done.10.far, bf16[128,512]{1,0:T(8,128)(2,1)S(1)} %get-tuple-element.75.b0, ...), custom_call_target="tpu_custom_call" | custom-call | flops 335544320 | bytes 3670016 | tf_op jit(solution)/shard_map/pallas_call | solution.py:76
  184.5 2.8 collective-permute-start.33
  188.9 3.7 %shard_map.254 = (bf16[4,256,384]{2,1,0:T(8,128)(2,1)S(1)}, bf16[4,256,384]{2,1,0:T(8,128)(2,1)}, bf16[512,1024]{1,0:T(8,128)(2,1)S(1)}, f32[4,16,384]{2,1,0:T(8,128)S(1)}) custom-call(bf16[512,256]{1,0:T(8,128)(2,1)S(1)} %get-tuple-element.79.query_grad, f32[512,512]{1,0:T(8,128)S(1)} %get-tuple-element.80.own_grad, ...), custom_call_target="tpu_custom_call" | custom-call | flops 1610612736 | bytes 9338880 | tf_op jit(solution)/shard_map/pallas_call | solution.py:76
  208.0 2.9 shard_map.260
  215.1 18.3 %collective-permute-done.42.p2 = bf16[272,384]{1,0:T(8,128)(2,1)S(1)} collective-permute-done((bf16[272,384]{1,0:T(8,128)(2,1)S(1)}, bf16[272,384]{1,0:T(8,128)(2,1)S(1)}, u32[]{:S(2)}, u32[]{:S(2)}) %collective-permute-start.42) | collective-permute-done | bytes 208928 | tf_op jit(solution)/shard_map/ppermute | solution.py:54
  241.9 5.0 %collective-permute-done.35.j2 = bf16[128,1024]{1,0:T(8,128)(2,1)S(1)} collective-permute-done((bf16[128,1024]{1,0:T(8,128)(2,1)}, bf16[128,1024]{1,0:T(8,128)(2,1)S(1)}, u32[]{:S(2)}, u32[]{:S(2)}) %collective-permute-start.35) | collective-permute-done | bytes 262176 | tf_op jit(solution)/shard_map/ppermute | solution.py:54
  250.1 20.2 %collective-permute-done.53.p2 = bf16[2,128,1024]{2,1,0:T(8,128)(2,1)} collective-permute-done((bf16[2,128,1024]{2,1,0:T(8,128)(2,1)}, bf16[2,128,1024]{2,1,0:T(8,128)(2,1)}, u32[]{:S(2)}, u32[]{:S(2)}) %collective-permute-start.53) | collective-permute-done | bytes 524320 | tf_op jit(solution)/shard_map/ppermute | solution.py:54
  270.7 13.0 %collective-permute-done.54.p3 = bf16[2,128,1024]{2,1,0:T(8,128)(2,1)} collective-permute-done((bf16[2,128,1024]{2,1,0:T(8,128)(2,1)}, bf16[2,128,1024]{2,1,0:T(8,128)(2,1)}, u32[]{:S(2)}, u32[]{:S(2)}) %collective-permute-start.54) | collective-permute-done | bytes 524320 | tf_op jit(solution)/shard_map/ppermute | solution.py:54
  294.9 4.5 %collective-permute-done.55.p1 = bf16[2,128,1024]{2,1,0:T(8,128)(2,1)S(1)} collective-permute-done((bf16[2,128,1024]{2,1,0:T(8,128)(2,1)S(1)}, bf16[2,128,1024]{2,1,0:T(8,128)(2,1)S(1)}, u32[]{:S(2)}, u32[]{:S(2)}) %collective-permute-start.55) | collective-permute-done | bytes 524320 | tf_op jit(solution)/shard_map/ppermute | solution.py:54
  300.6 12.0 %collective-permute-start.60 = (bf16[2,128,1024]{2,1,0:T(8,128)(2,1)S(1)}, bf16[2,128,1024]{2,1,0:T(8,128)(2,1)S(1)}, u32[]{:S(2)}, u32[]{:S(2)}) collective-permute-start(bf16[2,128,1024]{2,1,0:T(8,128)(2,1)S(1)} %collective-permute-done.56.p2), channel_id=1, source_target_pairs={{0,1},{1,0},{2,3},{3,2},{4,5},{5,4},{6,7},{7,6},{8,9},{9,8},{10,11... | collective-permute-start | bytes 1572872 | tf_op jit(solution)/shard_map/ppermute | solution.py:54
  314.9 3.9 %shard_map.262 = (f32[1024,1024]{1,0:T(8,128)}, f32[1024,1024]{1,0:T(8,128)}) custom-call(bf16[2,128,1024]{2,1,0:T(8,128)(2,1)S(1)} %shard_map.261.p0, bf16[2,128,1024]{2,1,0:T(8,128)(2,1)S(1)} %collective-permute-done.55.p1, bf16[2,128,1024]{2,1,0:T(8,128)(2,1)S(1)} %collective-permute-done.56.p2, bf16[2,128,1024]{2,1,0:T(8,128)(2,1)S(1)} %collective-permute-done.57.p3, ...), custom_call_target="tpu_custom_call" | custom-call | bytes 12582912 | tf_op jit(solution)/shard_map/pallas_call | solution.py:76
  (278 shorter events, 111.7 us)
Async XLA Ops:
  8.1 109.8 %all-gather.5.cloned.1.call-start = ((), (), s32[]{:S(2)}) async-start(), calls=%async_computation.2 | async-start | bytes 2359296 | tf_op jit(solution)/shard_map/all_gather | solution.py:521
  21.0 173.9 %all-gather.7.cloned.1.call-start = ((), (), s32[]{:S(2)}) async-start(), calls=%async_computation.3 | async-start | bytes 1310720 | tf_op jit(solution)/shard_map/all_gather | solution.py:574
  29.5 23.3 %collective-permute-start = (bf16[128,1024]{1,0:T(8,128)(2,1)S(1)}, bf16[128,1024]{1,0:T(8,128)(2,1)S(1)}, u32[]{:S(2)}, u32[]{:S(2)}) collective-permute-start(bf16[128,1024]{1,0:T(8,128)(2,1)S(1)} %copy-done.20), channel_id=1, source_target_pairs={{0,8},{8,0},{16,24},{24,16},{1,9},{9,1},{17,25},{25,17},{2,10},{10... | collective-permute-start | bytes 786440 | tf_op jit(solution)/shard_map/ppermute | solution.py:54
  30.7 22.1 %collective-permute-start.1 = (bf16[128,1024]{1,0:T(8,128)(2,1)S(1)}, bf16[128,1024]{1,0:T(8,128)(2,1)S(1)}, u32[]{:S(2)}, u32[]{:S(2)}) collective-permute-start(bf16[128,1024]{1,0:T(8,128)(2,1)S(1)} %copy-done.20), channel_id=1, source_target_pairs={{0,16},{8,24},{16,0},{24,8},{1,17},{9,25},{17,1},{25,9},{2,18},{10... | collective-permute-start | bytes 786440 | tf_op jit(solution)/shard_map/ppermute | solution.py:54
  61.7 21.9 %collective-permute-start.20 = (bf16[2,128,1024]{2,1,0:T(8,128)(2,1)}, bf16[2,128,1024]{2,1,0:T(8,128)(2,1)}, u32[]{:S(2)}, u32[]{:S(2)}) collective-permute-start(bf16[2,128,1024]{2,1,0:T(8,128)(2,1)} %get-tuple-element.71.refs_8_), channel_id=1, source_target_pairs={{0,2},{2,0},{4,6},{6,4},{1,3},{3,1},{5,7},{7,5},{8,10},{10,8},{12,... | collective-permute-start | bytes 1572872 | tf_op jit(solution)/shard_map/ppermute | solution.py:54
  61.7 25.4 %collective-permute-start.21 = (bf16[2,128,1024]{2,1,0:T(8,128)(2,1)}, bf16[2,128,1024]{2,1,0:T(8,128)(2,1)}, u32[]{:S(2)}, u32[]{:S(2)}) collective-permute-start(bf16[2,128,1024]{2,1,0:T(8,128)(2,1)} %get-tuple-element.71.refs_8_), channel_id=1, source_target_pairs={{0,4},{2,6},{4,0},{6,2},{1,5},{3,7},{5,1},{7,3},{8,12},{10,14},{12... | collective-permute-start | bytes 1572872 | tf_op jit(solution)/shard_map/ppermute | solution.py:54
  63.9 45.8 %collective-permute-start.22 = (bf16[2,128,1024]{2,1,0:T(8,128)(2,1)}, bf16[2,128,1024]{2,1,0:T(8,128)(2,1)}, u32[]{:S(2)}, u32[]{:S(2)}) collective-permute-start(bf16[2,128,1024]{2,1,0:T(8,128)(2,1)} %get-tuple-element.71.refs_8_), channel_id=1, source_target_pairs={{0,6},{2,4},{4,2},{6,0},{1,7},{3,5},{5,3},{7,1},{8,14},{10,12},{12... | collective-permute-start | bytes 1572872 | tf_op jit(solution)/shard_map/ppermute | solution.py:54
  64.6 21.0 %collective-permute-start.18 = (bf16[128,1024]{1,0:T(8,128)(2,1)}, bf16[128,1024]{1,0:T(8,128)(2,1)}, u32[]{:S(2)}, u32[]{:S(2)}) collective-permute-start(bf16[128,1024]{1,0:T(8,128)(2,1)} %get-tuple-element.70.refs_4_), channel_id=1, source_target_pairs={{0,16},{8,24},{16,0},{24,8},{1,17},{9,25},{17,1},{25,9},{2,18},{10... | collective-permute-start | bytes 786440 | tf_op jit(solution)/shard_map/ppermute | solution.py:54
  71.9 55.0 %collective-permute-start.23 = (bf16[2,128,1024]{2,1,0:T(8,128)(2,1)}, bf16[2,128,1024]{2,1,0:T(8,128)(2,1)}, u32[]{:S(2)}, u32[]{:S(2)}) collective-permute-start(bf16[2,128,1024]{2,1,0:T(8,128)(2,1)} %get-tuple-element.71.refs_8_), channel_id=1, source_target_pairs={{0,1},{1,0},{2,3},{3,2},{4,5},{5,4},{6,7},{7,6},{8,9},{9,8},{10,11... | collective-permute-start | bytes 1572872 | tf_op jit(solution)/shard_map/ppermute | solution.py:54
  83.6 43.3 %collective-permute-start.24 = (bf16[2,128,1024]{2,1,0:T(8,128)(2,1)}, bf16[2,128,1024]{2,1,0:T(8,128)(2,1)}, u32[]{:S(2)}, u32[]{:S(2)}) collective-permute-start(bf16[2,128,1024]{2,1,0:T(8,128)(2,1)} %collective-permute-done.20.refs_9_), channel_id=1, source_target_pairs={{0,1},{1,0},{2,3},{3,2},{4,5},{5,4},{6,7},{7,6},{8,9},{9,8},{10,11... | collective-permute-start | bytes 1572872 | tf_op jit(solution)/shard_map/ppermute | solution.py:54
  85.6 24.4 %collective-permute-start.11 = (bf16[128,256]{1,0:T(8,128)(2,1)S(1)}, bf16[128,256]{1,0:T(8,128)(2,1)S(1)}, u32[]{:S(2)}, u32[]{:S(2)}) collective-permute-start(bf16[128,256]{1,0:T(8,128)(2,1)S(1)} %get-tuple-element.130), channel_id=1, source_target_pairs={{0,8},{8,0},{16,24},{24,16},{1,9},{9,1},{17,25},{25,17},{2,10},{10... | collective-permute-start | bytes 196616 | tf_op jit(solution)/shard_map/ppermute | solution.py:54
  87.1 25.6 %collective-permute-start.12 = (bf16[128,256]{1,0:T(8,128)(2,1)S(1)}, bf16[128,256]{1,0:T(8,128)(2,1)S(1)}, u32[]{:S(2)}, u32[]{:S(2)}) collective-permute-start(bf16[128,256]{1,0:T(8,128)(2,1)S(1)} %get-tuple-element.129), channel_id=1, source_target_pairs={{0,16},{8,24},{16,0},{24,8},{1,17},{9,25},{17,1},{25,9},{2,18},{10... | collective-permute-start | bytes 196616 | tf_op jit(solution)/shard_map/ppermute | solution.py:54
  129.3 105.5 %reduce-scatter.2.cloned.1.call-start = ((), (), s32[]{:S(2)}) async-start(), calls=%async_computation.1 | async-start | bytes 589824 | tf_op jit(solution)/shard_map/reduce_scatter | solution.py:639
  158.7 48.2 %collective-permute-start.51 = (bf16[4,2,128,1024]{3,2,1,0:T(8,128)(2,1)}, bf16[4,2,128,1024]{3,2,1,0:T(8,128)(2,1)}, u32[]{:S(2)}, u32[]{:S(2)}) collective-permute-start(bf16[4,2,128,1024]{3,2,1,0:T(8,128)(2,1)} %get-tuple-element.109), channel_id=1, source_target_pairs={{0,1},{1,0},{2,3},{3,2},{4,5},{5,4},{6,7},{7,6},{8,9},{9,8},{10,11... | collective-permute-start | bytes 6291464 | tf_op jit(solution)/shard_map/ppermute | solution.py:54
  203.6 36.1 %collective-permute-start.39 = (bf16[128,1024]{1,0:T(8,128)(2,1)}, bf16[128,1024]{1,0:T(8,128)(2,1)}, u32[]{:S(2)}, u32[]{:S(2)}) collective-permute-start(bf16[128,1024]{1,0:T(8,128)(2,1)} %get-tuple-element.116), channel_id=1, source_target_pairs={{0,24},{8,16},{16,8},{24,0},{1,25},{9,17},{17,9},{25,1},{2,26},{10... | collective-permute-start | bytes 786440 | tf_op jit(solution)/shard_map/ppermute | solution.py:54
  206.8 34.2 %collective-permute-start.34 = (bf16[128,1024]{1,0:T(8,128)(2,1)}, bf16[128,1024]{1,0:T(8,128)(2,1)}, u32[]{:S(2)}, u32[]{:S(2)}) collective-permute-start(bf16[128,1024]{1,0:T(8,128)(2,1)} %get-tuple-element.122), channel_id=1, source_target_pairs={{0,8},{8,0},{16,24},{24,16},{1,9},{9,1},{17,25},{25,17},{2,10},{10... | collective-permute-start | bytes 786440 | tf_op jit(solution)/shard_map/ppermute | solution.py:54
  210.9 37.3 %collective-permute-start.52 = (bf16[2,128,1024]{2,1,0:T(8,128)(2,1)}, bf16[2,128,1024]{2,1,0:T(8,128)(2,1)}, u32[]{:S(2)}, u32[]{:S(2)}) collective-permute-start(bf16[2,128,1024]{2,1,0:T(8,128)(2,1)} %get-tuple-element.111), channel_id=1, source_target_pairs={{0,2},{2,0},{4,6},{6,4},{1,3},{3,1},{5,7},{7,5},{8,10},{10,8},{12,... | collective-permute-start | bytes 1572872 | tf_op jit(solution)/shard_map/ppermute | solution.py:54
  213.1 20.4 %collective-permute-start.42 = (bf16[272,384]{1,0:T(8,128)(2,1)S(1)}, bf16[272,384]{1,0:T(8,128)(2,1)S(1)}, u32[]{:S(2)}, u32[]{:S(2)}) collective-permute-start(bf16[272,384]{1,0:T(8,128)(2,1)S(1)} %get-tuple-element.103), channel_id=1, source_target_pairs={{0,4},{2,6},{4,0},{6,2},{1,5},{3,7},{5,1},{7,3},{8,12},{10,14},{12... | collective-permute-start | bytes 626696 | tf_op jit(solution)/shard_map/ppermute | solution.py:54
  234.1 36.1 %collective-permute-start.53 = (bf16[2,128,1024]{2,1,0:T(8,128)(2,1)}, bf16[2,128,1024]{2,1,0:T(8,128)(2,1)}, u32[]{:S(2)}, u32[]{:S(2)}) collective-permute-start(bf16[2,128,1024]{2,1,0:T(8,128)(2,1)} %get-tuple-element.112), channel_id=1, source_target_pairs={{0,4},{2,6},{4,0},{6,2},{1,5},{3,7},{5,1},{7,3},{8,12},{10,14},{12... | collective-permute-start | bytes 1572872 | tf_op jit(solution)/shard_map/ppermute | solution.py:54
  234.8 48.9 %collective-permute-start.54 = (bf16[2,128,1024]{2,1,0:T(8,128)(2,1)}, bf16[2,128,1024]{2,1,0:T(8,128)(2,1)}, u32[]{:S(2)}, u32[]{:S(2)}) collective-permute-start(bf16[2,128,1024]{2,1,0:T(8,128)(2,1)} %get-tuple-element.113), channel_id=1, source_target_pairs={{0,6},{2,4},{4,2},{6,0},{1,7},{3,5},{5,3},{7,1},{8,14},{10,12},{12... | collective-permute-start | bytes 1572872 | tf_op jit(solution)/shard_map/ppermute | solution.py:54
  246.9 40.2 %collective-permute-start.45 = (bf16[272,512]{1,0:T(8,128)(2,1)S(1)}, bf16[272,512]{1,0:T(8,128)(2,1)S(1)}, u32[]{:S(2)}, u32[]{:S(2)}) collective-permute-start(bf16[272,512]{1,0:T(8,128)(2,1)S(1)} %shard_map.258.p0), channel_id=1, source_target_pairs={{0,16},{8,24},{16,0},{24,8},{1,17},{9,25},{17,1},{25,9},{2,18},{10... | collective-permute-start | bytes 835592 | tf_op jit(solution)/shard_map/ppermute | solution.py:54
  247.7 40.3 %collective-permute-start.46 = (bf16[272,512]{1,0:T(8,128)(2,1)S(1)}, bf16[272,512]{1,0:T(8,128)(2,1)S(1)}, u32[]{:S(2)}, u32[]{:S(2)}) collective-permute-start(bf16[272,512]{1,0:T(8,128)(2,1)S(1)} %shard_map.258.p0), channel_id=1, source_target_pairs={{0,24},{8,16},{16,8},{24,0},{1,25},{9,17},{17,9},{25,1},{2,26},{10... | collective-permute-start | bytes 835592 | tf_op jit(solution)/shard_map/ppermute | solution.py:54
  248.2 37.6 %collective-permute-start.36 = (bf16[128,1024]{1,0:T(8,128)(2,1)}, bf16[128,1024]{1,0:T(8,128)(2,1)S(1)}, u32[]{:S(2)}, u32[]{:S(2)}) collective-permute-start(bf16[128,1024]{1,0:T(8,128)(2,1)} %get-tuple-element.120), channel_id=1, source_target_pairs={{0,24},{8,16},{16,8},{24,0},{1,25},{9,17},{17,9},{25,1},{2,26},{10... | collective-permute-start | bytes 786440 | tf_op jit(solution)/shard_map/ppermute | solution.py:54
  288.0 24.6 %collective-permute-start.57 = (bf16[2,128,1024]{2,1,0:T(8,128)(2,1)S(1)}, bf16[2,128,1024]{2,1,0:T(8,128)(2,1)S(1)}, u32[]{:S(2)}, u32[]{:S(2)}) collective-permute-start(bf16[2,128,1024]{2,1,0:T(8,128)(2,1)S(1)} %shard_map.261.p0), channel_id=1, source_target_pairs={{0,24},{8,16},{16,8},{24,0},{1,25},{9,17},{17,9},{25,1},{2,26},{10... | collective-permute-start | bytes 1572872 | tf_op jit(solution)/shard_map/ppermute | solution.py:54
  (103 other events, 1069.0 us)
Sparse Core Ops, SparseCore 0:
  21.1 35.7 all-gather.4
Sparse Core Ops, SparseCore 1:
  129.4 28.8 all-gather.6
  201.1 26.5 reduce-scatter.1
where the time goes:
time: 327 us; the launch traced here: 326 us
  waiting for transfers between devices  123 us (38%)
  starting transfers between devices  79 us (24%)
  Pallas kernels  54.8 us (17%)
  local copies, waits for them, and re-layouts  41.2 us (13%)
  between operations  16 us (5%)
  blocking collectives  11.9 us (4%)
    ppermute x62, waiting for transfers between devices, swap(): return lax.ppermute(value, axis, [(i, i ^ offset) for i in range(size)])  123 us
    ppermute x62, starting transfers between devices, swap(): return lax.ppermute(value, axis, [(i, i ^ offset) for i in range(size)])  78.7 us
    pallas_call x18, Pallas kernels, vmem_call(): pl.pallas_call(kernel, out_shape=[jax.ShapeDtypeStruct(s, t) for s, t in...  54.8 us
    unnamed x128, local copies, waits for them, and re-layouts  32.4 us
    all_gather x1, blocking collectives, tiled_body(): proj_full = lax.all_gather(proj_part, 'fsdp', axis=0)  11.9 us
  transfers between devices with their start and end apart: 65, of which 18 were waited for; matrix products, arithmetic and copies ran while one was open for 3% of the time, Pallas kernels for 16%

commit v1 on v0

--- a/solution.py
+++ b/solution.py
@@ -69,21 +69,44 @@
     return pl.ds(pl.multiple_of(start, LANE), size)
 
 
-def vmem_call(kernel, outs, args, hbm=(), scratch=(), flops=0):
+def vmem_call(kernel, outs, args, hbm=(), staged=(), scratch=(), flops=0, limit=16):
     moved = sum(a.size * a.dtype.itemsize for a in args)
     moved += sum(math.prod(s) * jnp.dtype(t).itemsize for s, t in outs)
     whole = pl.BlockSpec(memory_space=pltpu.VMEM)
+    far = pl.BlockSpec(memory_space=pl.ANY)
+    n, m, k = len(args), len(outs), len(staged)
+
+    def body(*refs):
+        ins, rest, held, sems = list(refs[:n]), refs[n:], refs[n + m : n + m + k], refs[n + m + k]
+        copies = [
+            pltpu.make_async_copy(ins[i], held[j], sems.at[j]) for j, i in enumerate(staged)
+        ]
+        for copy in copies:
+            copy.start()
+        for copy in copies:
+            copy.wait()
+        for j, i in enumerate(staged):
+            ins[i] = held[j]
+        kernel(*ins, *rest[:m], *rest[m + k + 1 :])
+
+    copied = [pltpu.VMEM(args[i].shape, args[i].dtype) for i in staged]
+    if staged:
+        copied.append(pltpu.SemaphoreType.DMA((k,)))
     return pl.pallas_call(
-        kernel,
+        body if staged else kernel,
         out_shape=[jax.ShapeDtypeStruct(s, t) for s, t in outs],
-        in_specs=[
-            pl.BlockSpec(memory_space=pl.ANY) if i in hbm else whole for i in range(len(args))
-        ],
-        out_specs=[whole] * len(outs),
-        scratch_shapes=list(scratch),
-        compiler_params=pltpu.CompilerParams(vmem_limit_bytes=40 * 1024 * 1024),
-        cost_estimate=pl.CostEstimate(flops=flops, bytes_accessed=moved, transcendentals=0),
+        in_specs=[far if i in hbm or i in staged else whole for i in range(n)],
+        out_specs=[whole] * m,
+        scratch_shapes=copied + list(scratch),
+        compiler_params=pltpu.CompilerParams(vmem_limit_bytes=limit * 1024 * 1024),
+        cost_estimate=pl.CostEstimate(
+            flops=flops * 8, bytes_accessed=moved * 8, transcendentals=0
+        ),
     )(*args)
+
+
+def after(value, *others):
+    return lax.optimization_barrier((value,) + others)[0]
 
 
 def mesh_place():
@@ -94,49 +117,65 @@
     return (read(refs[0]) + read(refs[1])) + (read(refs[2]) + read(refs[3]))
 
 
-def pack_kernel(qkv, vectors, packed, sems):
+def pack_kernel(*refs):
+    qkv, proj, x = refs[0:3]
+    vectors, (packed, x_copy, held, sems) = refs[3:-4], refs[-4:]
     rep, _, core = mesh_place()
+    mine = (rep * CORES + core) * LANE
+    parts = [qkv.at[:, lanes(t * WIDTH + mine, LANE)] for t in range(3)]
+    parts.append(proj.at[:, lanes(mine, LANE)])
+    targets = [packed.at[pl.ds(0, SHARD), pl.ds(t * LANE, LANE)] for t in range(4)]
+    parts += [x] * REPS
+    targets += [x_copy.at[pl.ds(k * ROWS, ROWS), :] for k in range(REPS)]
+    at = 0
+    for v in vectors:
+        parts.append(v)
+        targets.append(held.at[pl.ds(at, v.shape[0])])
+        at += v.shape[0]
     copies = [
-        pltpu.make_async_copy(
-            qkv.at[:, lanes(t * WIDTH + (rep * CORES + core) * LANE, LANE)],
-            packed.at[pl.ds(0, SHARD), pl.ds(t * LANE, LANE)],
-            sems.at[t],
-        )
-        for t in range(3)
+        pltpu.make_async_copy(part, target, sems.at[i])
+        for i, (part, target) in enumerate(zip(parts, targets))
     ]
     for copy in copies:
         copy.start()
-    packed[SHARD:, :] = vectors[...]
+    packed[SHARD:, SHARD:] = jnp.zeros((packed.shape[0] - SHARD, SHARD), bf16)
     for copy in copies:
         copy.wait()
-
-
-def unit_kernel(x0, x1, x2, x3, cot, fc, out, unit, scale, cot_copy, ff, sems):
-    rep, _, core = mesh_place()
-    piece = pl.ds(pl.multiple_of((rep * CORES + core) * LANE, LANE), LANE)
-    copies = [
-        pltpu.make_async_copy(fc.at[piece, :], ff.at[0], sems.at[0]),
-        pltpu.make_async_copy(out.at[piece, :], ff.at[1], sems.at[1]),
-        pltpu.make_async_copy(cot, cot_copy, sems.at[2]),
-    ]
-    for copy in copies:
-        copy.start()
-    for k, x in enumerate((x0, x1, x2, x3)):
-        unit[k * ROWS : (k + 1) * ROWS, :], spread = normalise(x[...].astype(f32))
-        if k == 0:
-            scale[...] = jnp.broadcast_to(spread, (ROWS, LANE))
-    for copy in copies:
-        copy.wait()
+    rows = [held[i * SHARD : (i + 1) * SHARD].astype(f32).reshape(1, SHARD) for i in range(8)]
+    biases = [held[i * SHARD : (i + 1) * SHARD].astype(f32).reshape(1, SHARD) for i in range(8, 12)]
+    rows.append(
+        jnp.where(
+            rep < 2,
+            jnp.where(rep == 0, biases[0], biases[1]),
+            jnp.where(rep == 2, biases[2], biases[3]),
+        )
+    )
+    rows.append(jnp.zeros((16 - len(rows), SHARD), f32))
+    packed[SHARD:, 0:SHARD] = jnp.concatenate(rows, 0).astype(bf16)
+
+
+def unit_kernel(x, unit, scale, unit_own):
+    for k in range(REPS):
+        at = pl.ds(k * ROWS, ROWS)
+        unit[at, :], spread = normalise(x[at, :].astype(f32))
+        scale[at, :] = jnp.broadcast_to(spread, (ROWS, LANE))
+    own = pl.ds(pl.multiple_of(lax.axis_index("rep") * ROWS, ROWS), ROWS)
+    unit_own[0] = unit[own, :]
+    unit_own[1, :, 0:LANE] = scale[own, :]
+    unit_own[1, :, LANE:] = jnp.zeros((ROWS, WIDTH - LANE), f32)
 
 
 def qkv_kernel(
-    unit, p0, p1, p2, p3, f0, f1, f2, f3, qkv, kv_send, normed, weight, vectors, biases
+    unit, p0, p1, p2, p3, f0, f1, f2, f3, qkv, kv_send, normed, weight, vectors, proj, biases
 ):
     rep, shard, core = mesh_place()
     for k, (own, far) in enumerate(((p0, f0), (p1, f1), (p2, f2), (p3, f3))):
         at = pl.ds(pl.multiple_of((shard ^ k) * SHARD, SHARD), SHARD)
-        weight[at, 0:TRIPLE] = own[0:SHARD, :]
-        weight[at, TRIPLE : 2 * TRIPLE] = far[0:SHARD, :]
+        weight[at, 0:TRIPLE] = own[0:SHARD, 0:TRIPLE]
+        weight[at, TRIPLE : 2 * TRIPLE] = far[0:SHARD, 0:TRIPLE]
+        for a in range(REPS):
+            start = a * WIDTH + (shard ^ k) * SHARD
+            proj[pl.ds(pl.multiple_of(start, SHARD), SHARD), :] = own[0:SHARD, TRIPLE:]
         vectors[:, at] = own[SHARD:, 0:SHARD].astype(f32)
     for p in range(CORES):
         for t, at in ((0, 0), (2, 2)):
@@ -185,9 +224,8 @@
     core = lax.axis_index("seq")
     causal, far_seen, first = head_masks(core)
 
-    @pl.loop(0, REPS)
-    def _(sequence):
-        at = pl.ds(pl.multiple_of(sequence * ROWS, ROWS), ROWS)
+    for sequence in range(REPS):
+        at = pl.ds(sequence * ROWS, ROWS)
         for p in range(CORES):
             base = p * TRIPLE
             query = qkv[at, base : base + LANE]
@@ -206,73 +244,72 @@
             attended[at, p * LANE : (p + 1) * LANE] = jnp.where(first, *heads).astype(bf16)
 
 
-def branch_kernel(a0, a1, a2, a3, x, proj, vectors, middle, unit, scale, normed, joined):
-    rep, _, core = mesh_place()
-    for k, a in enumerate((a0, a1, a2, a3)):
+def branch_kernel(a, own, far, x, vectors, middle, unit, scale, normed, proj, joined):
+    core = lax.axis_index("seq")
+    for k in range(REPS):
+        for p, piece in enumerate((own, far)):
+            proj[:, lanes((k * CORES + (core ^ p)) * LANE, LANE)] = piece[
+                k * WIDTH : (k + 1) * WIDTH, :
+            ]
+    for k in range(REPS):
         for p in range(CORES):
-            at = lanes(((rep ^ k) * CORES + (core ^ p)) * LANE, LANE)
-            joined[:, at] = a[:, p * LANE : (p + 1) * LANE]
+            at = lanes((k * CORES + (core ^ p)) * LANE, LANE)
+            joined[:, at] = a[k * ROWS : (k + 1) * ROWS, p * LANE : (p + 1) * LANE]
     branch = jnp.dot(joined[...], proj[...], preferred_element_type=f32)
     values = x[...].astype(f32) + branch + vectors[4:5, :]
     middle[...] = values
     norm, spread = normalise(values)
     unit[...] = norm
     scale[...] = jnp.broadcast_to(spread, (ROWS, LANE))
-    normed[...] = (norm * vectors[5:6, :] + vectors[6:7, :]).astype(bf16)
-
-
-def hidden_kernel(*refs):
-    h, c, own, far = refs[0:4], refs[4:8], refs[8:12], refs[12:16]
-    vectors, back, hidden, pre_grad, fc, out, h_all, c_all, bias = refs[16:]
-    _, shard, core = mesh_place()
-    for j, ff in enumerate((own, far)):
-        for k in range(SHARDS):
-            at = pl.ds((j * SHARDS + k) * LANE, LANE)
-            fc[at, :] = ff[k][0]
-            out[at, :] = ff[k][1]
-            start = (shard ^ k) * SHARD + (core ^ j) * LANE
-            bias[:, at] = jnp.broadcast_to(vectors[8:9, lanes(start, LANE)], (8, LANE))
+    low = (norm * vectors[5:6, :] + vectors[6:7, :]).astype(bf16)
     for k in range(REPS):
-        at = pl.ds(k * ROWS, ROWS)
-        h_all[at, :] = h[k][...]
-        c_all[at, :] = c[k][...]
+        normed[k * ROWS : (k + 1) * ROWS, :] = low
+
+
+def hidden_kernel(h, c0, c1, c2, c3, ff, vectors, back, hidden, pre_grad, c):
+    rep = lax.axis_index("rep")
+    for k, cot in enumerate((c0, c1, c2, c3)):
+        c[pl.ds(pl.multiple_of((rep ^ k) * ROWS, ROWS), ROWS), :] = cot[...]
 
     @pl.loop(0, 2)
     def _(block):
         at = pl.ds(pl.multiple_of(block * 2 * ROWS, 2 * ROWS), 2 * ROWS)
-        for n in range(HIDDEN // 256):
-            tile = pl.ds(n * 256, 256)
-            preact = dot_rows(h_all[at, :], fc[tile, :]) + bias[0:1, tile]
+        for n in range(SHARDS):
+            tile = pl.ds(n * 2 * LANE, 2 * LANE)
+            pair = pl.ds(n * CORES, CORES)
+            fc, out = ff[pair, 0].reshape(-1, WIDTH), ff[pair, 1].reshape(-1, WIDTH)
+            preact = dot_rows(h[at, :], fc) + vectors[8:9, tile]
             value, slope = gelu_and_slope(preact)
             hidden[at, tile] = value.astype(bf16)
-            grad = dot_rows(c_all[at, :], out[tile, :])
+            grad = dot_rows(c[at, :], out)
             pre_grad[at, tile] = (grad * slope).astype(bf16)
-        back[at, :] = jnp.dot(pre_grad[at, :], fc[...], preferred_element_type=f32).astype(bf16)
-
-
-def weights_kernel(hidden, pre_grad, h_all, c_all, out, output, own, far, sums):
-    @pl.loop(0, 2)
-    def _(block):
-        at = pl.ds(pl.multiple_of(block * 2 * ROWS, 2 * ROWS), 2 * ROWS)
-        output[at, :] = jnp.dot(hidden[at, :], out[...], preferred_element_type=f32).astype(bf16)
-
+        fc = ff[:, 0].reshape(HIDDEN, WIDTH)
+        back[at, :] = jnp.dot(pre_grad[at, :], fc, preferred_element_type=f32).astype(bf16)
+
+
+def weights_kernel(hidden, pre_grad, h, c, ff, output, grads, sums):
+    for n in range(SHARDS):
+        tile = pl.ds(n * 2 * LANE, 2 * LANE)
+        for i, (left, right) in enumerate(((pre_grad, h), (hidden, c))):
+            grad = contract(left[:, tile], right[...], 0, 0).astype(bf16)
+            for j in range(CORES):
+                grads[(n * CORES + j) * 2 + i] = grad[j * LANE : (j + 1) * LANE]
     sums[...] = jnp.broadcast_to(
         jnp.sum(pre_grad[...].astype(f32), 0, keepdims=True), sums.shape
     )
-    for j, grads in enumerate((own, far)):
-        for k in range(0, SHARDS, 2):
-            tile = pl.ds((j * SHARDS + k) * LANE, 2 * LANE)
-            for i, (left, right) in enumerate(((pre_grad, h_all), (hidden, c_all))):
-                grad = contract(left[:, tile], right[...], 0, 0).astype(bf16)
-                grads[k, i] = grad[0:LANE]
-                grads[k + 1, i] = grad[LANE:]
+
+    @pl.loop(0, REPS)
+    def _(block):
+        at = pl.ds(pl.multiple_of(block * ROWS, ROWS), ROWS)
+        out = ff[:, 1].reshape(HIDDEN, WIDTH)
+        output[at, :] = jnp.dot(hidden[at, :], out, preferred_element_type=f32).astype(bf16)
 
 
 def middle_kernel(
-    g0, g1, g2, g3, unit, scale, vectors, cot, proj, middle_grad, o0, o1, o2, o3, sums, low, back
+    g, unit, scale, vectors, cot, proj, middle_grad, pairs, sums, low, back
 ):
     rep, _, core = mesh_place()
-    grad = total((g0, g1, g2, g3), lambda g: g[...].astype(f32))
+    grad = total(range(REPS), lambda k: g[k * ROWS : (k + 1) * ROWS, :].astype(f32))
     part, gain, shift = norm_pull(unit[...], scale[:, 0:1], vectors[5:6, :], grad)
     cots = cot[...].astype(f32)
     values = cots + part
@@ -284,39 +321,32 @@
     for i, row in enumerate(rows):
         sums[i : i + 1, :] = row[None]
     sums[4:8, :] = jnp.zeros((4, WIDTH), f32)
-    for k, o in enumerate((o0, o1, o2, o3)):
+    for k in range(REPS):
+        rows = pl.ds(k * ROWS, ROWS)
         for p in range(CORES):
-            at = lanes(((rep ^ k) * CORES + (core ^ p)) * LANE, LANE)
-            o[:, p * LANE : (p + 1) * LANE] = back[:, at]
-        o[:, SHARD : 2 * SHARD] = low[:, lanes((rep ^ k) * SHARD, SHARD)]
-
-
-def proj_grad_kernel(attended, b0, b1, b2, b3, grads, cols):
-    rep, _, core = mesh_place()
-    for k, b in enumerate((b0, b1, b2, b3)):
-        cols[k * ROWS : (k + 1) * ROWS, :] = b[:, SHARD : 2 * SHARD]
-    for a in range(REPS):
-        blocks = [
-            cols[pl.ds(pl.multiple_of((a ^ j ^ rep) * ROWS, ROWS), ROWS), :] for j in range(REPS)
-        ]
-        grad = contract(attended[a], jnp.concatenate(blocks, 0), 0, 0).astype(bf16)
+            at = lanes((k * CORES + (core ^ p)) * LANE, LANE)
+            pairs[rows, p * LANE : (p + 1) * LANE] = back[:, at]
+        pairs[rows, SHARD : 2 * SHARD] = low[:, k * SHARD : (k + 1) * SHARD]
+
+
+def proj_grad_kernel(a0, a1, a2, a3, pairs, own, far):
+    rep, shard, core = mesh_place()
+    for k, a in enumerate((a0, a1, a2, a3)):
+        grad = contract(a[...], pairs[:, SHARD : 2 * SHARD], 0, 0).astype(bf16)
+        mine = jnp.where(core == 0, grad[:, 0:LANE], grad[:, LANE:])
+        other = jnp.where(core == 0, grad[:, LANE:], grad[:, 0:LANE])
         for p in range(CORES):
-            for j in range(CORES):
-                start = (a * CORES + j) * SHARD + (core ^ p) * LANE
-                grads[pl.ds(pl.multiple_of(start, LANE), LANE), :] = grad[
-                    p * LANE : (p + 1) * LANE, j * LANE : (j + 1) * LANE
-                ]
-
-
-def attend_back_kernel(qkv, far, b0, b1, b2, b3, query_grad, own_grad, far_grad, grads):
+            at = pl.ds(pl.multiple_of((core ^ p) * LANE, LANE), LANE)
+            own[rep ^ k ^ shard, at, :] = mine[p * LANE : (p + 1) * LANE]
+            far[rep ^ k ^ shard, at, :] = other[p * LANE : (p + 1) * LANE]
+
+
+def attend_back_kernel(qkv, far, pairs, query_grad, own_grad, far_grad):
     core = lax.axis_index("seq")
     causal, far_seen, first = head_masks(core)
-    for k, b in enumerate((b0, b1, b2, b3)):
-        grads[k * ROWS : (k + 1) * ROWS, :] = b[:, 0 : 2 * LANE]
-
-    @pl.loop(0, REPS)
-    def _(sequence):
-        at = pl.ds(pl.multiple_of(sequence * ROWS, ROWS), ROWS)
+
+    for sequence in range(REPS):
+        at = pl.ds(sequence * ROWS, ROWS)
         for p in range(CORES):
             base = p * TRIPLE
             query = qkv[at, base : base + LANE]
@@ -324,7 +354,7 @@
             value_own = qkv[at, base + 2 * LANE : base + 3 * LANE]
             key_far = far[at, 2 * p * LANE : (2 * p + 1) * LANE]
             value_far = far[at, (2 * p + 1) * LANE : (2 * p + 2) * LANE]
-            grad = grads[at, p * LANE : (p + 1) * LANE]
+            grad = pairs[at, p * LANE : (p + 1) * LANE]
             queries, sums = [], [0.0] * 4
             for mask in (first, ~first):
                 masked = jnp.where(mask, query, jnp.zeros_like(query))
@@ -359,7 +389,22 @@
 
 
 def qkv_back_kernel(
-    query_grad, own_grad, far_grad, weight, normed, unit, ff_sums, mid_sums, own, far, joined, small, mixed, sums
+    query_grad,
+    own_grad,
+    far_grad,
+    weight,
+    normed,
+    unit,
+    ff_sums,
+    mid_sums,
+    proj_own,
+    proj_far,
+    own,
+    far,
+    joined,
+    small,
+    mixed,
+    sums,
 ):
     rep, shard, core = mesh_place()
     for p in range(CORES):
@@ -372,8 +417,10 @@
     for k in range(SHARDS):
         at = lanes((shard ^ k) * SHARD, SHARD)
         grad = contract(normed[:, at], mixed[...], 0, 0).astype(bf16)
-        own[k] = grad[:, 0:TRIPLE]
-        far[k] = grad[:, TRIPLE:]
+        own[k, :, 0:TRIPLE] = grad[:, 0:TRIPLE]
+        far[k, :, 0:TRIPLE] = grad[:, TRIPLE:]
+        own[k, :, TRIPLE:] = proj_own[k]
+        far[k, :, TRIPLE:] = proj_far[k]
     gain = jnp.zeros((1, WIDTH), f32)
     shift = jnp.zeros((1, WIDTH), f32)
     for k in range(REPS):
@@ -402,10 +449,9 @@
         small[k, 3:4, 0:SHARD] = jnp.where(rep % 2 == 1, queries + values, 0.0)
         for i in range(4):
             small[k, 4 + i : 5 + i, 0:SHARD] = mid_sums[i : i + 1, at]
-        for j in range(CORES):
-            part = ff_sums[:, (j * SHARDS + k) * LANE : (j * SHARDS + k + 1) * LANE]
-            row = lax.broadcasted_iota(jnp.int32, part.shape, 0)
-            small[k, 8:16, lanes((core ^ j) * LANE, LANE)] = jnp.where(row == rep, part, 0.0)
+        part = ff_sums[:, at]
+        row = lax.broadcasted_iota(jnp.int32, part.shape, 0)
+        small[k, 8:16, 0:SHARD] = jnp.where(row == rep, part, 0.0)
 
 
 def tail_kernel(own, far, small, o0, o1, o2, o3):
@@ -414,18 +460,20 @@
         o[SHARD:, :] = small[k].astype(bf16)
 
 
-def gather_tail_kernel(p0, p1, p2, p3, proj, o):
-    o[:, 0:TRIPLE] = total((p0, p1, p2, p3), lambda p: p[...].astype(f32)).astype(bf16)
-    o[0:SHARD, TRIPLE:] = proj[...]
-    o[SHARD:, TRIPLE:] = jnp.zeros((o.shape[0] - SHARD, LANE), bf16)
-
-
-def input_kernel(j0, j1, j2, j3, r0, r1, r2, r3, unit, scale, vectors, middle_grad, middle, block, grad):
-    back = total((j0, j1, j2, j3), lambda g: g[...].astype(f32))
-    output = total((r0, r1, r2, r3), lambda g: g[...].astype(f32))
+def input_kernel(j, unit, vectors, middle_grad, grad):
+    back = total(range(REPS), lambda k: j[k * ROWS : (k + 1) * ROWS, :].astype(f32))
+    part, _, _ = norm_pull(unit[0], unit[1, :, 0:1], vectors[0:1, :], back)
+    grad[...] = middle_grad[...] + part
+
+
+def block_kernel(j, middle, vectors, block):
+    output = total(range(REPS), lambda k: j[k * ROWS : (k + 1) * ROWS, :].astype(f32))
     block[...] = (middle[...] + output + vectors[7:8, :]).astype(bf16)
-    part, _, _ = norm_pull(unit[0:ROWS, :], scale[:, 0:1], vectors[0:1, :], back)
-    grad[...] = middle_grad[...] + part
+
+
+def joined_sum(pieces):
+    pieces = [p.astype(f32) for p in pieces]
+    return ((pieces[0] + pieces[1]) + (pieces[2] + pieces[3])).astype(bf16)
 
 
 def final_kernel(p0, p1, p2, p3, f0, f1, f2, f3, qkv, proj, small):
@@ -452,15 +500,6 @@
             at = pl.ds(pl.multiple_of(((rep ^ k) * CORES + (core ^ j)) * LANE, LANE), LANE)
             fc[at, :] = piece[0].astype(f32)
             out[at, :] = piece[1].astype(f32)
-
-
-def add_kernel(own, far, o0, o1, o2, o3):
-    for k, o in enumerate((o0, o1, o2, o3)):
-        o[...] = (own[k].astype(f32) + far[k].astype(f32)).astype(bf16)
-
-
-def sum_kernel(p0, p1, p2, p3, o):
-    o[...] = total((p0, p1, p2, p3), lambda p: p[...].astype(f32)).astype(bf16)
 
 
 def tiled_body(
@@ -491,53 +530,41 @@
         return swap(value, "seq", CORES, 1)
 
     all_rows = REPS * ROWS
-    fc_bias_part = pick(fc_bias.reshape(REPS, -1), rep, 0)
     vectors = [
         ln1_gain,
         ln1_shift,
-        qv_bias[:SHARD],
-        qv_bias[SHARD:],
+        qv_bias,
         proj_bias,
         ln2_gain,
         ln2_shift,
         out_bias,
-        fc_bias_part,
+        fc_bias,
     ]
-    vectors = jnp.stack(vectors + [jnp.zeros_like(ln1_gain)] * (16 - len(vectors)))
-    vectors = jnp.pad(vectors, ((0, 0), (0, TRIPLE - SHARD)))
-    (packed,) = vmem_call(
+    packed, own_rows = vmem_call(
         pack_kernel,
-        [((SHARD + 16, TRIPLE), bf16)],
-        [qkv_weight, vectors],
-        hbm=(0,),
-        scratch=[pltpu.SemaphoreType.DMA((3,))],
+        [((SHARD + 16, TRIPLE + LANE), bf16), ((all_rows, WIDTH), bf16)],
+        [qkv_weight, proj_weight, block_input] + vectors,
+        hbm=tuple(range(11)),
+        scratch=[pltpu.VMEM((12 * SHARD,), bf16), pltpu.SemaphoreType.DMA((16,))],
+        limit=56,
     )
     own_packed = over_shards([packed] * SHARDS)
     far_packed = [over_cores(p) for p in own_packed]
-    inputs = over_rep([block_input] * REPS)
-
-    proj_part = pick(proj_weight.reshape(REPS * CORES, -1, WIDTH), rep * CORES + core, 0)
-    proj_full = lax.all_gather(proj_part, "fsdp", axis=0)
-    proj_full = lax.all_gather(proj_full, ("rep", "seq"), axis=1)
-    proj_full = proj_full.reshape(WIDTH, WIDTH)
-
-    unit_one, scale_one, own_cot, ff = vmem_call(
+    inputs = lax.all_to_all(own_rows, "rep", 0, 0, tiled=True)
+
+    unit_one, _, unit_own = vmem_call(
         unit_kernel,
-        [
-            ((all_rows, WIDTH), f32),
-            ((ROWS, LANE), f32),
-            ((ROWS, WIDTH), bf16),
-            ((2, LANE, WIDTH), bf16),
-        ],
-        inputs + [cotangent, fc_weight, out_weight],
-        hbm=(4, 5, 6),
-        scratch=[pltpu.SemaphoreType.DMA((3,))],
-    )
-    cots = over_rep([own_cot] * REPS)
-    own_ff = over_shards([ff] * SHARDS)
-    far_ff = [over_cores(f) for f in own_ff]
-
-    qkv, kv_send, normed_one, qkv_mine, vectors = vmem_call(
+        [((all_rows, WIDTH), f32), ((all_rows, LANE), f32), ((2, ROWS, WIDTH), f32)],
+        [inputs],
+    )
+    cots = over_rep([after(cotangent, unit_one)] * REPS)
+
+    mine = rep * CORES + core
+    ff = [pick(w.reshape(REPS * CORES, LANE, WIDTH), mine, 0) for w in (fc_weight, out_weight)]
+    ff = after(jnp.stack(ff), *own_packed[1:], inputs)
+    ff = lax.all_gather(ff, ("fsdp", "seq"), axis=0)
+
+    qkv, kv_send, normed_one, qkv_mine, vectors, proj_cols = vmem_call(
         qkv_kernel,
         [
             ((all_rows, 2 * TRIPLE), bf16),
@@ -545,79 +572,71 @@
             ((all_rows, WIDTH), bf16),
             ((WIDTH, 2 * TRIPLE), bf16),
             ((16, WIDTH), f32),
+            ((REPS * WIDTH, LANE), bf16),
         ],
         [unit_one] + own_packed + far_packed,
         scratch=[pltpu.VMEM((8, 2 * TRIPLE), f32)],
         flops=2 * all_rows * WIDTH * 2 * TRIPLE,
     )
     kv_far = over_cores(kv_send)
+    proj_cols = lax.all_to_all(proj_cols, "rep", 0, 0, tiled=True)
     (attended,) = vmem_call(
         attend_kernel,
         [((all_rows, SHARD), bf16)],
         [qkv, kv_far],
         flops=4 * all_rows * 2 * ROWS * SHARD,
     )
-    mine = over_rep([attended[k * ROWS : (k + 1) * ROWS] for k in range(REPS)])
-    middle, unit_two, scale_two, normed_two = vmem_call(
+    mine = lax.all_to_all(attended, "rep", 0, 0, tiled=True)
+    middle, unit_two, scale_two, normed_two, proj_full = vmem_call(
         branch_kernel,
         [
             ((ROWS, WIDTH), f32),
             ((ROWS, WIDTH), f32),
             ((ROWS, LANE), f32),
-            ((ROWS, WIDTH), bf16),
+            ((all_rows, WIDTH), bf16),
+            ((WIDTH, WIDTH), bf16),
         ],
-        mine + [block_input, proj_full, vectors],
+        [after(mine, *cots[1:]), proj_cols, over_cores(after(proj_cols, attended)), block_input, vectors],
         scratch=[pltpu.VMEM((ROWS, WIDTH), bf16)],
         flops=2 * ROWS * WIDTH * WIDTH,
     )
-    normed_two = over_rep([normed_two] * REPS)
-    attended_all = lax.all_gather(attended, "rep", axis=0)
-
-    back, hidden, pre_grad, _, out_mine, h_all, c_all, _ = vmem_call(
+    normed_two = lax.all_to_all(normed_two, "rep", 0, 0, tiled=True)
+    attended_all = over_rep([after(attended, normed_two)] * REPS)
+
+    back, hidden, pre_grad, c_all = vmem_call(
         hidden_kernel,
         [
-            ((all_rows, WIDTH), bf16),
             ((all_rows, HIDDEN), bf16),
             ((all_rows, HIDDEN), bf16),
-            ((HIDDEN, WIDTH), bf16),
-            ((HIDDEN, WIDTH), bf16),
             ((all_rows, WIDTH), bf16),
             ((all_rows, WIDTH), bf16),
-            ((8, HIDDEN), f32),
         ],
-        normed_two + cots + own_ff + far_ff + [vectors],
+        [normed_two] + cots + [ff, vectors],
         flops=6 * all_rows * WIDTH * HIDDEN,
     )
-    back = over_rep([back[k * ROWS : (k + 1) * ROWS] for k in range(REPS)])
-    output, ff_own, ff_far, ff_sums = vmem_call(
+    back = lax.all_to_all(back, "rep", 0, 0, tiled=True)
+    output, ff_grads, ff_sums = vmem_call(
         weights_kernel,
         [
             ((all_rows, WIDTH), bf16),
-            ((SHARDS, 2, LANE, WIDTH), bf16),
-            ((SHARDS, 2, LANE, WIDTH), bf16),
+            ((SHARDS * CORES * 2, LANE, WIDTH), bf16),
             ((8, HIDDEN), f32),
         ],
-        [hidden, pre_grad, h_all, c_all, out_mine],
+        [after(hidden, *attended_all[1:]), pre_grad, normed_two, c_all, ff],
         flops=6 * all_rows * WIDTH * HIDDEN,
     )
-    piece = ((2, LANE, WIDTH), bf16)
-    ff_pieces = vmem_call(add_kernel, [piece] * SHARDS, [ff_own, over_cores(ff_far)])
-    (ff_piece,) = vmem_call(sum_kernel, [piece], over_shards(ff_pieces))
-    ff_pieces = over_rep([ff_piece] * REPS)
-    fc_grads, out_grads = vmem_call(
-        spread_kernel,
-        [((2 * REPS * LANE, WIDTH), f32)] * 2,
-        ff_pieces + [over_cores(p) for p in ff_pieces],
-    )
-
-    middle_grad, o0, o1, o2, o3, mid_sums = vmem_call(
+    ff_piece = lax.psum_scatter(ff_grads, ("fsdp", "seq"), scatter_dimension=0, tiled=True)
+
+    middle_grad, pairs, mid_sums = vmem_call(
         middle_kernel,
-        [((ROWS, WIDTH), f32)] + [((ROWS, 2 * SHARD), bf16)] * REPS + [((8, WIDTH), f32)],
-        back + [unit_two, scale_two, vectors, cotangent, proj_full],
+        [((ROWS, WIDTH), f32), ((all_rows, 2 * SHARD), bf16), ((8, WIDTH), f32)],
+        [back, unit_two, scale_two, vectors, cotangent, proj_full],
         scratch=[pltpu.VMEM((ROWS, WIDTH), bf16)] * 2,
         flops=2 * ROWS * WIDTH * WIDTH,
     )
-    pairs = over_rep([o0, o1, o2, o3])
+    pairs = lax.all_to_all(pairs, "rep", 0, 0, tiled=True)
+    output = lax.all_to_all(after(output, pairs), "rep", 0, 0, tiled=True)
+    (block_output,) = vmem_call(block_kernel, [((ROWS, WIDTH), bf16)], [output, middle, vectors])
     query_grad, own_grad, far_grad = vmem_call(
         attend_back_kernel,
         [
@@ -625,53 +644,50 @@
             ((all_rows, 4 * LANE), f32),
             ((all_rows, 4 * LANE), bf16),
         ],
-        [qkv, kv_far] + pairs,
-        scratch=[pltpu.VMEM((all_rows, SHARD), bf16)],
+        [qkv, kv_far, pairs],
         flops=10 * all_rows * 2 * ROWS * SHARD,
     )
-    (proj_grads,) = vmem_call(
+    proj_own, proj_far = vmem_call(
         proj_grad_kernel,
-        [((WIDTH * CORES, LANE), bf16)],
-        [attended_all] + pairs,
-        scratch=[pltpu.VMEM((all_rows, SHARD), bf16)],
+        [((SHARDS, SHARD, LANE), bf16)] * 2,
+        attended_all + [pairs],
         flops=2 * all_rows * WIDTH * SHARD,
     )
-    proj_grads = lax.psum_scatter(proj_grads, ("fsdp", "seq"), scatter_dimension=0, tiled=True)
-
     qkv_own, qkv_far, joined, small = vmem_call(
         qkv_back_kernel,
         [
-            ((SHARDS, SHARD, TRIPLE), bf16),
-            ((SHARDS, SHARD, TRIPLE), bf16),
+            ((SHARDS, SHARD, TRIPLE + LANE), bf16),
+            ((SHARDS, SHARD, TRIPLE + LANE), bf16),
             ((all_rows, WIDTH), bf16),
-            ((SHARDS, 16, TRIPLE), f32),
+            ((SHARDS, 16, TRIPLE + LANE), f32),
         ],
-        [query_grad, own_grad, over_cores(far_grad), qkv_mine, normed_one, unit_one, ff_sums, mid_sums],
+        [query_grad, own_grad, over_cores(far_grad), qkv_mine, normed_one, unit_one, ff_sums, mid_sums]
+        + [proj_own, proj_far],
         scratch=[pltpu.VMEM((all_rows, 2 * TRIPLE), bf16), pltpu.VMEM((8, WIDTH), f32)],
         flops=4 * all_rows * WIDTH * 2 * TRIPLE,
     )
     tail = vmem_call(
         tail_kernel,
-        [((SHARD + 16, TRIPLE), bf16)] * SHARDS,
-        [qkv_own, over_cores(qkv_far), small],
-    )
-    (tail,) = vmem_call(
-        gather_tail_kernel,
-        [((SHARD + 16, TRIPLE + LANE), bf16)],
-        over_shards(tail) + [proj_grads],
+        [((SHARD + 16, TRIPLE + LANE), bf16)] * SHARDS,
+        [qkv_own, over_cores(qkv_far), after(small, block_output)],
+    )
+    tail = over_shards(tail)
+    joined = lax.all_to_all(joined, "rep", 0, 0, tiled=True)
+    ff_pieces = over_rep([ff_piece] * REPS)
+    tail = joined_sum([after(tail[0], joined, *ff_pieces[1:])] + tail[1:])
+    (input_grad,) = vmem_call(
+        input_kernel, [((ROWS, WIDTH), f32)], [joined, unit_own, vectors, middle_grad]
     )
     tail = over_rep([tail] * REPS)
+    fc_grads, out_grads = vmem_call(
+        spread_kernel,
+        [((2 * REPS * LANE, WIDTH), f32)] * 2,
+        ff_pieces + [over_cores(after(p, tail[1])) for p in ff_pieces],
+    )
     qkv_grads, proj_grads, small = vmem_call(
         final_kernel,
         [((SHARD, 3 * WIDTH), f32), ((SHARD, WIDTH), f32), ((16, SHARD), f32)],
         tail + [over_cores(t) for t in tail],
-    )
-    joined = over_rep([joined[k * ROWS : (k + 1) * ROWS] for k in range(REPS)])
-    output = over_rep([output[k * ROWS : (k + 1) * ROWS] for k in range(REPS)])
-    block_output, input_grad = vmem_call(
-        input_kernel,
-        [((ROWS, WIDTH), bf16), ((ROWS, WIDTH), f32)],
-        joined + output + [unit_one, scale_one, vectors, middle_grad, middle],
     )
     return (
         block_output,

time: 327 us -> 262 us (0.80)
  waiting for transfers between devices: 123 us -> 68.6 us
  blocking collectives: 11.9 us -> 37.8 us
  starting transfers between devices: 79 us -> 59.3 us
  local copies, waits for them, and re-layouts: 41.2 us -> 23.3 us
    ppermute x62 -> x34, waiting for transfers between devices: 123 us -> 51.4 us  [swap(): return lax.ppermute(value, axis, [(i, i ^ offset) for i in range(size)])]
    all_to_all x0 -> x3, blocking collectives: none -> 37.8 us  [the longest x1 15.5 us: tiled_body(): normed_two = lax.all_to_all(normed_two, 'rep', 0, 0, tiled=True)]
    ppermute x62 -> x34, starting transfers between devices: 78.7 us -> 41.3 us  [swap(): return lax.ppermute(value, axis, [(i, i ^ offset) for i in range(size)])]
    all_to_all x0 -> x5, starting transfers between devices: none -> 17.8 us  [the longest x1 3.74 us: tiled_body(): joined = lax.all_to_all(joined, 'rep', 0, 0, tiled=True)]
    all_to_all x0 -> x5, waiting for transfers between devices: none -> 17.2 us  [the longest x1 9.67 us: tiled_body(): joined = lax.all_to_all(joined, 'rep', 0, 0, tiled=True)]
    all_gather x1 -> x0, blocking collectives: 11.9 us -> none  [tiled_body(): proj_full = lax.all_gather(proj_part, 'fsdp', axis=0)]
    unnamed x128 -> x84, local copies, waits for them, and re-layouts: 32.4 us -> 21.6 us
    another operation x12 -> x0, local copies, waits for them, and re-layouts: 4.03 us -> none  [tiled_body(): jnp.stack(vectors + [jnp.zeros_like(ln1_gain)] * (16 - len(vectors)))]
  transfers between devices with their start and end apart: 65 -> 41, of which waited for: 18 -> 15; matrix products, arithmetic and copies ran while one was open for 3% -> 1% of each run, Pallas kernels for 16% -> 16%
where the time goes in v1:
time: 262 us; the launch traced here: 261 us
  waiting for transfers between devices  68.6 us (26%)
  starting transfers between devices  59.3 us (23%)
  Pallas kernels  55.9 us (21%)
  blocking collectives  37.8 us (14%)
  local copies, waits for them, and re-layouts  23.3 us (9%)
  between operations  14.4 us (5%)
    pallas_call x16, Pallas kernels, vmem_call(): pl.pallas_call(body if staged else kernel, out_shape=[jax.ShapeDtypeStruc...  55.9 us
    ppermute x34, waiting for transfers between devices, swap(): return lax.ppermute(value, axis, [(i, i ^ offset) for i in range(size)])  51.4 us
    ppermute x34, starting transfers between devices, swap(): return lax.ppermute(value, axis, [(i, i ^ offset) for i in range(size)])  41.3 us
    unnamed x84, local copies, waits for them, and re-layouts  21.6 us
    all_to_all x1, blocking collectives, tiled_body(): normed_two = lax.all_to_all(normed_two, 'rep', 0, 0, tiled=True)  15.5 us
    all_to_all x1, blocking collectives, tiled_body(): back = lax.all_to_all(back, 'rep', 0, 0, tiled=True)  13.9 us
    all_to_all x1, waiting for transfers between devices, tiled_body(): joined = lax.all_to_all(joined, 'rep', 0, 0, tiled=True)  9.67 us
    all_to_all x1, blocking collectives, tiled_body(): pairs = lax.all_to_all(pairs, 'rep', 0, 0, tiled=True)  8.38 us
  transfers between devices with their start and end apart: 41, of which 15 were waited for; matrix products, arithmetic and copies ran while one was open for 1% of the time, Pallas kernels for 16%

profile of v1, /device:TPU:9, one launch (start us, length us, event | category | flops | bytes accessed | tf_op | source)
XLA Modules:
  0.0 261.4 jit_solution(16843616381305736419)
XLA Ops:
  9.8 3.7 %all-to-all-start = ((bf16[4,128,1024]{2,1,0:T(8,128)(2,1)}), bf16[4,128,1024]{2,1,0:T(8,128)(2,1)S(1)}, u32[]{:S(2)}, u32[]{:S(2)}) async-start(bf16[4,128,1024]{2,1,0:T(8,128)(2,1)} %bitcast.48), calls=%async_computation | async-start | bytes 2097152 | tf_op jit(solution)/shard_map/all_to_all | solution.py:553
  18.2 5.1 %collective-permute-done.p1 = bf16[272,512]{1,0:T(8,128)(2,1)S(1)} collective-permute-done((bf16[272,512]{1,0:T(8,128)(2,1)S(1)}, bf16[272,512]{1,0:T(8,128)(2,1)S(1)}, u32[]{:S(2)}, u32[]{:S(2)}) %collective-permute-start) | collective-permute-done | bytes 278560 | tf_op jit(solution)/shard_map/ppermute | solution.py:54
  23.3 4.7 %collective-permute-done.1.p2 = bf16[272,512]{1,0:T(8,128)(2,1)S(1)} collective-permute-done((bf16[272,512]{1,0:T(8,128)(2,1)S(1)}, bf16[272,512]{1,0:T(8,128)(2,1)S(1)}, u32[]{:S(2)}, u32[]{:S(2)}) %collective-permute-start.1) | collective-permute-done | bytes 278560 | tf_op jit(solution)/shard_map/ppermute | solution.py:54
  27.9 11.9 %collective-permute-done.2.p3 = bf16[272,512]{1,0:T(8,128)(2,1)S(1)} collective-permute-done((bf16[272,512]{1,0:T(8,128)(2,1)S(1)}, bf16[272,512]{1,0:T(8,128)(2,1)S(1)}, u32[]{:S(2)}, u32[]{:S(2)}) %collective-permute-start.2) | collective-permute-done | bytes 278560 | tf_op jit(solution)/shard_map/ppermute | solution.py:54
  51.5 3.5 %all-to-all-start.2 = ((bf16[4,1024,128]{2,1,0:T(8,128)(2,1)}), bf16[4,1024,128]{2,1,0:T(8,128)(2,1)S(1)}, u32[]{:S(2)}, u32[]{:S(2)}) async-start(bf16[4,1024,128]{2,1,0:T(8,128)(2,1)} %bitcast.4), calls=%async_computation.2 | async-start | bytes 2097152 | tf_op jit(solution)/shard_map/all_to_all | solution.py:582
  58.6 6.5 %shard_map.248.a0 = bf16[512,256]{1,0:T(8,128)(2,1)} custom-call(bf16[512,768]{1,0:T(8,128)(2,1)S(1)} %copy-done.24, bf16[512,512]{1,0:T(8,128)(2,1)S(1)} %collective-permute-done.7.far), custom_call_target="tpu_custom_call" | custom-call | flops 1073741824 | bytes 12582912 | tf_op jit(solution)/shard_map/pallas_call | solution.py:95
  65.0 3.2 %all-to-all-done.2 = bf16[4,1024,128]{2,1,0:T(8,128)(2,1)S(1)} async-done(((bf16[4,1024,128]{2,1,0:T(8,128)(2,1)}), bf16[4,1024,128]{2,1,0:T(8,128)(2,1)S(1)}, u32[]{:S(2)}, u32[]{:S(2)}) %all-to-all-start.2) | async-done | bytes 1048608 | tf_op jit(solution)/shard_map/all_to_all | solution.py:582
  72.2 3.4 %all-to-all-start.1 = ((bf16[4,128,256]{2,1,0:T(8,128)(2,1)}), bf16[4,128,256]{2,1,0:T(8,128)(2,1)S(1)}, u32[]{:S(2)}, u32[]{:S(2)}) async-start(bf16[4,128,256]{2,1,0:T(8,128)(2,1)} %bitcast.2), calls=%async_computation.1 | async-start | bytes 524288 | tf_op jit(solution)/shard_map/all_to_all | solution.py:589
  78.6 5.6 %collective-permute-done.8.c1 = bf16[128,1024]{1,0:T(8,128)(2,1)} collective-permute-done((bf16[128,1024]{1,0:T(8,128)(2,1)S(1)}, bf16[128,1024]{1,0:T(8,128)(2,1)}, u32[]{:S(2)}, u32[]{:S(2)}) %collective-permute-start.8) | collective-permute-done | bytes 262176 | tf_op jit(solution)/shard_map/ppermute | solution.py:54
  92.0 15.5 %all_to_all.89 = bf16[4,128,1024]{2,1,0:T(8,128)(2,1)S(1)} all-to-all(bf16[4,128,1024]{2,1,0:T(8,128)(2,1)S(1)} %bitcast.40), channel_id=1, replica_groups=mesh['rep'=4,'fsdp'=4,'seq'=2] {'rep'}, dimensions={0} | all-to-all | bytes 2097152 | tf_op jit(solution)/shard_map/all_to_all | solution.py:603
  112.3 5.9 %shard_map.250 = (bf16[512,1024]{1,0:T(8,128)(2,1)S(1)}, bf16[512,1024]{1,0:T(8,128)(2,1)S(1)}, bf16[512,1024]{1,0:T(8,128)(2,1)S(1)}, bf16[512,1024]{1,0:T(8,128)(2,1)S(1)}) custom-call(bf16[512,1024]{1,0:T(8,128)(2,1)S(1)} %bitcast.37, bf16[128,1024]{1,0:T(8,128)(2,1)S(1)} %copy-done.20, bf16[128,1024]{1,0:T(8,128)(2,1)} %collective-permute-done.8.c1, ...), custom_call_target="tpu_custom_call" | custom-call | flops 25769803776 | bytes 84410368 | tf_op jit(solution)/shard_map/pallas_call | solution.py:95
  120.6 5.3 %shard_map.251 = (bf16[512,1024]{1,0:T(8,128)(2,1)}, bf16[16,128,1024]{2,1,0:T(8,128)(2,1)S(1)}, f32[8,1024]{1,0:T(8,128)S(1)}) custom-call(bf16[512,1024]{1,0:T(8,128)(2,1)S(1)} %get-tuple-element.84.hidden, bf16[512,1024]{1,0:T(8,128)(2,1)S(1)} %get-tuple-element.85.pre_grad, bf16[512,1024]{1,0:T(8,128)(2,1)S(1)} %bitcast.38, ...), custom_call_target="tpu_custom_call" | custom-call | flops 25769803776 | bytes 109314048 | tf_op jit(solution)/shard_map/pallas_call | solution.py:95
  128.5 13.9 %all_to_all.90 = bf16[4,128,1024]{2,1,0:T(8,128)(2,1)S(1)} all-to-all(bf16[4,128,1024]{2,1,0:T(8,128)(2,1)S(1)} %bitcast.39), channel_id=1, replica_groups=mesh['rep'=4,'fsdp'=4,'seq'=2] {'rep'}, dimensions={0} | all-to-all | bytes 2097152 | tf_op jit(solution)/shard_map/all_to_all | solution.py:617
  144.8 8.4 %all_to_all.91 = bf16[4,128,512]{2,1,0:T(8,128)(2,1)S(1)} all-to-all(bf16[4,128,512]{2,1,0:T(8,128)(2,1)S(1)} %bitcast.44), channel_id=1, replica_groups=mesh['rep'=4,'fsdp'=4,'seq'=2] {'rep'}, dimensions={0} | all-to-all | bytes 1048576 | tf_op jit(solution)/shard_map/all_to_all | solution.py:637
  153.2 9.3 %shard_map.254 = (bf16[512,256]{1,0:T(8,128)(2,1)S(1)}, f32[512,512]{1,0:T(8,128)S(1)}, bf16[512,512]{1,0:T(8,128)(2,1)}) custom-call(bf16[512,768]{1,0:T(8,128)(2,1)S(1)} %copy-done.25, bf16[512,512]{1,0:T(8,128)(2,1)S(1)} %copy-done.14, bf16[512,512]{1,0:T(8,128)(2,1)S(1)} %bitcast.42), custom_call_target="tpu_custom_call" | custom-call | flops 2684354560 | bytes 29360128 | tf_op jit(solution)/shard_map/pallas_call | solution.py:95
  164.2 5.0 %collective-permute-start.15 = (bf16[512,512]{1,0:T(8,128)(2,1)}, bf16[512,512]{1,0:T(8,128)(2,1)}, u32[]{:S(2)}, u32[]{:S(2)}) collective-permute-start(bf16[512,512]{1,0:T(8,128)(2,1)} %get-tuple-element.97), channel_id=1, source_target_pairs={{0,1},{1,0},{2,3},{3,2},{4,5},{5,4},{6,7},{7,6},{8,9},{9,8},{10,11... | collective-permute-start | bytes 1572872 | tf_op jit(solution)/shard_map/ppermute | solution.py:54
  169.2 3.5 %all-to-all-start.6 = ((bf16[4,128,1024]{2,1,0:T(8,128)(2,1)}), bf16[4,128,1024]{2,1,0:T(8,128)(2,1)S(1)}, u32[]{:S(2)}, u32[]{:S(2)}) async-start(bf16[4,128,1024]{2,1,0:T(8,128)(2,1)} %bitcast.15), calls=%async_computation.6 | async-start | bytes 2097152 | tf_op jit(solution)/shard_map/all_to_all | solution.py:638
  175.8 5.1 %shard_map.256 = (bf16[4,256,512]{2,1,0:T(8,128)(2,1)S(1)}, bf16[4,256,512]{2,1,0:T(8,128)(2,1)}, bf16[512,1024]{1,0:T(8,128)(2,1)S(1)}, f32[4,16,512]{2,1,0:T(8,128)S(1)}) custom-call(bf16[512,256]{1,0:T(8,128)(2,1)S(1)} %copy-done.33, f32[512,512]{1,0:T(8,128)S(1)} %copy-done.29, bf16[512,512]{1,0:T(8,128)(2,1)} %collective-permute-done.15.far_grad, ...), custom_call_target="tpu_custom_call" | custom-call | flops 12884901888 | bytes 83361792 | tf_op jit(solution)/shard_map/pallas_call | solution.py:95
  186.5 3.7 %all-to-all-start.7 = ((bf16[4,128,1024]{2,1,0:T(8,128)(2,1)}), bf16[4,128,1024]{2,1,0:T(8,128)(2,1)S(1)}, u32[]{:S(2)}, u32[]{:S(2)}) async-start(bf16[4,128,1024]{2,1,0:T(8,128)(2,1)} %bitcast.34), calls=%async_computation.7 | async-start | bytes 2097152 | tf_op jit(solution)/shard_map/all_to_all | solution.py:675
  199.5 9.7 %all-to-all-done.7 = bf16[4,128,1024]{2,1,0:T(8,128)(2,1)S(1)} async-done(((bf16[4,128,1024]{2,1,0:T(8,128)(2,1)}), bf16[4,128,1024]{2,1,0:T(8,128)(2,1)S(1)}, u32[]{:S(2)}, u32[]{:S(2)}) %all-to-all-start.7) | async-done | bytes 1048608 | tf_op jit(solution)/shard_map/all_to_all | solution.py:675
  209.1 15.9 %collective-permute-done.18.p2 = bf16[2,128,1024]{2,1,0:T(8,128)(2,1)} collective-permute-done((bf16[2,128,1024]{2,1,0:T(8,128)(2,1)}, bf16[2,128,1024]{2,1,0:T(8,128)(2,1)}, u32[]{:S(2)}, u32[]{:S(2)}) %collective-permute-start.18) | collective-permute-done | bytes 524320 | tf_op jit(solution)/shard_map/ppermute | solution.py:54
  232.5 5.6 %collective-permute-start.27 = (bf16[272,512]{1,0:T(8,128)(2,1)S(1)}, bf16[272,512]{1,0:T(8,128)(2,1)S(1)}, u32[]{:S(2)}, u32[]{:S(2)}) collective-permute-start(bf16[272,512]{1,0:T(8,128)(2,1)S(1)} %collective-permute-done.23.p1), channel_id=1, source_target_pairs={{0,1},{1,0},{2,3},{3,2},{4,5},{5,4},{6,7},{7,6},{8,9},{9,8},{10,11... | collective-permute-start | bytes 835592 | tf_op jit(solution)/shard_map/ppermute | solution.py:54
  238.1 4.6 %collective-permute-start.28 = (bf16[272,512]{1,0:T(8,128)(2,1)S(1)}, bf16[272,512]{1,0:T(8,128)(2,1)S(1)}, u32[]{:S(2)}, u32[]{:S(2)}) collective-permute-start(bf16[272,512]{1,0:T(8,128)(2,1)S(1)} %collective-permute-done.24.p2), channel_id=1, source_target_pairs={{0,1},{1,0},{2,3},{3,2},{4,5},{5,4},{6,7},{7,6},{8,9},{9,8},{10,11... | collective-permute-start | bytes 835592 | tf_op jit(solution)/shard_map/ppermute | solution.py:54
  249.2 5.3 %shard_map.260 = (f32[1024,1024]{1,0:T(8,128)}, f32[1024,1024]{1,0:T(8,128)}) custom-call(bf16[2,128,1024]{2,1,0:T(8,128)(2,1)S(1)} %copy-done.8, bf16[2,128,1024]{2,1,0:T(8,128)(2,1)} %collective-permute-done.17.p1, bf16[2,128,1024]{2,1,0:T(8,128)(2,1)} %collective-permute-done.18.p2, bf16[2,128,1024]{2,1,0:T(8,128)(2,1)} %collective-permute-done.19.p3, ...), custom_call_target="tpu_custom_call" | custom-call | bytes 100663296 | tf_op jit(solution)/shard_map/pallas_call | solution.py:95
  (167 shorter events, 82.8 us)
Async XLA Ops:
  9.8 30.0 %all-to-all-start = ((bf16[4,128,1024]{2,1,0:T(8,128)(2,1)}), bf16[4,128,1024]{2,1,0:T(8,128)(2,1)S(1)}, u32[]{:S(2)}, u32[]{:S(2)}) async-start(bf16[4,128,1024]{2,1,0:T(8,128)(2,1)} %bitcast.48), calls=%async_computation | async-start | bytes 2097152 | tf_op jit(solution)/shard_map/all_to_all | solution.py:553
  13.5 96.6 %all-gather.3.cloned.1.call-start = ((), (), s32[]{:S(2)}) async-start(), calls=%async_computation.10 | async-start | bytes 4718592 | tf_op jit(solution)/shard_map/all_gather | solution.py:565
  13.6 14.3 %collective-permute-start.1 = (bf16[272,512]{1,0:T(8,128)(2,1)S(1)}, bf16[272,512]{1,0:T(8,128)(2,1)S(1)}, u32[]{:S(2)}, u32[]{:S(2)}) collective-permute-start(bf16[272,512]{1,0:T(8,128)(2,1)S(1)} %copy-done.15), channel_id=1, source_target_pairs={{0,4},{2,6},{4,0},{6,2},{1,5},{3,7},{5,1},{7,3},{8,12},{10,14},{12... | collective-permute-start | bytes 835592 | tf_op jit(solution)/shard_map/ppermute | solution.py:54
  16.1 23.7 %collective-permute-start.2 = (bf16[272,512]{1,0:T(8,128)(2,1)S(1)}, bf16[272,512]{1,0:T(8,128)(2,1)S(1)}, u32[]{:S(2)}, u32[]{:S(2)}) collective-permute-start(bf16[272,512]{1,0:T(8,128)(2,1)S(1)} %copy-done.15), channel_id=1, source_target_pairs={{0,6},{2,4},{4,2},{6,0},{1,7},{3,5},{5,3},{7,1},{8,14},{10,12},{12... | collective-permute-start | bytes 835592 | tf_op jit(solution)/shard_map/ppermute | solution.py:54
  51.5 16.7 %all-to-all-start.2 = ((bf16[4,1024,128]{2,1,0:T(8,128)(2,1)}), bf16[4,1024,128]{2,1,0:T(8,128)(2,1)S(1)}, u32[]{:S(2)}, u32[]{:S(2)}) async-start(bf16[4,1024,128]{2,1,0:T(8,128)(2,1)} %bitcast.4), calls=%async_computation.2 | async-start | bytes 2097152 | tf_op jit(solution)/shard_map/all_to_all | solution.py:582
  68.2 18.9 %collective-permute-start.11 = (bf16[4096,128]{1,0:T(8,128)(2,1)S(1)}, bf16[4096,128]{1,0:T(8,128)(2,1)}, u32[]{:S(2)}, u32[]{:S(2)}) collective-permute-start(bf16[4096,128]{1,0:T(8,128)(2,1)S(1)} %bitcast.35), channel_id=1, source_target_pairs={{0,1},{1,0},{2,3},{3,2},{4,5},{5,4},{6,7},{7,6},{8,9},{9,8},{10,11... | collective-permute-start | bytes 3145736 | tf_op jit(solution)/shard_map/ppermute | solution.py:54
  70.7 13.5 %collective-permute-start.8 = (bf16[128,1024]{1,0:T(8,128)(2,1)S(1)}, bf16[128,1024]{1,0:T(8,128)(2,1)}, u32[]{:S(2)}, u32[]{:S(2)}) collective-permute-start(bf16[128,1024]{1,0:T(8,128)(2,1)S(1)} %copy-done.20), channel_id=1, source_target_pairs={{0,8},{8,0},{16,24},{24,16},{1,9},{9,1},{17,25},{25,17},{2,10},{10... | collective-permute-start | bytes 786440 | tf_op jit(solution)/shard_map/ppermute | solution.py:54
  72.0 12.7 %collective-permute-start.9 = (bf16[128,1024]{1,0:T(8,128)(2,1)S(1)}, bf16[128,1024]{1,0:T(8,128)(2,1)}, u32[]{:S(2)}, u32[]{:S(2)}) collective-permute-start(bf16[128,1024]{1,0:T(8,128)(2,1)S(1)} %copy-done.20), channel_id=1, source_target_pairs={{0,16},{8,24},{16,0},{24,8},{1,17},{9,25},{17,1},{25,9},{2,18},{10... | collective-permute-start | bytes 786440 | tf_op jit(solution)/shard_map/ppermute | solution.py:54
  72.2 14.9 %all-to-all-start.1 = ((bf16[4,128,256]{2,1,0:T(8,128)(2,1)}), bf16[4,128,256]{2,1,0:T(8,128)(2,1)S(1)}, u32[]{:S(2)}, u32[]{:S(2)}) async-start(bf16[4,128,256]{2,1,0:T(8,128)(2,1)} %bitcast.2), calls=%async_computation.1 | async-start | bytes 524288 | tf_op jit(solution)/shard_map/all_to_all | solution.py:589
  75.7 107.3 %reduce-scatter.2.cloned.1.call-start = ((), (), s32[]{:S(2)}) async-start(), calls=%async_computation.9 | async-start | bytes 4718592 | tf_op jit(solution)/shard_map/reduce_scatter | solution.py:628
  107.5 10.7 %collective-permute-start.12 = (bf16[512,256]{1,0:T(8,128)(2,1)}, bf16[512,256]{1,0:T(8,128)(2,1)}, u32[]{:S(2)}, u32[]{:S(2)}) collective-permute-start(bf16[512,256]{1,0:T(8,128)(2,1)} %shard_map.248.a0), channel_id=1, source_target_pairs={{0,8},{8,0},{16,24},{24,16},{1,9},{9,1},{17,25},{25,17},{2,10},{10... | collective-permute-start | bytes 786440 | tf_op jit(solution)/shard_map/ppermute | solution.py:54
  109.0 11.6 %collective-permute-start.14 = (bf16[512,256]{1,0:T(8,128)(2,1)}, bf16[512,256]{1,0:T(8,128)(2,1)}, u32[]{:S(2)}, u32[]{:S(2)}) collective-permute-start(bf16[512,256]{1,0:T(8,128)(2,1)} %shard_map.248.a0), channel_id=1, source_target_pairs={{0,24},{8,16},{16,8},{24,0},{1,25},{9,17},{17,9},{25,1},{2,26},{10... | collective-permute-start | bytes 786440 | tf_op jit(solution)/shard_map/ppermute | solution.py:54
  169.2 17.3 %all-to-all-start.6 = ((bf16[4,128,1024]{2,1,0:T(8,128)(2,1)}), bf16[4,128,1024]{2,1,0:T(8,128)(2,1)S(1)}, u32[]{:S(2)}, u32[]{:S(2)}) async-start(bf16[4,128,1024]{2,1,0:T(8,128)(2,1)} %bitcast.15), calls=%async_computation.6 | async-start | bytes 2097152 | tf_op jit(solution)/shard_map/all_to_all | solution.py:638
  182.9 11.7 %collective-permute-start.16 = (bf16[4,256,512]{2,1,0:T(8,128)(2,1)}, bf16[4,256,512]{2,1,0:T(8,128)(2,1)}, u32[]{:S(2)}, u32[]{:S(2)}) collective-permute-start(bf16[4,256,512]{2,1,0:T(8,128)(2,1)} %get-tuple-element.108), channel_id=1, source_target_pairs={{0,1},{1,0},{2,3},{3,2},{4,5},{5,4},{6,7},{7,6},{8,9},{9,8},{10,11... | collective-permute-start | bytes 3145736 | tf_op jit(solution)/shard_map/ppermute | solution.py:54
  182.9 16.3 %collective-permute-start.17 = (bf16[2,128,1024]{2,1,0:T(8,128)(2,1)}, bf16[2,128,1024]{2,1,0:T(8,128)(2,1)}, u32[]{:S(2)}, u32[]{:S(2)}) collective-permute-start(bf16[2,128,1024]{2,1,0:T(8,128)(2,1)} %reduce-scatter.2.cloned.1.call-done.p0), channel_id=1, source_target_pairs={{0,8},{8,0},{16,24},{24,16},{1,9},{9,1},{17,25},{25,17},{2,10},{10... | collective-permute-start | bytes 1572872 | tf_op jit(solution)/shard_map/ppermute | solution.py:54
  186.5 22.6 %all-to-all-start.7 = ((bf16[4,128,1024]{2,1,0:T(8,128)(2,1)}), bf16[4,128,1024]{2,1,0:T(8,128)(2,1)S(1)}, u32[]{:S(2)}, u32[]{:S(2)}) async-start(bf16[4,128,1024]{2,1,0:T(8,128)(2,1)} %bitcast.34), calls=%async_computation.7 | async-start | bytes 2097152 | tf_op jit(solution)/shard_map/all_to_all | solution.py:675
  190.3 34.8 %collective-permute-start.18 = (bf16[2,128,1024]{2,1,0:T(8,128)(2,1)}, bf16[2,128,1024]{2,1,0:T(8,128)(2,1)}, u32[]{:S(2)}, u32[]{:S(2)}) collective-permute-start(bf16[2,128,1024]{2,1,0:T(8,128)(2,1)} %reduce-scatter.2.cloned.1.call-done.p0), channel_id=1, source_target_pairs={{0,16},{8,24},{16,0},{24,8},{1,17},{9,25},{17,1},{25,9},{2,18},{10... | collective-permute-start | bytes 1572872 | tf_op jit(solution)/shard_map/ppermute | solution.py:54
  191.5 33.5 %collective-permute-start.19 = (bf16[2,128,1024]{2,1,0:T(8,128)(2,1)}, bf16[2,128,1024]{2,1,0:T(8,128)(2,1)}, u32[]{:S(2)}, u32[]{:S(2)}) collective-permute-start(bf16[2,128,1024]{2,1,0:T(8,128)(2,1)} %reduce-scatter.2.cloned.1.call-done.p0), channel_id=1, source_target_pairs={{0,24},{8,16},{16,8},{24,0},{1,25},{9,17},{17,9},{25,1},{2,26},{10... | collective-permute-start | bytes 1572872 | tf_op jit(solution)/shard_map/ppermute | solution.py:54
  196.8 28.3 %collective-permute-start.20 = (bf16[272,512]{1,0:T(8,128)(2,1)}, bf16[272,512]{1,0:T(8,128)(2,1)S(1)}, u32[]{:S(2)}, u32[]{:S(2)}) collective-permute-start(bf16[272,512]{1,0:T(8,128)(2,1)} %get-tuple-element.114), channel_id=1, source_target_pairs={{0,2},{2,0},{4,6},{6,4},{1,3},{3,1},{5,7},{7,5},{8,10},{10,8},{12,... | collective-permute-start | bytes 835592 | tf_op jit(solution)/shard_map/ppermute | solution.py:54
  196.8 28.3 %collective-permute-start.21 = (bf16[272,512]{1,0:T(8,128)(2,1)}, bf16[272,512]{1,0:T(8,128)(2,1)}, u32[]{:S(2)}, u32[]{:S(2)}) collective-permute-start(bf16[272,512]{1,0:T(8,128)(2,1)} %get-tuple-element.115), channel_id=1, source_target_pairs={{0,4},{2,6},{4,0},{6,2},{1,5},{3,7},{5,1},{7,3},{8,12},{10,14},{12... | collective-permute-start | bytes 835592 | tf_op jit(solution)/shard_map/ppermute | solution.py:54
  199.2 25.8 %collective-permute-start.22 = (bf16[272,512]{1,0:T(8,128)(2,1)}, bf16[272,512]{1,0:T(8,128)(2,1)}, u32[]{:S(2)}, u32[]{:S(2)}) collective-permute-start(bf16[272,512]{1,0:T(8,128)(2,1)} %get-tuple-element.116), channel_id=1, source_target_pairs={{0,6},{2,4},{4,2},{6,0},{1,7},{3,5},{5,3},{7,1},{8,14},{10,12},{12... | collective-permute-start | bytes 835592 | tf_op jit(solution)/shard_map/ppermute | solution.py:54
  227.9 14.8 %collective-permute-start.25 = (bf16[272,512]{1,0:T(8,128)(2,1)S(1)}, bf16[272,512]{1,0:T(8,128)(2,1)S(1)}, u32[]{:S(2)}, u32[]{:S(2)}) collective-permute-start(bf16[272,512]{1,0:T(8,128)(2,1)S(1)} %add_convert_fusion.p0), channel_id=1, source_target_pairs={{0,24},{8,16},{16,8},{24,0},{1,25},{9,17},{17,9},{25,1},{2,26},{10... | collective-permute-start | bytes 835592 | tf_op jit(solution)/shard_map/ppermute | solution.py:54
  229.0 15.3 %collective-permute-start.26 = (bf16[272,512]{1,0:T(8,128)(2,1)S(1)}, bf16[272,512]{1,0:T(8,128)(2,1)S(1)}, u32[]{:S(2)}, u32[]{:S(2)}) collective-permute-start(bf16[272,512]{1,0:T(8,128)(2,1)S(1)} %add_convert_fusion.p0), channel_id=1, source_target_pairs={{0,1},{1,0},{2,3},{3,2},{4,5},{5,4},{6,7},{7,6},{8,9},{9,8},{10,11... | collective-permute-start | bytes 835592 | tf_op jit(solution)/shard_map/ppermute | solution.py:54
  232.5 11.9 %collective-permute-start.27 = (bf16[272,512]{1,0:T(8,128)(2,1)S(1)}, bf16[272,512]{1,0:T(8,128)(2,1)S(1)}, u32[]{:S(2)}, u32[]{:S(2)}) collective-permute-start(bf16[272,512]{1,0:T(8,128)(2,1)S(1)} %collective-permute-done.23.p1), channel_id=1, source_target_pairs={{0,1},{1,0},{2,3},{3,2},{4,5},{5,4},{6,7},{7,6},{8,9},{9,8},{10,11... | collective-permute-start | bytes 835592 | tf_op jit(solution)/shard_map/ppermute | solution.py:54
  (57 other events, 368.5 us)
Sparse Core Ops, SparseCore 0:
  39.9 47.5 all-gather.2
  128.7 49.8 reduce-scatter.1

commit v2 on v1

--- a/solution.py
+++ b/solution.py
@@ -69,11 +69,11 @@
     return pl.ds(pl.multiple_of(start, LANE), size)
 
 
-def vmem_call(kernel, outs, args, hbm=(), staged=(), scratch=(), flops=0, limit=16):
+def vmem_call(kernel, outs, args, hbm=(), staged=(), scratch=(), flops=0, limit=16, away=(), weight=8):
     moved = sum(a.size * a.dtype.itemsize for a in args)
     moved += sum(math.prod(s) * jnp.dtype(t).itemsize for s, t in outs)
     whole = pl.BlockSpec(memory_space=pltpu.VMEM)
-    far = pl.BlockSpec(memory_space=pl.ANY)
+    far = pl.BlockSpec(memory_space=pltpu.HBM)
     n, m, k = len(args), len(outs), len(staged)
 
     def body(*refs):
@@ -96,11 +96,11 @@
         body if staged else kernel,
         out_shape=[jax.ShapeDtypeStruct(s, t) for s, t in outs],
         in_specs=[far if i in hbm or i in staged else whole for i in range(n)],
-        out_specs=[whole] * m,
+        out_specs=[far if i in away else whole for i in range(m)],
         scratch_shapes=copied + list(scratch),
         compiler_params=pltpu.CompilerParams(vmem_limit_bytes=limit * 1024 * 1024),
         cost_estimate=pl.CostEstimate(
-            flops=flops * 8, bytes_accessed=moved * 8, transcendentals=0
+            flops=flops * weight, bytes_accessed=moved * weight, transcendentals=0
         ),
     )(*args)
 
@@ -173,9 +173,7 @@
         at = pl.ds(pl.multiple_of((shard ^ k) * SHARD, SHARD), SHARD)
         weight[at, 0:TRIPLE] = own[0:SHARD, 0:TRIPLE]
         weight[at, TRIPLE : 2 * TRIPLE] = far[0:SHARD, 0:TRIPLE]
-        for a in range(REPS):
-            start = a * WIDTH + (shard ^ k) * SHARD
-            proj[pl.ds(pl.multiple_of(start, SHARD), SHARD), :] = own[0:SHARD, TRIPLE:]
+        proj[at, :] = own[0:SHARD, TRIPLE:]
         vectors[:, at] = own[SHARD:, 0:SHARD].astype(f32)
     for p in range(CORES):
         for t, at in ((0, 0), (2, 2)):
@@ -244,13 +242,13 @@
             attended[at, p * LANE : (p + 1) * LANE] = jnp.where(first, *heads).astype(bf16)
 
 
-def branch_kernel(a, own, far, x, vectors, middle, unit, scale, normed, proj, joined):
-    core = lax.axis_index("seq")
-    for k in range(REPS):
-        for p, piece in enumerate((own, far)):
-            proj[:, lanes((k * CORES + (core ^ p)) * LANE, LANE)] = piece[
-                k * WIDTH : (k + 1) * WIDTH, :
-            ]
+def branch_kernel(
+    a, p0, p1, p2, p3, f0, f1, f2, f3, x, vectors, middle, unit, scale, normed, proj, joined
+):
+    rep, _, core = mesh_place()
+    for k, pair in enumerate(((p0, f0), (p1, f1), (p2, f2), (p3, f3))):
+        for p, piece in enumerate(pair):
+            proj[:, lanes(((rep ^ k) * CORES + (core ^ p)) * LANE, LANE)] = piece[...]
     for k in range(REPS):
         for p in range(CORES):
             at = lanes((k * CORES + (core ^ p)) * LANE, LANE)
@@ -266,11 +264,7 @@
         normed[k * ROWS : (k + 1) * ROWS, :] = low
 
 
-def hidden_kernel(h, c0, c1, c2, c3, ff, vectors, back, hidden, pre_grad, c):
-    rep = lax.axis_index("rep")
-    for k, cot in enumerate((c0, c1, c2, c3)):
-        c[pl.ds(pl.multiple_of((rep ^ k) * ROWS, ROWS), ROWS), :] = cot[...]
-
+def hidden_kernel(h, c, ff, vectors, back, hidden, pre_grad):
     @pl.loop(0, 2)
     def _(block):
         at = pl.ds(pl.multiple_of(block * 2 * ROWS, 2 * ROWS), 2 * ROWS)
@@ -287,22 +281,29 @@
         back[at, :] = jnp.dot(pre_grad[at, :], fc, preferred_element_type=f32).astype(bf16)
 
 
-def weights_kernel(hidden, pre_grad, h, c, ff, output, grads, sums):
+def weights_kernel(hidden, pre_grad, h, c, ff, output, grads, sums, held, sems):
+    copies = []
     for n in range(SHARDS):
         tile = pl.ds(n * 2 * LANE, 2 * LANE)
         for i, (left, right) in enumerate(((pre_grad, h), (hidden, c))):
             grad = contract(left[:, tile], right[...], 0, 0).astype(bf16)
             for j in range(CORES):
-                grads[(n * CORES + j) * 2 + i] = grad[j * LANE : (j + 1) * LANE]
+                held[(n * CORES + j) * 2 + i] = grad[j * LANE : (j + 1) * LANE]
+        part = pl.ds(n * CORES * 2, CORES * 2)
+        copies.append(pltpu.make_async_copy(held.at[part], grads.at[part], sems.at[n]))
+        copies[-1].start()
     sums[...] = jnp.broadcast_to(
         jnp.sum(pre_grad[...].astype(f32), 0, keepdims=True), sums.shape
     )
 
-    @pl.loop(0, REPS)
+    @pl.loop(0, 2)
     def _(block):
-        at = pl.ds(pl.multiple_of(block * ROWS, ROWS), ROWS)
+        at = pl.ds(pl.multiple_of(block * 2 * ROWS, 2 * ROWS), 2 * ROWS)
         out = ff[:, 1].reshape(HIDDEN, WIDTH)
         output[at, :] = jnp.dot(hidden[at, :], out, preferred_element_type=f32).astype(bf16)
+
+    for copy in copies:
+        copy.wait()
 
 
 def middle_kernel(
@@ -557,7 +558,7 @@
         [((all_rows, WIDTH), f32), ((all_rows, LANE), f32), ((2, ROWS, WIDTH), f32)],
         [inputs],
     )
-    cots = over_rep([after(cotangent, unit_one)] * REPS)
+    cots = lax.all_gather(cotangent, "rep", axis=0, tiled=True)
 
     mine = rep * CORES + core
     ff = [pick(w.reshape(REPS * CORES, LANE, WIDTH), mine, 0) for w in (fc_weight, out_weight)]
@@ -572,14 +573,14 @@
             ((all_rows, WIDTH), bf16),
             ((WIDTH, 2 * TRIPLE), bf16),
             ((16, WIDTH), f32),
-            ((REPS * WIDTH, LANE), bf16),
+            ((WIDTH, LANE), bf16),
         ],
         [unit_one] + own_packed + far_packed,
         scratch=[pltpu.VMEM((8, 2 * TRIPLE), f32)],
         flops=2 * all_rows * WIDTH * 2 * TRIPLE,
     )
     kv_far = over_cores(kv_send)
-    proj_cols = lax.all_to_all(proj_cols, "rep", 0, 0, tiled=True)
+    proj_cols = over_rep([proj_cols] * REPS)
     (attended,) = vmem_call(
         attend_kernel,
         [((all_rows, SHARD), bf16)],
@@ -587,6 +588,7 @@
         flops=4 * all_rows * 2 * ROWS * SHARD,
     )
     mine = lax.all_to_all(attended, "rep", 0, 0, tiled=True)
+    marker = over_cores(attended[:16, :LANE])
     middle, unit_two, scale_two, normed_two, proj_full = vmem_call(
         branch_kernel,
         [
@@ -596,22 +598,24 @@
             ((all_rows, WIDTH), bf16),
             ((WIDTH, WIDTH), bf16),
         ],
-        [after(mine, *cots[1:]), proj_cols, over_cores(after(proj_cols, attended)), block_input, vectors],
+        [mine]
+        + proj_cols
+        + [over_cores(after(p, marker)) for p in proj_cols]
+        + [block_input, vectors],
         scratch=[pltpu.VMEM((ROWS, WIDTH), bf16)],
         flops=2 * ROWS * WIDTH * WIDTH,
     )
     normed_two = lax.all_to_all(normed_two, "rep", 0, 0, tiled=True)
     attended_all = over_rep([after(attended, normed_two)] * REPS)
 
-    back, hidden, pre_grad, c_all = vmem_call(
+    back, hidden, pre_grad = vmem_call(
         hidden_kernel,
         [
+            ((all_rows, WIDTH), bf16),
             ((all_rows, HIDDEN), bf16),
             ((all_rows, HIDDEN), bf16),
-            ((all_rows, WIDTH), bf16),
-            ((all_rows, WIDTH), bf16),
         ],
-        [normed_two] + cots + [ff, vectors],
+        [normed_two, cots, ff, vectors],
         flops=6 * all_rows * WIDTH * HIDDEN,
     )
     back = lax.all_to_all(back, "rep", 0, 0, tiled=True)
@@ -622,7 +626,12 @@
             ((SHARDS * CORES * 2, LANE, WIDTH), bf16),
             ((8, HIDDEN), f32),
         ],
-        [after(hidden, *attended_all[1:]), pre_grad, normed_two, c_all, ff],
+        [after(hidden, *attended_all[1:]), pre_grad, normed_two, cots, ff],
+        scratch=[
+            pltpu.VMEM((SHARDS * CORES * 2, LANE, WIDTH), bf16),
+            pltpu.SemaphoreType.DMA((SHARDS,)),
+        ],
+        away=(1,),
         flops=6 * all_rows * WIDTH * HIDDEN,
     )
     ff_piece = lax.psum_scatter(ff_grads, ("fsdp", "seq"), scatter_dimension=0, tiled=True)
@@ -645,6 +654,7 @@
             ((all_rows, 4 * LANE), bf16),
         ],
         [qkv, kv_far, pairs],
+        weight=1,
         flops=10 * all_rows * 2 * ROWS * SHARD,
     )
     proj_own, proj_far = vmem_call(
@@ -669,25 +679,25 @@
     tail = vmem_call(
         tail_kernel,
         [((SHARD + 16, TRIPLE + LANE), bf16)] * SHARDS,
-        [qkv_own, over_cores(qkv_far), after(small, block_output)],
+        [qkv_own, over_cores(qkv_far), small],
     )
     tail = over_shards(tail)
     joined = lax.all_to_all(joined, "rep", 0, 0, tiled=True)
     ff_pieces = over_rep([ff_piece] * REPS)
-    tail = joined_sum([after(tail[0], joined, *ff_pieces[1:])] + tail[1:])
+    tail = joined_sum([after(tail[0], joined, block_output, *ff_pieces[1:])] + tail[1:])
     (input_grad,) = vmem_call(
         input_kernel, [((ROWS, WIDTH), f32)], [joined, unit_own, vectors, middle_grad]
     )
-    tail = over_rep([tail] * REPS)
+    whole_tail, tail = tail, over_rep([tail] * REPS)
     fc_grads, out_grads = vmem_call(
         spread_kernel,
         [((2 * REPS * LANE, WIDTH), f32)] * 2,
-        ff_pieces + [over_cores(after(p, tail[1])) for p in ff_pieces],
+        ff_pieces + [over_cores(after(p, whole_tail)) for p in ff_pieces],
     )
     qkv_grads, proj_grads, small = vmem_call(
         final_kernel,
         [((SHARD, 3 * WIDTH), f32), ((SHARD, WIDTH), f32), ((16, SHARD), f32)],
-        tail + [over_cores(t) for t in tail],
+        [after(tail[0], fc_grads)] + tail[1:] + [over_cores(t) for t in tail],
     )
     return (
         block_output,

time: 262 us -> 249 us (0.950); the launches traced: 261 us -> 245 us
  waiting for transfers between devices: 68.6 us -> 58.4 us
  starting transfers between devices: 59.3 us -> 50.4 us
  blocking collectives: 37.8 us -> 43.7 us
  Pallas kernels: 55.9 us -> 51.6 us
    all_to_all x0 -> x1, blocking collectives: none -> 7.74 us  [tiled_body(): mine = lax.all_to_all(attended, 'rep', 0, 0, tiled=True)]
    all_to_all x2 -> x0, starting transfers between devices: 6.92 us -> none  [the longest x1 3.52 us: tiled_body(): proj_cols = lax.all_to_all(proj_cols, 'rep', 0, 0, tiled=True)]
    all_to_all x2 -> x0, waiting for transfers between devices: 5.65 us -> none  [the longest x1 3.18 us: tiled_body(): proj_cols = lax.all_to_all(proj_cols, 'rep', 0, 0, tiled=True)]
    pallas_call x16, Pallas kernels: 55.9 us -> 51.6 us  [vmem_call(): pl.pallas_call(body if staged else kernel, out_shape=[jax.ShapeDtypeStruc...]
    ppermute x34 -> x38, waiting for transfers between devices: 51.4 us -> 49.1 us  [swap(): return lax.ppermute(value, axis, [(i, i ^ offset) for i in range(size)])]
    ppermute x34 -> x38, starting transfers between devices: 41.3 us -> 39.3 us  [swap(): return lax.ppermute(value, axis, [(i, i ^ offset) for i in range(size)])]
  transfers between devices with their start and end apart: 41 -> 44, of which waited for: 15 -> 12; matrix products, arithmetic and copies ran while one was open for 1% -> 1% of each run, Pallas kernels for 16% -> 18%
where the time goes in v2:
time: 249 us; the launch traced here: 245 us
  waiting for transfers between devices  58.4 us (23%)
  Pallas kernels  51.6 us (21%)
  starting transfers between devices  50.4 us (20%)
  blocking collectives  43.7 us (18%)
  local copies, waits for them, and re-layouts  24.4 us (10%)
  between operations  14.2 us (6%)
    pallas_call x16, Pallas kernels, vmem_call(): pl.pallas_call(body if staged else kernel, out_shape=[jax.ShapeDtypeStruc...  51.6 us
    ppermute x38, waiting for transfers between devices, swap(): return lax.ppermute(value, axis, [(i, i ^ offset) for i in range(size)])  49.1 us
    ppermute x38, starting transfers between devices, swap(): return lax.ppermute(value, axis, [(i, i ^ offset) for i in range(size)])  39.3 us
    unnamed x84, local copies, waits for them, and re-layouts  22.7 us
    all_to_all x1, blocking collectives, tiled_body(): normed_two = lax.all_to_all(normed_two, 'rep', 0, 0, tiled=True)  14.9 us
    all_to_all x1, blocking collectives, tiled_body(): back = lax.all_to_all(back, 'rep', 0, 0, tiled=True)  12.7 us
    all_to_all x1, blocking collectives, tiled_body(): pairs = lax.all_to_all(pairs, 'rep', 0, 0, tiled=True)  8.37 us
    all_to_all x1, waiting for transfers between devices, tiled_body(): joined = lax.all_to_all(joined, 'rep', 0, 0, tiled=True)  8.08 us
  transfers between devices with their start and end apart: 44, of which 12 were waited for; matrix products, arithmetic and copies ran while one was open for 1% of the time, Pallas kernels for 18%

profile of v2, /device:TPU:9, one launch (start us, length us, event | category | flops | bytes accessed | tf_op | source)
XLA Modules:
  0.0 244.8 jit_solution(1870876717610529706)
XLA Ops:
  7.9 2.6 %shard_map.245 = (bf16[272,512]{1,0:T(8,128)(2,1)}, bf16[512,1024]{1,0:T(8,128)(2,1)}) custom-call(bf16[256,3072]{1,0:T(8,128)(2,1)} %refs_0_.1, bf16[256,1024]{1,0:T(8,128)(2,1)} %refs_1_.1, bf16[128,1024]{1,0:T(8,128)(2,1)} %x.1, bf16[256]{0:T(256)(128)(2,1)} %refs_3_.1, bf16[256]{0:T(256)(128)(2,1)} %refs_4_.1, bf16[512]{0:T(512)(128)(2,1)} %refs_5_.1, ...), custom_call_target="tpu_custom_call" | custom-call | bytes 29540352 | tf_op jit(solution)/shard_map/pallas_call | solution.py:95
  10.5 3.7 %all-to-all-start = ((bf16[4,128,1024]{2,1,0:T(8,128)(2,1)}), bf16[4,128,1024]{2,1,0:T(8,128)(2,1)S(1)}, u32[]{:S(2)}, u32[]{:S(2)}) async-start(bf16[4,128,1024]{2,1,0:T(8,128)(2,1)} %bitcast.46), calls=%async_computation | async-start | bytes 2097152 | tf_op jit(solution)/shard_map/all_to_all | solution.py:554
  18.9 5.1 %collective-permute-done.p1 = bf16[272,512]{1,0:T(8,128)(2,1)S(1)} collective-permute-done((bf16[272,512]{1,0:T(8,128)(2,1)S(1)}, bf16[272,512]{1,0:T(8,128)(2,1)S(1)}, u32[]{:S(2)}, u32[]{:S(2)}) %collective-permute-start) | collective-permute-done | bytes 278560 | tf_op jit(solution)/shard_map/ppermute | solution.py:54
  24.0 4.7 %collective-permute-done.1.p2 = bf16[272,512]{1,0:T(8,128)(2,1)S(1)} collective-permute-done((bf16[272,512]{1,0:T(8,128)(2,1)S(1)}, bf16[272,512]{1,0:T(8,128)(2,1)S(1)}, u32[]{:S(2)}, u32[]{:S(2)}) %collective-permute-start.1) | collective-permute-done | bytes 278560 | tf_op jit(solution)/shard_map/ppermute | solution.py:54
  28.7 12.0 %collective-permute-done.2.p3 = bf16[272,512]{1,0:T(8,128)(2,1)S(1)} collective-permute-done((bf16[272,512]{1,0:T(8,128)(2,1)S(1)}, bf16[272,512]{1,0:T(8,128)(2,1)S(1)}, u32[]{:S(2)}, u32[]{:S(2)}) %collective-permute-start.2) | collective-permute-done | bytes 278560 | tf_op jit(solution)/shard_map/ppermute | solution.py:54
  51.7 5.8 %shard_map.248.a0 = bf16[512,256]{1,0:T(8,128)(2,1)S(1)} custom-call(bf16[512,768]{1,0:T(8,128)(2,1)S(1)} %get-tuple-element.73.qkv, bf16[512,512]{1,0:T(8,128)(2,1)S(1)} %collective-permute-done.7.far), custom_call_target="tpu_custom_call" | custom-call | flops 1073741824 | bytes 12582912 | tf_op jit(solution)/shard_map/pallas_call | solution.py:95
  59.7 4.2 %collective-permute-done.9.p2 = bf16[1024,128]{1,0:T(8,128)(2,1)S(1)} collective-permute-done((bf16[1024,128]{1,0:T(8,128)(2,1)S(1)}, bf16[1024,128]{1,0:T(8,128)(2,1)S(1)}, u32[]{:S(2)}, u32[]{:S(2)}) %collective-permute-start.9) | collective-permute-done | bytes 262176 | tf_op jit(solution)/shard_map/ppermute | solution.py:54
  64.8 7.7 %all_to_all.77 = bf16[4,128,256]{2,1,0:T(8,128)(2,1)S(1)} all-to-all(bf16[4,128,256]{2,1,0:T(8,128)(2,1)S(1)} %bitcast.42), channel_id=1, replica_groups=mesh['rep'=4,'fsdp'=4,'seq'=2] {'rep'}, dimensions={0} | all-to-all | bytes 524288 | tf_op jit(solution)/shard_map/all_to_all | solution.py:590
  75.4 14.9 %all_to_all.78 = bf16[4,128,1024]{2,1,0:T(8,128)(2,1)S(1)} all-to-all(bf16[4,128,1024]{2,1,0:T(8,128)(2,1)S(1)} %bitcast.39), channel_id=1, replica_groups=mesh['rep'=4,'fsdp'=4,'seq'=2] {'rep'}, dimensions={0} | all-to-all | bytes 2097152 | tf_op jit(solution)/shard_map/all_to_all | solution.py:608
  96.3 4.7 %shard_map.250 = (bf16[512,1024]{1,0:T(8,128)(2,1)S(1)}, bf16[512,1024]{1,0:T(8,128)(2,1)S(1)}, bf16[512,1024]{1,0:T(8,128)(2,1)S(1)}) custom-call(bf16[512,1024]{1,0:T(8,128)(2,1)S(1)} %bitcast.36, bf16[512,1024]{1,0:T(8,128)(2,1)S(1)} %copy-done.21, bf16[8,2,128,1024]{3,2,1,0:T(8,128)(2,1)S(1)} %bitcast.44, f32[16,1024]{1,0:T(8,128)S(1)} %get-tuple-element.80.vectors), custom_call_target="tpu_custom_call" | custom-call | flops 25769803776 | bytes 76021760 | tf_op jit(solution)/shard_map/pallas_call | solution.py:95
  102.2 4.9 %shard_map.251 = (bf16[512,1024]{1,0:T(8,128)(2,1)S(1)}, bf16[16,128,1024]{2,1,0:T(8,128)(2,1)S(1)}, f32[8,1024]{1,0:T(8,128)S(1)}) custom-call(bf16[512,1024]{1,0:T(8,128)(2,1)S(1)} %get-tuple-element.85.hidden, bf16[512,1024]{1,0:T(8,128)(2,1)S(1)} %get-tuple-element.86.pre_grad, bf16[512,1024]{1,0:T(8,128)(2,1)S(1)} %bitcast.37, ...), custom_call_target="tpu_custom_call" | custom-call | flops 25769803776 | bytes 109314048 | tf_op jit(solution)/shard_map/pallas_call | solution.py:95
  110.8 12.7 %all_to_all.79 = bf16[4,128,1024]{2,1,0:T(8,128)(2,1)S(1)} all-to-all(bf16[4,128,1024]{2,1,0:T(8,128)(2,1)S(1)} %bitcast.38), channel_id=1, replica_groups=mesh['rep'=4,'fsdp'=4,'seq'=2] {'rep'}, dimensions={0} | all-to-all | bytes 2097152 | tf_op jit(solution)/shard_map/all_to_all | solution.py:621
  126.9 8.4 %all_to_all.80 = bf16[4,128,512]{2,1,0:T(8,128)(2,1)S(1)} all-to-all(bf16[4,128,512]{2,1,0:T(8,128)(2,1)S(1)} %bitcast.41), channel_id=1, replica_groups=mesh['rep'=4,'fsdp'=4,'seq'=2] {'rep'}, dimensions={0} | all-to-all | bytes 1048576 | tf_op jit(solution)/shard_map/all_to_all | solution.py:646
  135.3 9.3 %shard_map.254 = (bf16[512,256]{1,0:T(8,128)(2,1)S(1)}, f32[512,512]{1,0:T(8,128)S(1)}, bf16[512,512]{1,0:T(8,128)(2,1)}) custom-call(bf16[512,768]{1,0:T(8,128)(2,1)S(1)} %copy-done.6, bf16[512,512]{1,0:T(8,128)(2,1)S(1)} %copy-done.10, bf16[512,512]{1,0:T(8,128)(2,1)S(1)} %bitcast.32), custom_call_target="tpu_custom_call" | custom-call | flops 335544320 | bytes 3670016 | tf_op jit(solution)/shard_map/pallas_call | solution.py:95
  145.5 6.1 %collective-permute-start.19 = (bf16[512,512]{1,0:T(8,128)(2,1)}, bf16[512,512]{1,0:T(8,128)(2,1)}, u32[]{:S(2)}, u32[]{:S(2)}) collective-permute-start(bf16[512,512]{1,0:T(8,128)(2,1)} %get-tuple-element.97), channel_id=1, source_target_pairs={{0,1},{1,0},{2,3},{3,2},{4,5},{5,4},{6,7},{7,6},{8,9},{9,8},{10,11... | collective-permute-start | bytes 1572872 | tf_op jit(solution)/shard_map/ppermute | solution.py:54
  151.7 3.7 %all-to-all-start.5 = ((bf16[4,128,1024]{2,1,0:T(8,128)(2,1)}), bf16[4,128,1024]{2,1,0:T(8,128)(2,1)S(1)}, u32[]{:S(2)}, u32[]{:S(2)}) async-start(bf16[4,128,1024]{2,1,0:T(8,128)(2,1)} %bitcast.34), calls=%async_computation.5 | async-start | bytes 2097152 | tf_op jit(solution)/shard_map/all_to_all | solution.py:647
  159.3 5.1 %shard_map.256 = (bf16[4,256,512]{2,1,0:T(8,128)(2,1)S(1)}, bf16[4,256,512]{2,1,0:T(8,128)(2,1)}, bf16[512,1024]{1,0:T(8,128)(2,1)S(1)}, f32[4,16,512]{2,1,0:T(8,128)S(1)}) custom-call(bf16[512,256]{1,0:T(8,128)(2,1)S(1)} %copy-done.27, f32[512,512]{1,0:T(8,128)S(1)} %copy-done.24, bf16[512,512]{1,0:T(8,128)(2,1)} %collective-permute-done.19.far_grad, ...), custom_call_target="tpu_custom_call" | custom-call | flops 12884901888 | bytes 83361792 | tf_op jit(solution)/shard_map/pallas_call | solution.py:95
  169.0 3.5 %all-to-all-start.6 = ((bf16[4,128,1024]{2,1,0:T(8,128)(2,1)}), bf16[4,128,1024]{2,1,0:T(8,128)(2,1)S(1)}, u32[]{:S(2)}, u32[]{:S(2)}) async-start(bf16[4,128,1024]{2,1,0:T(8,128)(2,1)} %bitcast.35), calls=%async_computation.6 | async-start | bytes 2097152 | tf_op jit(solution)/shard_map/all_to_all | solution.py:685
  183.5 8.1 %all-to-all-done.6 = bf16[4,128,1024]{2,1,0:T(8,128)(2,1)S(1)} async-done(((bf16[4,128,1024]{2,1,0:T(8,128)(2,1)}), bf16[4,128,1024]{2,1,0:T(8,128)(2,1)S(1)}, u32[]{:S(2)}, u32[]{:S(2)}) %all-to-all-start.6) | async-done | bytes 1048608 | tf_op jit(solution)/shard_map/all_to_all | solution.py:685
  191.6 16.3 %collective-permute-done.22.p2 = bf16[2,128,1024]{2,1,0:T(8,128)(2,1)} collective-permute-done((bf16[2,128,1024]{2,1,0:T(8,128)(2,1)}, bf16[2,128,1024]{2,1,0:T(8,128)(2,1)}, u32[]{:S(2)}, u32[]{:S(2)}) %collective-permute-start.22) | collective-permute-done | bytes 524320 | tf_op jit(solution)/shard_map/ppermute | solution.py:54
  217.0 2.9 %collective-permute-start.27 = (bf16[2,128,1024]{2,1,0:T(8,128)(2,1)}, bf16[2,128,1024]{2,1,0:T(8,128)(2,1)S(1)}, u32[]{:S(2)}, u32[]{:S(2)}) collective-permute-start(bf16[2,128,1024]{2,1,0:T(8,128)(2,1)} %reduce-scatter.2.cloned.1.call-done.p0), channel_id=1, source_target_pairs={{0,1},{1,0},{2,3},{3,2},{4,5},{5,4},{6,7},{7,6},{8,9},{9,8},{10,11... | collective-permute-start | bytes 1572872 | tf_op jit(solution)/shard_map/ppermute | solution.py:54
  222.1 3.7 %collective-permute-start.34 = (bf16[272,512]{1,0:T(8,128)(2,1)S(1)}, bf16[272,512]{1,0:T(8,128)(2,1)S(1)}, u32[]{:S(2)}, u32[]{:S(2)}) collective-permute-start(bf16[272,512]{1,0:T(8,128)(2,1)S(1)} %add_convert_fusion.p0), channel_id=1, source_target_pairs={{0,1},{1,0},{2,3},{3,2},{4,5},{5,4},{6,7},{7,6},{8,9},{9,8},{10,11... | collective-permute-start | bytes 835592 | tf_op jit(solution)/shard_map/ppermute | solution.py:54
  228.7 5.3 %shard_map.259 = (f32[1024,1024]{1,0:T(8,128)}, f32[1024,1024]{1,0:T(8,128)}) custom-call(bf16[2,128,1024]{2,1,0:T(8,128)(2,1)S(1)} %copy-done.13, bf16[2,128,1024]{2,1,0:T(8,128)(2,1)} %collective-permute-done.21.p1, bf16[2,128,1024]{2,1,0:T(8,128)(2,1)} %collective-permute-done.22.p2, bf16[2,128,1024]{2,1,0:T(8,128)(2,1)} %collective-permute-done.23.p3, ...), custom_call_target="tpu_custom_call" | custom-call | bytes 100663296 | tf_op jit(solution)/shard_map/pallas_call | solution.py:95
  233.9 2.5 %shard_map.260 = (f32[256,3072]{1,0:T(8,128)}, f32[256,1024]{1,0:T(8,128)}, f32[16,256]{1,0:T(8,128)S(1)}) custom-call(bf16[272,512]{1,0:T(8,128)(2,1)S(1)} %add_convert_fusion.p0, bf16[272,512]{1,0:T(8,128)(2,1)S(1)} %collective-permute-done.31.p1, bf16[272,512]{1,0:T(8,128)(2,1)S(1)} %collective-permute-done.32.p2, ...), custom_call_target="tpu_custom_call" | custom-call | bytes 51511296 | tf_op jit(solution)/shard_map/pallas_call | solution.py:95
  (176 shorter events, 72.8 us)
Async XLA Ops:
  7.2 85.7 %all-gather.4.cloned.1.call-start = ((), (), s32[]{:S(2)}) async-start(), calls=%async_computation.8 | async-start | bytes 1310720 | tf_op jit(solution)/shard_map/all_gather | solution.py:561
  10.5 30.1 %all-to-all-start = ((bf16[4,128,1024]{2,1,0:T(8,128)(2,1)}), bf16[4,128,1024]{2,1,0:T(8,128)(2,1)S(1)}, u32[]{:S(2)}, u32[]{:S(2)}) async-start(bf16[4,128,1024]{2,1,0:T(8,128)(2,1)} %bitcast.46), calls=%async_computation | async-start | bytes 2097152 | tf_op jit(solution)/shard_map/all_to_all | solution.py:554
  14.2 78.7 %all-gather.6.cloned.1.call-start = ((), (), s32[]{:S(2)}) async-start(), calls=%async_computation.10 | async-start | bytes 4718592 | tf_op jit(solution)/shard_map/all_gather | solution.py:566
  14.3 14.3 %collective-permute-start.1 = (bf16[272,512]{1,0:T(8,128)(2,1)S(1)}, bf16[272,512]{1,0:T(8,128)(2,1)S(1)}, u32[]{:S(2)}, u32[]{:S(2)}) collective-permute-start(bf16[272,512]{1,0:T(8,128)(2,1)S(1)} %copy-done.25), channel_id=1, source_target_pairs={{0,4},{2,6},{4,0},{6,2},{1,5},{3,7},{5,1},{7,3},{8,12},{10,14},{12... | collective-permute-start | bytes 835592 | tf_op jit(solution)/shard_map/ppermute | solution.py:54
  16.8 23.8 %collective-permute-start.2 = (bf16[272,512]{1,0:T(8,128)(2,1)S(1)}, bf16[272,512]{1,0:T(8,128)(2,1)S(1)}, u32[]{:S(2)}, u32[]{:S(2)}) collective-permute-start(bf16[272,512]{1,0:T(8,128)(2,1)S(1)} %copy-done.25), channel_id=1, source_target_pairs={{0,6},{2,4},{4,2},{6,0},{1,7},{3,5},{5,3},{7,1},{8,14},{10,12},{12... | collective-permute-start | bytes 835592 | tf_op jit(solution)/shard_map/ppermute | solution.py:54
  40.6 126.4 %reduce-scatter.2.cloned.1.call-start = ((), (), s32[]{:S(2)}) async-start(), calls=%async_computation.9 | async-start | bytes 4718592 | tf_op jit(solution)/shard_map/reduce_scatter | solution.py:637
  51.2 12.7 %collective-permute-start.9 = (bf16[1024,128]{1,0:T(8,128)(2,1)S(1)}, bf16[1024,128]{1,0:T(8,128)(2,1)S(1)}, u32[]{:S(2)}, u32[]{:S(2)}) collective-permute-start(bf16[1024,128]{1,0:T(8,128)(2,1)S(1)} %get-tuple-element.76.p0), channel_id=1, source_target_pairs={{0,16},{8,24},{16,0},{24,8},{1,17},{9,25},{17,1},{25,9},{2,18},{10... | collective-permute-start | bytes 786440 | tf_op jit(solution)/shard_map/ppermute | solution.py:54
  51.5 12.8 %collective-permute-start.8 = (bf16[1024,128]{1,0:T(8,128)(2,1)S(1)}, bf16[1024,128]{1,0:T(8,128)(2,1)S(1)}, u32[]{:S(2)}, u32[]{:S(2)}) collective-permute-start(bf16[1024,128]{1,0:T(8,128)(2,1)S(1)} %get-tuple-element.76.p0), channel_id=1, source_target_pairs={{0,8},{8,0},{16,24},{24,16},{1,9},{9,1},{17,25},{25,17},{2,10},{10... | collective-permute-start | bytes 786440 | tf_op jit(solution)/shard_map/ppermute | solution.py:54
  59.4 13.2 %collective-permute-start.15 = (bf16[1024,128]{1,0:T(8,128)(2,1)S(1)}, bf16[1024,128]{1,0:T(8,128)(2,1)S(1)}, u32[]{:S(2)}, u32[]{:S(2)}) collective-permute-start(bf16[1024,128]{1,0:T(8,128)(2,1)S(1)} %collective-permute-done.10.p3), channel_id=1, source_target_pairs={{0,1},{1,0},{2,3},{3,2},{4,5},{5,4},{6,7},{7,6},{8,9},{9,8},{10,11... | collective-permute-start | bytes 786440 | tf_op jit(solution)/shard_map/ppermute | solution.py:54
  90.3 10.8 %collective-permute-start.16 = (bf16[512,256]{1,0:T(8,128)(2,1)S(1)}, bf16[512,256]{1,0:T(8,128)(2,1)}, u32[]{:S(2)}, u32[]{:S(2)}) collective-permute-start(bf16[512,256]{1,0:T(8,128)(2,1)S(1)} %shard_map.248.a0), channel_id=1, source_target_pairs={{0,8},{8,0},{16,24},{24,16},{1,9},{9,1},{17,25},{25,17},{2,10},{10... | collective-permute-start | bytes 786440 | tf_op jit(solution)/shard_map/ppermute | solution.py:54
  145.5 11.7 %collective-permute-start.19 = (bf16[512,512]{1,0:T(8,128)(2,1)}, bf16[512,512]{1,0:T(8,128)(2,1)}, u32[]{:S(2)}, u32[]{:S(2)}) collective-permute-start(bf16[512,512]{1,0:T(8,128)(2,1)} %get-tuple-element.97), channel_id=1, source_target_pairs={{0,1},{1,0},{2,3},{3,2},{4,5},{5,4},{6,7},{7,6},{8,9},{9,8},{10,11... | collective-permute-start | bytes 1572872 | tf_op jit(solution)/shard_map/ppermute | solution.py:54
  151.7 17.3 %all-to-all-start.5 = ((bf16[4,128,1024]{2,1,0:T(8,128)(2,1)}), bf16[4,128,1024]{2,1,0:T(8,128)(2,1)S(1)}, u32[]{:S(2)}, u32[]{:S(2)}) async-start(bf16[4,128,1024]{2,1,0:T(8,128)(2,1)} %bitcast.34), calls=%async_computation.5 | async-start | bytes 2097152 | tf_op jit(solution)/shard_map/all_to_all | solution.py:647
  167.0 14.6 %collective-permute-start.21 = (bf16[2,128,1024]{2,1,0:T(8,128)(2,1)}, bf16[2,128,1024]{2,1,0:T(8,128)(2,1)}, u32[]{:S(2)}, u32[]{:S(2)}) collective-permute-start(bf16[2,128,1024]{2,1,0:T(8,128)(2,1)} %reduce-scatter.2.cloned.1.call-done.p0), channel_id=1, source_target_pairs={{0,8},{8,0},{16,24},{24,16},{1,9},{9,1},{17,25},{25,17},{2,10},{10... | collective-permute-start | bytes 1572872 | tf_op jit(solution)/shard_map/ppermute | solution.py:54
  169.0 22.7 %all-to-all-start.6 = ((bf16[4,128,1024]{2,1,0:T(8,128)(2,1)}), bf16[4,128,1024]{2,1,0:T(8,128)(2,1)S(1)}, u32[]{:S(2)}, u32[]{:S(2)}) async-start(bf16[4,128,1024]{2,1,0:T(8,128)(2,1)} %bitcast.35), calls=%async_computation.6 | async-start | bytes 2097152 | tf_op jit(solution)/shard_map/all_to_all | solution.py:685
  172.5 35.4 %collective-permute-start.22 = (bf16[2,128,1024]{2,1,0:T(8,128)(2,1)}, bf16[2,128,1024]{2,1,0:T(8,128)(2,1)}, u32[]{:S(2)}, u32[]{:S(2)}) collective-permute-start(bf16[2,128,1024]{2,1,0:T(8,128)(2,1)} %reduce-scatter.2.cloned.1.call-done.p0), channel_id=1, source_target_pairs={{0,16},{8,24},{16,0},{24,8},{1,17},{9,25},{17,1},{25,9},{2,18},{10... | collective-permute-start | bytes 1572872 | tf_op jit(solution)/shard_map/ppermute | solution.py:54
  173.9 34.0 %collective-permute-start.23 = (bf16[2,128,1024]{2,1,0:T(8,128)(2,1)}, bf16[2,128,1024]{2,1,0:T(8,128)(2,1)}, u32[]{:S(2)}, u32[]{:S(2)}) collective-permute-start(bf16[2,128,1024]{2,1,0:T(8,128)(2,1)} %reduce-scatter.2.cloned.1.call-done.p0), channel_id=1, source_target_pairs={{0,24},{8,16},{16,8},{24,0},{1,25},{9,17},{17,9},{25,1},{2,26},{10... | collective-permute-start | bytes 1572872 | tf_op jit(solution)/shard_map/ppermute | solution.py:54
  179.5 28.4 %collective-permute-start.24 = (bf16[272,512]{1,0:T(8,128)(2,1)}, bf16[272,512]{1,0:T(8,128)(2,1)}, u32[]{:S(2)}, u32[]{:S(2)}) collective-permute-start(bf16[272,512]{1,0:T(8,128)(2,1)} %get-tuple-element.113), channel_id=1, source_target_pairs={{0,2},{2,0},{4,6},{6,4},{1,3},{3,1},{5,7},{7,5},{8,10},{10,8},{12,... | collective-permute-start | bytes 835592 | tf_op jit(solution)/shard_map/ppermute | solution.py:54
  181.5 26.4 %collective-permute-start.25 = (bf16[272,512]{1,0:T(8,128)(2,1)}, bf16[272,512]{1,0:T(8,128)(2,1)}, u32[]{:S(2)}, u32[]{:S(2)}) collective-permute-start(bf16[272,512]{1,0:T(8,128)(2,1)} %get-tuple-element.114), channel_id=1, source_target_pairs={{0,4},{2,6},{4,0},{6,2},{1,5},{3,7},{5,1},{7,3},{8,12},{10,14},{12... | collective-permute-start | bytes 835592 | tf_op jit(solution)/shard_map/ppermute | solution.py:54
  181.6 26.3 %collective-permute-start.26 = (bf16[272,512]{1,0:T(8,128)(2,1)}, bf16[272,512]{1,0:T(8,128)(2,1)}, u32[]{:S(2)}, u32[]{:S(2)}) collective-permute-start(bf16[272,512]{1,0:T(8,128)(2,1)} %get-tuple-element.115), channel_id=1, source_target_pairs={{0,6},{2,4},{4,2},{6,0},{1,7},{3,5},{5,3},{7,1},{8,14},{10,12},{12... | collective-permute-start | bytes 835592 | tf_op jit(solution)/shard_map/ppermute | solution.py:54
  210.8 15.1 %collective-permute-start.30 = (bf16[2,128,1024]{2,1,0:T(8,128)(2,1)}, bf16[2,128,1024]{2,1,0:T(8,128)(2,1)S(1)}, u32[]{:S(2)}, u32[]{:S(2)}) collective-permute-start(bf16[2,128,1024]{2,1,0:T(8,128)(2,1)} %collective-permute-done.23.p3), channel_id=1, source_target_pairs={{0,1},{1,0},{2,3},{3,2},{4,5},{5,4},{6,7},{7,6},{8,9},{9,8},{10,11... | collective-permute-start | bytes 1572872 | tf_op jit(solution)/shard_map/ppermute | solution.py:54
  213.0 12.8 %collective-permute-start.29 = (bf16[2,128,1024]{2,1,0:T(8,128)(2,1)}, bf16[2,128,1024]{2,1,0:T(8,128)(2,1)S(1)}, u32[]{:S(2)}, u32[]{:S(2)}) collective-permute-start(bf16[2,128,1024]{2,1,0:T(8,128)(2,1)} %collective-permute-done.22.p2), channel_id=1, source_target_pairs={{0,1},{1,0},{2,3},{3,2},{4,5},{5,4},{6,7},{7,6},{8,9},{9,8},{10,11... | collective-permute-start | bytes 1572872 | tf_op jit(solution)/shard_map/ppermute | solution.py:54
  213.0 13.3 %collective-permute-start.28 = (bf16[2,128,1024]{2,1,0:T(8,128)(2,1)}, bf16[2,128,1024]{2,1,0:T(8,128)(2,1)S(1)}, u32[]{:S(2)}, u32[]{:S(2)}) collective-permute-start(bf16[2,128,1024]{2,1,0:T(8,128)(2,1)} %collective-permute-done.21.p1), channel_id=1, source_target_pairs={{0,1},{1,0},{2,3},{3,2},{4,5},{5,4},{6,7},{7,6},{8,9},{9,8},{10,11... | collective-permute-start | bytes 1572872 | tf_op jit(solution)/shard_map/ppermute | solution.py:54
  217.0 11.7 %collective-permute-start.27 = (bf16[2,128,1024]{2,1,0:T(8,128)(2,1)}, bf16[2,128,1024]{2,1,0:T(8,128)(2,1)S(1)}, u32[]{:S(2)}, u32[]{:S(2)}) collective-permute-start(bf16[2,128,1024]{2,1,0:T(8,128)(2,1)} %reduce-scatter.2.cloned.1.call-done.p0), channel_id=1, source_target_pairs={{0,1},{1,0},{2,3},{3,2},{4,5},{5,4},{6,7},{7,6},{8,9},{9,8},{10,11... | collective-permute-start | bytes 1572872 | tf_op jit(solution)/shard_map/ppermute | solution.py:54
  222.1 11.8 %collective-permute-start.34 = (bf16[272,512]{1,0:T(8,128)(2,1)S(1)}, bf16[272,512]{1,0:T(8,128)(2,1)S(1)}, u32[]{:S(2)}, u32[]{:S(2)}) collective-permute-start(bf16[272,512]{1,0:T(8,128)(2,1)S(1)} %add_convert_fusion.p0), channel_id=1, source_target_pairs={{0,1},{1,0},{2,3},{3,2},{4,5},{5,4},{6,7},{7,6},{8,9},{9,8},{10,11... | collective-permute-start | bytes 835592 | tf_op jit(solution)/shard_map/ppermute | solution.py:54
  (60 other events, 375.2 us)
Sparse Core Ops, SparseCore 0:
  9.9 34.7 all-gather.3
  46.8 46.0 all-gather.5
  110.9 50.5 reduce-scatter.1

commit v3 on v2

--- a/solution.py
+++ b/solution.py
@@ -200,13 +200,10 @@
     return contract(left, right, 1, 1)
 
 
-def head_probs(query, key_own, key_far, causal, far_seen):
+def head_scores(query, key_own, key_far, causal, far_seen):
     own = jnp.where(causal, dot_rows(query, key_own) * SCALE, masked_value)
     far = jnp.where(far_seen, dot_rows(query, key_far) * SCALE, masked_value)
-    peak = jnp.maximum(jnp.max(own, -1, keepdims=True), jnp.max(far, -1, keepdims=True))
-    own, far = jnp.exp(own - peak), jnp.exp(far - peak)
-    share = 1.0 / (jnp.sum(own, -1, keepdims=True) + jnp.sum(far, -1, keepdims=True))
-    return own * share, far * share
+    return own, far
 
 
 def head_masks(core):
@@ -218,9 +215,10 @@
     return causal, far_seen, first
 
 
-def attend_kernel(qkv, far, attended):
+def attend_kernel(qkv, far, attended, logs):
     core = lax.axis_index("seq")
     causal, far_seen, first = head_masks(core)
+    lane = lax.broadcasted_iota(jnp.int32, (ROWS, LANE), 1)
 
     for sequence in range(REPS):
         at = pl.ds(sequence * ROWS, ROWS)
@@ -232,13 +230,22 @@
             key_far = far[at, 2 * p * LANE : (2 * p + 1) * LANE]
             value_far = far[at, (2 * p + 1) * LANE : (2 * p + 2) * LANE]
             heads = []
-            for mask in (first, ~first):
+            for h, mask in enumerate((first, ~first)):
                 masked = jnp.where(mask, query, jnp.zeros_like(query))
-                own, other = head_probs(masked, key_own, key_far, causal, far_seen)
+                own, other = head_scores(masked, key_own, key_far, causal, far_seen)
+                peak = jnp.max(jnp.maximum(own, other), -1, keepdims=True)
+                own, other = jnp.exp(own - peak), jnp.exp(other - peak)
+                whole = jnp.sum(own + other, -1, keepdims=True)
+                share = 1.0 / whole
+                own, other = own * share, other * share
+                log = jnp.broadcast_to(peak + jnp.log(whole), (ROWS, LANE))
+                kept = log if p + h == 0 else jnp.where(lane == 2 * p + h, log, kept)
                 heads.append(
                     jnp.dot(own.astype(bf16), value_own, preferred_element_type=f32)
                     + jnp.dot(other.astype(bf16), value_far, preferred_element_type=f32)
                 )
+            if p == CORES - 1:
+                logs[at, :] = kept
             attended[at, p * LANE : (p + 1) * LANE] = jnp.where(first, *heads).astype(bf16)
 
 
@@ -264,7 +271,11 @@
         normed[k * ROWS : (k + 1) * ROWS, :] = low
 
 
-def hidden_kernel(h, c, ff, vectors, back, hidden, pre_grad):
+def hidden_kernel(h, c0, c1, c2, c3, ff, vectors, back, hidden, pre_grad, c):
+    rep = lax.axis_index("rep")
+    for k, cot in enumerate((c0, c1, c2, c3)):
+        c[pl.ds(pl.multiple_of((rep ^ k) * ROWS, ROWS), ROWS), :] = cot[...]
+
     @pl.loop(0, 2)
     def _(block):
         at = pl.ds(pl.multiple_of(block * 2 * ROWS, 2 * ROWS), 2 * ROWS)
@@ -342,7 +353,7 @@
             far[rep ^ k ^ shard, at, :] = other[p * LANE : (p + 1) * LANE]
 
 
-def attend_back_kernel(qkv, far, pairs, query_grad, own_grad, far_grad):
+def attend_back_kernel(qkv, far, logs, pairs, query_grad, own_grad, far_grad):
     core = lax.axis_index("seq")
     causal, far_seen, first = head_masks(core)
 
@@ -357,14 +368,14 @@
             value_far = far[at, (2 * p + 1) * LANE : (2 * p + 2) * LANE]
             grad = pairs[at, p * LANE : (p + 1) * LANE]
             queries, sums = [], [0.0] * 4
-            for mask in (first, ~first):
+            for h, mask in enumerate((first, ~first)):
                 masked = jnp.where(mask, query, jnp.zeros_like(query))
                 back = jnp.where(mask, grad, jnp.zeros_like(grad))
-                own, other = head_probs(masked, key_own, key_far, causal, far_seen)
+                own, other = head_scores(masked, key_own, key_far, causal, far_seen)
+                log = logs[at, 2 * p + h : 2 * p + h + 1]
+                own, other = jnp.exp(own - log), jnp.exp(other - log)
                 own_back, other_back = dot_rows(back, value_own), dot_rows(back, value_far)
-                row = jnp.sum(own * own_back, -1, keepdims=True) + jnp.sum(
-                    other * other_back, -1, keepdims=True
-                )
+                row = jnp.sum(own * own_back + other * other_back, -1, keepdims=True)
                 own_score = (own * (own_back - row)).astype(bf16)
                 other_score = (other * (other_back - row)).astype(bf16)
                 queries.append(
@@ -558,11 +569,11 @@
         [((all_rows, WIDTH), f32), ((all_rows, LANE), f32), ((2, ROWS, WIDTH), f32)],
         [inputs],
     )
-    cots = lax.all_gather(cotangent, "rep", axis=0, tiled=True)
+    cots = over_rep([cotangent] * REPS)
 
     mine = rep * CORES + core
     ff = [pick(w.reshape(REPS * CORES, LANE, WIDTH), mine, 0) for w in (fc_weight, out_weight)]
-    ff = after(jnp.stack(ff), *own_packed[1:], inputs)
+    ff = after(jnp.stack(ff), *own_packed[1:], inputs, *cots[1:])
     ff = lax.all_gather(ff, ("fsdp", "seq"), axis=0)
 
     qkv, kv_send, normed_one, qkv_mine, vectors, proj_cols = vmem_call(
@@ -581,14 +592,13 @@
     )
     kv_far = over_cores(kv_send)
     proj_cols = over_rep([proj_cols] * REPS)
-    (attended,) = vmem_call(
+    attended, logs = vmem_call(
         attend_kernel,
-        [((all_rows, SHARD), bf16)],
+        [((all_rows, SHARD), bf16), ((all_rows, LANE), f32)],
         [qkv, kv_far],
         flops=4 * all_rows * 2 * ROWS * SHARD,
     )
     mine = lax.all_to_all(attended, "rep", 0, 0, tiled=True)
-    marker = over_cores(attended[:16, :LANE])
     middle, unit_two, scale_two, normed_two, proj_full = vmem_call(
         branch_kernel,
         [
@@ -600,7 +610,7 @@
         ],
         [mine]
         + proj_cols
-        + [over_cores(after(p, marker)) for p in proj_cols]
+        + [over_cores(after(p, mine)) for p in proj_cols]
         + [block_input, vectors],
         scratch=[pltpu.VMEM((ROWS, WIDTH), bf16)],
         flops=2 * ROWS * WIDTH * WIDTH,
@@ -608,14 +618,15 @@
     normed_two = lax.all_to_all(normed_two, "rep", 0, 0, tiled=True)
     attended_all = over_rep([after(attended, normed_two)] * REPS)
 
-    back, hidden, pre_grad = vmem_call(
+    back, hidden, pre_grad, c_all = vmem_call(
         hidden_kernel,
         [
             ((all_rows, WIDTH), bf16),
             ((all_rows, HIDDEN), bf16),
             ((all_rows, HIDDEN), bf16),
+            ((all_rows, WIDTH), bf16),
         ],
-        [normed_two, cots, ff, vectors],
+        [normed_two] + cots + [ff, vectors],
         flops=6 * all_rows * WIDTH * HIDDEN,
     )
     back = lax.all_to_all(back, "rep", 0, 0, tiled=True)
@@ -626,7 +637,7 @@
             ((SHARDS * CORES * 2, LANE, WIDTH), bf16),
             ((8, HIDDEN), f32),
         ],
-        [after(hidden, *attended_all[1:]), pre_grad, normed_two, cots, ff],
+        [after(hidden, *attended_all[1:]), pre_grad, normed_two, c_all, ff],
         scratch=[
             pltpu.VMEM((SHARDS * CORES * 2, LANE, WIDTH), bf16),
             pltpu.SemaphoreType.DMA((SHARDS,)),
@@ -653,7 +664,7 @@
             ((all_rows, 4 * LANE), f32),
             ((all_rows, 4 * LANE), bf16),
         ],
-        [qkv, kv_far, pairs],
+        [qkv, kv_far, logs, pairs],
         weight=1,
         flops=10 * all_rows * 2 * ROWS * SHARD,
     )
@@ -697,7 +708,7 @@
     qkv_grads, proj_grads, small = vmem_call(
         final_kernel,
         [((SHARD, 3 * WIDTH), f32), ((SHARD, WIDTH), f32), ((16, SHARD), f32)],
-        [after(tail[0], fc_grads)] + tail[1:] + [over_cores(t) for t in tail],
+        tail + [over_cores(after(t, fc_grads, input_grad)) for t in tail],
     )
     return (
         block_output,

time: 249 us -> 238 us (0.956); the launches traced: 245 us -> 237 us
  waiting for transfers between devices: 58.4 us -> 50.1 us
  blocking collectives: 43.7 us -> 47.4 us
  Pallas kernels: 51.6 us -> 49 us
    ppermute x38 -> x40, waiting for transfers between devices: 49.1 us -> 40.8 us  [swap(): return lax.ppermute(value, axis, [(i, i ^ offset) for i in range(size)])]
    pallas_call x16, Pallas kernels: 51.6 us -> 49 us  [vmem_call(): pl.pallas_call(body if staged else kernel, out_shape=[jax.ShapeDtypeStruc...]
    ppermute x38 -> x40, starting transfers between devices: 39.3 us -> 37.2 us  [swap(): return lax.ppermute(value, axis, [(i, i ^ offset) for i in range(size)])]
    unnamed x84 -> x100, local copies, waits for them, and re-layouts: 22.7 us -> 23.9 us
  transfers between devices with their start and end apart: 44 -> 45, of which waited for: 12 -> 14; matrix products, arithmetic and copies ran while one was open for 1% -> 1% of each run, Pallas kernels for 18% -> 16%
where the time goes in v3:
time: 238 us; the launch traced here: 237 us
  waiting for transfers between devices  50.1 us (21%)
  Pallas kernels  49 us (21%)
  starting transfers between devices  48.2 us (20%)
  blocking collectives  47.4 us (20%)
  local copies, waits for them, and re-layouts  25.6 us (11%)
  between operations  14.5 us (6%)
    pallas_call x16, Pallas kernels, vmem_call(): pl.pallas_call(body if staged else kernel, out_shape=[jax.ShapeDtypeStruc...  49 us
    ppermute x40, waiting for transfers between devices, swap(): return lax.ppermute(value, axis, [(i, i ^ offset) for i in range(size)])  40.8 us
    ppermute x40, starting transfers between devices, swap(): return lax.ppermute(value, axis, [(i, i ^ offset) for i in range(size)])  37.2 us
    unnamed x100, local copies, waits for them, and re-layouts  23.9 us
    all_to_all x1, blocking collectives, tiled_body(): normed_two = lax.all_to_all(normed_two, 'rep', 0, 0, tiled=True)  15.8 us
    all_to_all x1, blocking collectives, tiled_body(): back = lax.all_to_all(back, 'rep', 0, 0, tiled=True)  13.9 us
    all_to_all x1, blocking collectives, tiled_body(): mine = lax.all_to_all(attended, 'rep', 0, 0, tiled=True)  9.36 us
    all_to_all x1, waiting for transfers between devices, tiled_body(): joined = lax.all_to_all(joined, 'rep', 0, 0, tiled=True)  9.18 us
  transfers between devices with their start and end apart: 45, of which 14 were waited for; matrix products, arithmetic and copies ran while one was open for 1% of the time, Pallas kernels for 16%

profile of v3, /device:TPU:9, one launch (start us, length us, event | category | flops | bytes accessed | tf_op | source)
XLA Modules:
  0.0 237.0 jit_solution(17443151786971936977)
XLA Ops:
  7.2 2.6 %shard_map.245 = (bf16[272,512]{1,0:T(8,128)(2,1)}, bf16[512,1024]{1,0:T(8,128)(2,1)}) custom-call(bf16[256,3072]{1,0:T(8,128)(2,1)} %refs_0_.1, bf16[256,1024]{1,0:T(8,128)(2,1)} %refs_1_.1, bf16[128,1024]{1,0:T(8,128)(2,1)} %x.1, bf16[256]{0:T(256)(128)(2,1)} %refs_3_.1, bf16[256]{0:T(256)(128)(2,1)} %refs_4_.1, bf16[512]{0:T(512)(128)(2,1)} %refs_5_.1, ...), custom_call_target="tpu_custom_call" | custom-call | bytes 29540352 | tf_op jit(solution)/shard_map/pallas_call | solution.py:95
  9.8 3.7 %all-to-all-start = ((bf16[4,128,1024]{2,1,0:T(8,128)(2,1)}), bf16[4,128,1024]{2,1,0:T(8,128)(2,1)S(1)}, u32[]{:S(2)}, u32[]{:S(2)}) async-start(bf16[4,128,1024]{2,1,0:T(8,128)(2,1)} %bitcast.46), calls=%async_computation | async-start | bytes 2097152 | tf_op jit(solution)/shard_map/all_to_all | solution.py:565
  18.8 13.1 %collective-permute-done.15.c1 = bf16[128,1024]{1,0:T(8,128)(2,1)S(1)} collective-permute-done((bf16[128,1024]{1,0:T(8,128)(2,1)S(1)}, bf16[128,1024]{1,0:T(8,128)(2,1)S(1)}, u32[]{:S(2)}, u32[]{:S(2)}) %collective-permute-start.15) | collective-permute-done | bytes 262176 | tf_op jit(solution)/shard_map/ppermute | solution.py:54
  34.9 3.9 %collective-permute-done.17.c3 = bf16[128,1024]{1,0:T(8,128)(2,1)S(1)} collective-permute-done((bf16[128,1024]{1,0:T(8,128)(2,1)S(1)}, bf16[128,1024]{1,0:T(8,128)(2,1)S(1)}, u32[]{:S(2)}, u32[]{:S(2)}) %collective-permute-start.17) | collective-permute-done | bytes 262176 | tf_op jit(solution)/shard_map/ppermute | solution.py:54
  40.6 2.7 %collective-permute-start.3 = (bf16[272,512]{1,0:T(8,128)(2,1)S(1)}, bf16[272,512]{1,0:T(8,128)(2,1)S(1)}, u32[]{:S(2)}, u32[]{:S(2)}) collective-permute-start(bf16[272,512]{1,0:T(8,128)(2,1)S(1)} %copy-done.24), channel_id=1, source_target_pairs={{0,1},{1,0},{2,3},{3,2},{4,5},{5,4},{6,7},{7,6},{8,9},{9,8},{10,11... | collective-permute-start | bytes 835592 | tf_op jit(solution)/shard_map/ppermute | solution.py:54
  52.3 5.6 %shard_map.248 = (bf16[512,256]{1,0:T(8,128)(2,1)S(1)}, f32[512,128]{1,0:T(8,128)S(1)}) custom-call(bf16[512,768]{1,0:T(8,128)(2,1)S(1)} %get-tuple-element.79.qkv, bf16[512,512]{1,0:T(8,128)(2,1)S(1)} %collective-permute-done.7.far), custom_call_target="tpu_custom_call" | custom-call | flops 1073741824 | bytes 14680064 | tf_op jit(solution)/shard_map/pallas_call | solution.py:95
  57.9 9.4 %all_to_all.77 = bf16[4,128,256]{2,1,0:T(8,128)(2,1)S(1)} all-to-all(bf16[4,128,256]{2,1,0:T(8,128)(2,1)S(1)} %bitcast.42), channel_id=1, replica_groups=mesh['rep'=4,'fsdp'=4,'seq'=2] {'rep'}, dimensions={0} | all-to-all | bytes 524288 | tf_op jit(solution)/shard_map/all_to_all | solution.py:601
  72.9 15.8 %all_to_all.78 = bf16[4,128,1024]{2,1,0:T(8,128)(2,1)S(1)} all-to-all(bf16[4,128,1024]{2,1,0:T(8,128)(2,1)S(1)} %bitcast.39), channel_id=1, replica_groups=mesh['rep'=4,'fsdp'=4,'seq'=2] {'rep'}, dimensions={0} | all-to-all | bytes 2097152 | tf_op jit(solution)/shard_map/all_to_all | solution.py:618
  97.4 4.8 %shard_map.250 = (bf16[512,1024]{1,0:T(8,128)(2,1)S(1)}, bf16[512,1024]{1,0:T(8,128)(2,1)S(1)}, bf16[512,1024]{1,0:T(8,128)(2,1)S(1)}, bf16[512,1024]{1,0:T(8,128)(2,1)S(1)}) custom-call(bf16[512,1024]{1,0:T(8,128)(2,1)S(1)} %bitcast.36, bf16[128,1024]{1,0:T(8,128)(2,1)S(1)} %copy-done.26, bf16[128,1024]{1,0:T(8,128)(2,1)S(1)} %copy-done.29, ...), custom_call_target="tpu_custom_call" | custom-call | flops 25769803776 | bytes 84410368 | tf_op jit(solution)/shard_map/pallas_call | solution.py:95
  102.2 4.9 %shard_map.251 = (bf16[512,1024]{1,0:T(8,128)(2,1)S(1)}, bf16[16,128,1024]{2,1,0:T(8,128)(2,1)S(1)}, f32[8,1024]{1,0:T(8,128)S(1)}) custom-call(bf16[512,1024]{1,0:T(8,128)(2,1)S(1)} %get-tuple-element.92.hidden, bf16[512,1024]{1,0:T(8,128)(2,1)S(1)} %get-tuple-element.93.pre_grad, bf16[512,1024]{1,0:T(8,128)(2,1)S(1)} %bitcast.37, ...), custom_call_target="tpu_custom_call" | custom-call | flops 25769803776 | bytes 109314048 | tf_op jit(solution)/shard_map/pallas_call | solution.py:95
  110.8 13.9 %all_to_all.79 = bf16[4,128,1024]{2,1,0:T(8,128)(2,1)S(1)} all-to-all(bf16[4,128,1024]{2,1,0:T(8,128)(2,1)S(1)} %bitcast.38), channel_id=1, replica_groups=mesh['rep'=4,'fsdp'=4,'seq'=2] {'rep'}, dimensions={0} | all-to-all | bytes 2097152 | tf_op jit(solution)/shard_map/all_to_all | solution.py:632
  127.5 8.4 %all_to_all.80 = bf16[4,128,512]{2,1,0:T(8,128)(2,1)S(1)} all-to-all(bf16[4,128,512]{2,1,0:T(8,128)(2,1)S(1)} %bitcast.41), channel_id=1, replica_groups=mesh['rep'=4,'fsdp'=4,'seq'=2] {'rep'}, dimensions={0} | all-to-all | bytes 1048576 | tf_op jit(solution)/shard_map/all_to_all | solution.py:657
  135.9 6.7 %shard_map.254 = (bf16[512,256]{1,0:T(8,128)(2,1)S(1)}, f32[512,512]{1,0:T(8,128)S(1)}, bf16[512,512]{1,0:T(8,128)(2,1)}) custom-call(bf16[512,768]{1,0:T(8,128)(2,1)S(1)} %copy-done.6, bf16[512,512]{1,0:T(8,128)(2,1)S(1)} %copy-done.12, f32[512,128]{1,0:T(8,128)S(1)} %copy-done.16, bf16[512,512]{1,0:T(8,128)(2,1)S(1)} %bitcast.32), custom_call_target="tpu_custom_call" | custom-call | flops 335544320 | bytes 3932160 | tf_op jit(solution)/shard_map/pallas_call | solution.py:95
  143.6 4.9 %collective-permute-start.21 = (bf16[512,512]{1,0:T(8,128)(2,1)}, bf16[512,512]{1,0:T(8,128)(2,1)}, u32[]{:S(2)}, u32[]{:S(2)}) collective-permute-start(bf16[512,512]{1,0:T(8,128)(2,1)} %get-tuple-element.106), channel_id=1, source_target_pairs={{0,1},{1,0},{2,3},{3,2},{4,5},{5,4},{6,7},{7,6},{8,9},{9,8},{10,11... | collective-permute-start | bytes 1572872 | tf_op jit(solution)/shard_map/ppermute | solution.py:54
  148.6 3.7 %all-to-all-start.5 = ((bf16[4,128,1024]{2,1,0:T(8,128)(2,1)}), bf16[4,128,1024]{2,1,0:T(8,128)(2,1)S(1)}, u32[]{:S(2)}, u32[]{:S(2)}) async-start(bf16[4,128,1024]{2,1,0:T(8,128)(2,1)} %bitcast.34), calls=%async_computation.5 | async-start | bytes 2097152 | tf_op jit(solution)/shard_map/all_to_all | solution.py:658
  155.3 5.1 %shard_map.256 = (bf16[4,256,512]{2,1,0:T(8,128)(2,1)S(1)}, bf16[4,256,512]{2,1,0:T(8,128)(2,1)}, bf16[512,1024]{1,0:T(8,128)(2,1)S(1)}, f32[4,16,512]{2,1,0:T(8,128)S(1)}) custom-call(bf16[512,256]{1,0:T(8,128)(2,1)S(1)} %copy-done.35, f32[512,512]{1,0:T(8,128)S(1)} %copy-done.23, bf16[512,512]{1,0:T(8,128)(2,1)} %collective-permute-done.21.far_grad, ...), custom_call_target="tpu_custom_call" | custom-call | flops 12884901888 | bytes 83361792 | tf_op jit(solution)/shard_map/pallas_call | solution.py:95
  165.3 3.5 %all-to-all-start.6 = ((bf16[4,128,1024]{2,1,0:T(8,128)(2,1)}), bf16[4,128,1024]{2,1,0:T(8,128)(2,1)S(1)}, u32[]{:S(2)}, u32[]{:S(2)}) async-start(bf16[4,128,1024]{2,1,0:T(8,128)(2,1)} %bitcast.35), calls=%async_computation.6 | async-start | bytes 2097152 | tf_op jit(solution)/shard_map/all_to_all | solution.py:696
  175.8 2.4 collective-permute-start.27
  179.8 9.2 %all-to-all-done.6 = bf16[4,128,1024]{2,1,0:T(8,128)(2,1)S(1)} async-done(((bf16[4,128,1024]{2,1,0:T(8,128)(2,1)}), bf16[4,128,1024]{2,1,0:T(8,128)(2,1)S(1)}, u32[]{:S(2)}, u32[]{:S(2)}) %all-to-all-start.6) | async-done | bytes 1048608 | tf_op jit(solution)/shard_map/all_to_all | solution.py:696
  189.0 14.6 %collective-permute-done.24.p2 = bf16[2,128,1024]{2,1,0:T(8,128)(2,1)} collective-permute-done((bf16[2,128,1024]{2,1,0:T(8,128)(2,1)}, bf16[2,128,1024]{2,1,0:T(8,128)(2,1)}, u32[]{:S(2)}, u32[]{:S(2)}) %collective-permute-start.24) | collective-permute-done | bytes 524320 | tf_op jit(solution)/shard_map/ppermute | solution.py:54
  204.9 2.4 %collective-permute-start.35 = (bf16[2,128,1024]{2,1,0:T(8,128)(2,1)}, bf16[2,128,1024]{2,1,0:T(8,128)(2,1)S(1)}, u32[]{:S(2)}, u32[]{:S(2)}) collective-permute-start(bf16[2,128,1024]{2,1,0:T(8,128)(2,1)} %collective-permute-done.25.p3), channel_id=1, source_target_pairs={{0,1},{1,0},{2,3},{3,2},{4,5},{5,4},{6,7},{7,6},{8,9},{9,8},{10,11... | collective-permute-start | bytes 1572872 | tf_op jit(solution)/shard_map/ppermute | solution.py:54
  213.2 5.3 %shard_map.259 = (f32[1024,1024]{1,0:T(8,128)}, f32[1024,1024]{1,0:T(8,128)}) custom-call(bf16[2,128,1024]{2,1,0:T(8,128)(2,1)S(1)} %copy-done.13, bf16[2,128,1024]{2,1,0:T(8,128)(2,1)} %collective-permute-done.23.p1, bf16[2,128,1024]{2,1,0:T(8,128)(2,1)} %collective-permute-done.24.p2, bf16[2,128,1024]{2,1,0:T(8,128)(2,1)} %collective-permute-done.25.p3, ...), custom_call_target="tpu_custom_call" | custom-call | bytes 100663296 | tf_op jit(solution)/shard_map/pallas_call | solution.py:95
  219.3 4.0 %collective-permute-done.30.p2 = bf16[272,512]{1,0:T(8,128)(2,1)S(1)} collective-permute-done((bf16[272,512]{1,0:T(8,128)(2,1)S(1)}, bf16[272,512]{1,0:T(8,128)(2,1)S(1)}, u32[]{:S(2)}, u32[]{:S(2)}) %collective-permute-start.30) | collective-permute-done | bytes 278560 | tf_op jit(solution)/shard_map/ppermute | solution.py:54
  225.8 2.5 %shard_map.260 = (f32[256,3072]{1,0:T(8,128)}, f32[256,1024]{1,0:T(8,128)}, f32[16,256]{1,0:T(8,128)S(1)}) custom-call(bf16[272,512]{1,0:T(8,128)(2,1)S(1)} %add_convert_fusion.p0, bf16[272,512]{1,0:T(8,128)(2,1)S(1)} %collective-permute-done.29.p1, bf16[272,512]{1,0:T(8,128)(2,1)S(1)} %collective-permute-done.30.p2, ...), custom_call_target="tpu_custom_call" | custom-call | bytes 51511296 | tf_op jit(solution)/shard_map/pallas_call | solution.py:95
  (192 shorter events, 69.4 us)
Async XLA Ops:
  9.8 30.7 %all-to-all-start = ((bf16[4,128,1024]{2,1,0:T(8,128)(2,1)}), bf16[4,128,1024]{2,1,0:T(8,128)(2,1)S(1)}, u32[]{:S(2)}, u32[]{:S(2)}) async-start(bf16[4,128,1024]{2,1,0:T(8,128)(2,1)} %bitcast.46), calls=%async_computation | async-start | bytes 2097152 | tf_op jit(solution)/shard_map/all_to_all | solution.py:565
  13.5 77.9 %all-gather.3.cloned.1.call-start = ((), (), s32[]{:S(2)}) async-start(), calls=%async_computation.9 | async-start | bytes 4718592 | tf_op jit(solution)/shard_map/all_gather | solution.py:577
  13.5 18.3 %collective-permute-start.15 = (bf16[128,1024]{1,0:T(8,128)(2,1)S(1)}, bf16[128,1024]{1,0:T(8,128)(2,1)S(1)}, u32[]{:S(2)}, u32[]{:S(2)}) collective-permute-start(bf16[128,1024]{1,0:T(8,128)(2,1)S(1)} %copy-done.25), channel_id=1, source_target_pairs={{0,8},{8,0},{16,24},{24,16},{1,9},{9,1},{17,25},{25,17},{2,10},{10... | collective-permute-start | bytes 786440 | tf_op jit(solution)/shard_map/ppermute | solution.py:54
  14.9 23.9 %collective-permute-start = (bf16[272,512]{1,0:T(8,128)(2,1)S(1)}, bf16[272,512]{1,0:T(8,128)(2,1)S(1)}, u32[]{:S(2)}, u32[]{:S(2)}) collective-permute-start(bf16[272,512]{1,0:T(8,128)(2,1)S(1)} %copy-done.24), channel_id=1, source_target_pairs={{0,2},{2,0},{4,6},{6,4},{1,3},{3,1},{5,7},{7,5},{8,10},{10,8},{12,... | collective-permute-start | bytes 835592 | tf_op jit(solution)/shard_map/ppermute | solution.py:54
  15.0 23.8 %collective-permute-start.1 = (bf16[272,512]{1,0:T(8,128)(2,1)S(1)}, bf16[272,512]{1,0:T(8,128)(2,1)S(1)}, u32[]{:S(2)}, u32[]{:S(2)}) collective-permute-start(bf16[272,512]{1,0:T(8,128)(2,1)S(1)} %copy-done.24), channel_id=1, source_target_pairs={{0,4},{2,6},{4,0},{6,2},{1,5},{3,7},{5,1},{7,3},{8,12},{10,14},{12... | collective-permute-start | bytes 835592 | tf_op jit(solution)/shard_map/ppermute | solution.py:54
  17.4 23.1 %collective-permute-start.2 = (bf16[272,512]{1,0:T(8,128)(2,1)S(1)}, bf16[272,512]{1,0:T(8,128)(2,1)S(1)}, u32[]{:S(2)}, u32[]{:S(2)}) collective-permute-start(bf16[272,512]{1,0:T(8,128)(2,1)S(1)} %copy-done.24), channel_id=1, source_target_pairs={{0,6},{2,4},{4,2},{6,0},{1,7},{3,5},{5,3},{7,1},{8,14},{10,12},{12... | collective-permute-start | bytes 835592 | tf_op jit(solution)/shard_map/ppermute | solution.py:54
  17.6 17.4 %collective-permute-start.16 = (bf16[128,1024]{1,0:T(8,128)(2,1)S(1)}, bf16[128,1024]{1,0:T(8,128)(2,1)S(1)}, u32[]{:S(2)}, u32[]{:S(2)}) collective-permute-start(bf16[128,1024]{1,0:T(8,128)(2,1)S(1)} %copy-done.25), channel_id=1, source_target_pairs={{0,16},{8,24},{16,0},{24,8},{1,17},{9,25},{17,1},{25,9},{2,18},{10... | collective-permute-start | bytes 786440 | tf_op jit(solution)/shard_map/ppermute | solution.py:54
  40.5 123.3 %reduce-scatter.2.cloned.1.call-start = ((), (), s32[]{:S(2)}) async-start(), calls=%async_computation.8 | async-start | bytes 4718592 | tf_op jit(solution)/shard_map/reduce_scatter | solution.py:648
  49.6 17.7 %collective-permute-start.10 = (bf16[1024,128]{1,0:T(8,128)(2,1)S(1)}, bf16[1024,128]{1,0:T(8,128)(2,1)S(1)}, u32[]{:S(2)}, u32[]{:S(2)}) collective-permute-start(bf16[1024,128]{1,0:T(8,128)(2,1)S(1)} %get-tuple-element.83.p0), channel_id=1, source_target_pairs={{0,24},{8,16},{16,8},{24,0},{1,25},{9,17},{17,9},{25,1},{2,26},{10... | collective-permute-start | bytes 786440 | tf_op jit(solution)/shard_map/ppermute | solution.py:54
  50.8 17.0 %collective-permute-start.9 = (bf16[1024,128]{1,0:T(8,128)(2,1)S(1)}, bf16[1024,128]{1,0:T(8,128)(2,1)S(1)}, u32[]{:S(2)}, u32[]{:S(2)}) collective-permute-start(bf16[1024,128]{1,0:T(8,128)(2,1)S(1)} %get-tuple-element.83.p0), channel_id=1, source_target_pairs={{0,16},{8,24},{16,0},{24,8},{1,17},{9,25},{17,1},{25,9},{2,18},{10... | collective-permute-start | bytes 786440 | tf_op jit(solution)/shard_map/ppermute | solution.py:54
  51.0 16.9 %collective-permute-start.8 = (bf16[1024,128]{1,0:T(8,128)(2,1)S(1)}, bf16[1024,128]{1,0:T(8,128)(2,1)S(1)}, u32[]{:S(2)}, u32[]{:S(2)}) collective-permute-start(bf16[1024,128]{1,0:T(8,128)(2,1)S(1)} %get-tuple-element.83.p0), channel_id=1, source_target_pairs={{0,8},{8,0},{16,24},{24,16},{1,9},{9,1},{17,25},{25,17},{2,10},{10... | collective-permute-start | bytes 786440 | tf_op jit(solution)/shard_map/ppermute | solution.py:54
  88.7 13.4 %collective-permute-start.18 = (bf16[512,256]{1,0:T(8,128)(2,1)S(1)}, bf16[512,256]{1,0:T(8,128)(2,1)}, u32[]{:S(2)}, u32[]{:S(2)}) collective-permute-start(bf16[512,256]{1,0:T(8,128)(2,1)S(1)} %get-tuple-element.91.a0), channel_id=1, source_target_pairs={{0,8},{8,0},{16,24},{24,16},{1,9},{9,1},{17,25},{25,17},{2,10},{10... | collective-permute-start | bytes 786440 | tf_op jit(solution)/shard_map/ppermute | solution.py:54
  89.7 12.5 %collective-permute-start.19 = (bf16[512,256]{1,0:T(8,128)(2,1)S(1)}, bf16[512,256]{1,0:T(8,128)(2,1)}, u32[]{:S(2)}, u32[]{:S(2)}) collective-permute-start(bf16[512,256]{1,0:T(8,128)(2,1)S(1)} %get-tuple-element.91.a0), channel_id=1, source_target_pairs={{0,16},{8,24},{16,0},{24,8},{1,17},{9,25},{17,1},{25,9},{2,18},{10... | collective-permute-start | bytes 786440 | tf_op jit(solution)/shard_map/ppermute | solution.py:54
  90.1 12.1 %collective-permute-start.20 = (bf16[512,256]{1,0:T(8,128)(2,1)S(1)}, bf16[512,256]{1,0:T(8,128)(2,1)}, u32[]{:S(2)}, u32[]{:S(2)}) collective-permute-start(bf16[512,256]{1,0:T(8,128)(2,1)S(1)} %get-tuple-element.91.a0), channel_id=1, source_target_pairs={{0,24},{8,16},{16,8},{24,0},{1,25},{9,17},{17,9},{25,1},{2,26},{10... | collective-permute-start | bytes 786440 | tf_op jit(solution)/shard_map/ppermute | solution.py:54
  148.6 16.7 %all-to-all-start.5 = ((bf16[4,128,1024]{2,1,0:T(8,128)(2,1)}), bf16[4,128,1024]{2,1,0:T(8,128)(2,1)S(1)}, u32[]{:S(2)}, u32[]{:S(2)}) async-start(bf16[4,128,1024]{2,1,0:T(8,128)(2,1)} %bitcast.34), calls=%async_computation.5 | async-start | bytes 2097152 | tf_op jit(solution)/shard_map/all_to_all | solution.py:658
  163.8 14.3 %collective-permute-start.23 = (bf16[2,128,1024]{2,1,0:T(8,128)(2,1)}, bf16[2,128,1024]{2,1,0:T(8,128)(2,1)}, u32[]{:S(2)}, u32[]{:S(2)}) collective-permute-start(bf16[2,128,1024]{2,1,0:T(8,128)(2,1)} %reduce-scatter.2.cloned.1.call-done.p0), channel_id=1, source_target_pairs={{0,8},{8,0},{16,24},{24,16},{1,9},{9,1},{17,25},{25,17},{2,10},{10... | collective-permute-start | bytes 1572872 | tf_op jit(solution)/shard_map/ppermute | solution.py:54
  165.3 23.7 %all-to-all-start.6 = ((bf16[4,128,1024]{2,1,0:T(8,128)(2,1)}), bf16[4,128,1024]{2,1,0:T(8,128)(2,1)S(1)}, u32[]{:S(2)}, u32[]{:S(2)}) async-start(bf16[4,128,1024]{2,1,0:T(8,128)(2,1)} %bitcast.35), calls=%async_computation.6 | async-start | bytes 2097152 | tf_op jit(solution)/shard_map/all_to_all | solution.py:696
  168.8 34.8 %collective-permute-start.24 = (bf16[2,128,1024]{2,1,0:T(8,128)(2,1)}, bf16[2,128,1024]{2,1,0:T(8,128)(2,1)}, u32[]{:S(2)}, u32[]{:S(2)}) collective-permute-start(bf16[2,128,1024]{2,1,0:T(8,128)(2,1)} %reduce-scatter.2.cloned.1.call-done.p0), channel_id=1, source_target_pairs={{0,16},{8,24},{16,0},{24,8},{1,17},{9,25},{17,1},{25,9},{2,18},{10... | collective-permute-start | bytes 1572872 | tf_op jit(solution)/shard_map/ppermute | solution.py:54
  170.2 33.3 %collective-permute-start.25 = (bf16[2,128,1024]{2,1,0:T(8,128)(2,1)}, bf16[2,128,1024]{2,1,0:T(8,128)(2,1)}, u32[]{:S(2)}, u32[]{:S(2)}) collective-permute-start(bf16[2,128,1024]{2,1,0:T(8,128)(2,1)} %reduce-scatter.2.cloned.1.call-done.p0), channel_id=1, source_target_pairs={{0,24},{8,16},{16,8},{24,0},{1,25},{9,17},{17,9},{25,1},{2,26},{10... | collective-permute-start | bytes 1572872 | tf_op jit(solution)/shard_map/ppermute | solution.py:54
  175.8 27.8 %collective-permute-start.26 = (bf16[272,512]{1,0:T(8,128)(2,1)}, bf16[272,512]{1,0:T(8,128)(2,1)}, u32[]{:S(2)}, u32[]{:S(2)}) collective-permute-start(bf16[272,512]{1,0:T(8,128)(2,1)} %get-tuple-element.122), channel_id=1, source_target_pairs={{0,2},{2,0},{4,6},{6,4},{1,3},{3,1},{5,7},{7,5},{8,10},{10,8},{12,... | collective-permute-start | bytes 835592 | tf_op jit(solution)/shard_map/ppermute | solution.py:54
  175.8 27.8 %collective-permute-start.27 = (bf16[272,512]{1,0:T(8,128)(2,1)}, bf16[272,512]{1,0:T(8,128)(2,1)}, u32[]{:S(2)}, u32[]{:S(2)}) collective-permute-start(bf16[272,512]{1,0:T(8,128)(2,1)} %get-tuple-element.123), channel_id=1, source_target_pairs={{0,4},{2,6},{4,0},{6,2},{1,5},{3,7},{5,1},{7,3},{8,12},{10,14},{12... | collective-permute-start | bytes 835592 | tf_op jit(solution)/shard_map/ppermute | solution.py:54
  178.1 25.4 %collective-permute-start.28 = (bf16[272,512]{1,0:T(8,128)(2,1)}, bf16[272,512]{1,0:T(8,128)(2,1)}, u32[]{:S(2)}, u32[]{:S(2)}) collective-permute-start(bf16[272,512]{1,0:T(8,128)(2,1)} %get-tuple-element.124), channel_id=1, source_target_pairs={{0,6},{2,4},{4,2},{6,0},{1,7},{3,5},{5,3},{7,1},{8,14},{10,12},{12... | collective-permute-start | bytes 835592 | tf_op jit(solution)/shard_map/ppermute | solution.py:54
  209.1 14.3 %collective-permute-start.30 = (bf16[272,512]{1,0:T(8,128)(2,1)S(1)}, bf16[272,512]{1,0:T(8,128)(2,1)S(1)}, u32[]{:S(2)}, u32[]{:S(2)}) collective-permute-start(bf16[272,512]{1,0:T(8,128)(2,1)S(1)} %add_convert_fusion.p0), channel_id=1, source_target_pairs={{0,16},{8,24},{16,0},{24,8},{1,17},{9,25},{17,1},{25,9},{2,18},{10... | collective-permute-start | bytes 835592 | tf_op jit(solution)/shard_map/ppermute | solution.py:54
  210.3 13.6 %collective-permute-start.29 = (bf16[272,512]{1,0:T(8,128)(2,1)S(1)}, bf16[272,512]{1,0:T(8,128)(2,1)S(1)}, u32[]{:S(2)}, u32[]{:S(2)}) collective-permute-start(bf16[272,512]{1,0:T(8,128)(2,1)S(1)} %add_convert_fusion.p0), channel_id=1, source_target_pairs={{0,8},{8,0},{16,24},{24,16},{1,9},{9,1},{17,25},{25,17},{2,10},{10... | collective-permute-start | bytes 835592 | tf_op jit(solution)/shard_map/ppermute | solution.py:54
  (69 other events, 360.3 us)
Sparse Core Ops, SparseCore 0:
  40.6 47.1 all-gather.2
  110.9 49.1 reduce-scatter.1

commit v4 on v3

--- a/solution.py
+++ b/solution.py
@@ -69,7 +69,7 @@
     return pl.ds(pl.multiple_of(start, LANE), size)
 
 
-def vmem_call(kernel, outs, args, hbm=(), staged=(), scratch=(), flops=0, limit=16, away=(), weight=8):
+def vmem_call(kernel, outs, args, hbm=(), staged=(), scratch=(), flops=0, limit=16, away=(), weight=24):
     moved = sum(a.size * a.dtype.itemsize for a in args)
     moved += sum(math.prod(s) * jnp.dtype(t).itemsize for s, t in outs)
     whole = pl.BlockSpec(memory_space=pltpu.VMEM)
@@ -695,7 +695,7 @@
     tail = over_shards(tail)
     joined = lax.all_to_all(joined, "rep", 0, 0, tiled=True)
     ff_pieces = over_rep([ff_piece] * REPS)
-    tail = joined_sum([after(tail[0], joined, block_output, *ff_pieces[1:])] + tail[1:])
+    tail = joined_sum([after(tail[0], joined, block_output)] + tail[1:])
     (input_grad,) = vmem_call(
         input_kernel, [((ROWS, WIDTH), f32)], [joined, unit_own, vectors, middle_grad]
     )

time: 238 us -> 236 us (level)
  waiting for transfers between devices: 50.1 us -> 47.7 us
    all_to_all x1, waiting for transfers between devices: 9.18 us -> 1.95 us  [tiled_body(): joined = lax.all_to_all(joined, 'rep', 0, 0, tiled=True)]
    ppermute x40, waiting for transfers between devices: 40.8 us -> 44.3 us  [swap(): return lax.ppermute(value, axis, [(i, i ^ offset) for i in range(size)])]
  transfers between devices with their start and end apart: 45 -> 45, of which waited for: 14 -> 17; matrix products, arithmetic and copies ran while one was open for 1% -> 1% of each run, Pallas kernels for 16% -> 16%
where the time goes in v4:
time: 236 us; the launch traced here: 235 us
  Pallas kernels  48.7 us (21%)
  starting transfers between devices  48.3 us (20%)
  waiting for transfers between devices  47.7 us (20%)
  blocking collectives  47.2 us (20%)
  local copies, waits for them, and re-layouts  26.6 us (11%)
  between operations  14.5 us (6%)
    pallas_call x16, Pallas kernels, vmem_call(): pl.pallas_call(body if staged else kernel, out_shape=[jax.ShapeDtypeStruc...  48.7 us
    ppermute x40, waiting for transfers between devices, swap(): return lax.ppermute(value, axis, [(i, i ^ offset) for i in range(size)])  44.3 us
    ppermute x40, starting transfers between devices, swap(): return lax.ppermute(value, axis, [(i, i ^ offset) for i in range(size)])  37.3 us
    unnamed x100, local copies, waits for them, and re-layouts  25 us
    all_to_all x1, blocking collectives, tiled_body(): normed_two = lax.all_to_all(normed_two, 'rep', 0, 0, tiled=True)  15.8 us
    all_to_all x1, blocking collectives, tiled_body(): back = lax.all_to_all(back, 'rep', 0, 0, tiled=True)  13.9 us
    all_to_all x1, blocking collectives, tiled_body(): mine = lax.all_to_all(attended, 'rep', 0, 0, tiled=True)  9.15 us
    all_to_all x1, blocking collectives, tiled_body(): pairs = lax.all_to_all(pairs, 'rep', 0, 0, tiled=True)  8.38 us
  transfers between devices with their start and end apart: 45, of which 17 were waited for; matrix products, arithmetic and copies ran while one was open for 1% of the time, Pallas kernels for 16%

profile of v4, /device:TPU:9, one launch (start us, length us, event | category | flops | bytes accessed | tf_op | source)
XLA Modules:
  0.0 235.0 jit_solution(10444640254929539284)
XLA Ops:
  7.2 2.6 %shard_map.245 = (bf16[272,512]{1,0:T(8,128)(2,1)}, bf16[512,1024]{1,0:T(8,128)(2,1)}) custom-call(bf16[256,3072]{1,0:T(8,128)(2,1)} %refs_0_.1, bf16[256,1024]{1,0:T(8,128)(2,1)} %refs_1_.1, bf16[128,1024]{1,0:T(8,128)(2,1)} %x.1, bf16[256]{0:T(256)(128)(2,1)} %refs_3_.1, bf16[256]{0:T(256)(128)(2,1)} %refs_4_.1, bf16[512]{0:T(512)(128)(2,1)} %refs_5_.1, ...), custom_call_target="tpu_custom_call" | custom-call | bytes 88621056 | tf_op jit(solution)/shard_map/pallas_call | solution.py:95
  9.8 3.7 %all-to-all-start = ((bf16[4,128,1024]{2,1,0:T(8,128)(2,1)}), bf16[4,128,1024]{2,1,0:T(8,128)(2,1)S(1)}, u32[]{:S(2)}, u32[]{:S(2)}) async-start(bf16[4,128,1024]{2,1,0:T(8,128)(2,1)} %bitcast.46), calls=%async_computation | async-start | bytes 2097152 | tf_op jit(solution)/shard_map/all_to_all | solution.py:565
  18.8 13.1 %collective-permute-done.15.c1 = bf16[128,1024]{1,0:T(8,128)(2,1)S(1)} collective-permute-done((bf16[128,1024]{1,0:T(8,128)(2,1)S(1)}, bf16[128,1024]{1,0:T(8,128)(2,1)S(1)}, u32[]{:S(2)}, u32[]{:S(2)}) %collective-permute-start.15) | collective-permute-done | bytes 262176 | tf_op jit(solution)/shard_map/ppermute | solution.py:54
  34.9 3.9 %collective-permute-done.17.c3 = bf16[128,1024]{1,0:T(8,128)(2,1)S(1)} collective-permute-done((bf16[128,1024]{1,0:T(8,128)(2,1)S(1)}, bf16[128,1024]{1,0:T(8,128)(2,1)S(1)}, u32[]{:S(2)}, u32[]{:S(2)}) %collective-permute-start.17) | collective-permute-done | bytes 262176 | tf_op jit(solution)/shard_map/ppermute | solution.py:54
  40.6 2.7 %collective-permute-start.3 = (bf16[272,512]{1,0:T(8,128)(2,1)S(1)}, bf16[272,512]{1,0:T(8,128)(2,1)S(1)}, u32[]{:S(2)}, u32[]{:S(2)}) collective-permute-start(bf16[272,512]{1,0:T(8,128)(2,1)S(1)} %copy-done.24), channel_id=1, source_target_pairs={{0,1},{1,0},{2,3},{3,2},{4,5},{5,4},{6,7},{7,6},{8,9},{9,8},{10,11... | collective-permute-start | bytes 835592 | tf_op jit(solution)/shard_map/ppermute | solution.py:54
  52.3 5.6 %shard_map.248 = (bf16[512,256]{1,0:T(8,128)(2,1)S(1)}, f32[512,128]{1,0:T(8,128)S(1)}) custom-call(bf16[512,768]{1,0:T(8,128)(2,1)S(1)} %get-tuple-element.79.qkv, bf16[512,512]{1,0:T(8,128)(2,1)S(1)} %collective-permute-done.7.far), custom_call_target="tpu_custom_call" | custom-call | flops 3221225472 | bytes 44040192 | tf_op jit(solution)/shard_map/pallas_call | solution.py:95
  58.0 9.2 %all_to_all.77 = bf16[4,128,256]{2,1,0:T(8,128)(2,1)S(1)} all-to-all(bf16[4,128,256]{2,1,0:T(8,128)(2,1)S(1)} %bitcast.42), channel_id=1, replica_groups=mesh['rep'=4,'fsdp'=4,'seq'=2] {'rep'}, dimensions={0} | all-to-all | bytes 524288 | tf_op jit(solution)/shard_map/all_to_all | solution.py:601
  72.8 15.8 %all_to_all.78 = bf16[4,128,1024]{2,1,0:T(8,128)(2,1)S(1)} all-to-all(bf16[4,128,1024]{2,1,0:T(8,128)(2,1)S(1)} %bitcast.39), channel_id=1, replica_groups=mesh['rep'=4,'fsdp'=4,'seq'=2] {'rep'}, dimensions={0} | all-to-all | bytes 2097152 | tf_op jit(solution)/shard_map/all_to_all | solution.py:618
  97.3 4.8 %shard_map.250 = (bf16[512,1024]{1,0:T(8,128)(2,1)S(1)}, bf16[512,1024]{1,0:T(8,128)(2,1)S(1)}, bf16[512,1024]{1,0:T(8,128)(2,1)S(1)}, bf16[512,1024]{1,0:T(8,128)(2,1)S(1)}) custom-call(bf16[512,1024]{1,0:T(8,128)(2,1)S(1)} %bitcast.36, bf16[128,1024]{1,0:T(8,128)(2,1)S(1)} %copy-done.26, bf16[128,1024]{1,0:T(8,128)(2,1)S(1)} %copy-done.29, ...), custom_call_target="tpu_custom_call" | custom-call | flops 77309411328 | bytes 253231104 | tf_op jit(solution)/shard_map/pallas_call | solution.py:95
  102.1 4.9 %shard_map.251 = (bf16[512,1024]{1,0:T(8,128)(2,1)S(1)}, bf16[16,128,1024]{2,1,0:T(8,128)(2,1)S(1)}, f32[8,1024]{1,0:T(8,128)S(1)}) custom-call(bf16[512,1024]{1,0:T(8,128)(2,1)S(1)} %get-tuple-element.92.hidden, bf16[512,1024]{1,0:T(8,128)(2,1)S(1)} %get-tuple-element.93.pre_grad, bf16[512,1024]{1,0:T(8,128)(2,1)S(1)} %bitcast.37, ...), custom_call_target="tpu_custom_call" | custom-call | flops 77309411328 | bytes 327942144 | tf_op jit(solution)/shard_map/pallas_call | solution.py:95
  110.7 13.9 %all_to_all.79 = bf16[4,128,1024]{2,1,0:T(8,128)(2,1)S(1)} all-to-all(bf16[4,128,1024]{2,1,0:T(8,128)(2,1)S(1)} %bitcast.38), channel_id=1, replica_groups=mesh['rep'=4,'fsdp'=4,'seq'=2] {'rep'}, dimensions={0} | all-to-all | bytes 2097152 | tf_op jit(solution)/shard_map/all_to_all | solution.py:632
  127.5 8.4 %all_to_all.80 = bf16[4,128,512]{2,1,0:T(8,128)(2,1)S(1)} all-to-all(bf16[4,128,512]{2,1,0:T(8,128)(2,1)S(1)} %bitcast.41), channel_id=1, replica_groups=mesh['rep'=4,'fsdp'=4,'seq'=2] {'rep'}, dimensions={0} | all-to-all | bytes 1048576 | tf_op jit(solution)/shard_map/all_to_all | solution.py:657
  135.9 6.7 %shard_map.254 = (bf16[512,256]{1,0:T(8,128)(2,1)S(1)}, f32[512,512]{1,0:T(8,128)S(1)}, bf16[512,512]{1,0:T(8,128)(2,1)}) custom-call(bf16[512,768]{1,0:T(8,128)(2,1)S(1)} %copy-done.6, bf16[512,512]{1,0:T(8,128)(2,1)S(1)} %copy-done.12, f32[512,128]{1,0:T(8,128)S(1)} %copy-done.16, bf16[512,512]{1,0:T(8,128)(2,1)S(1)} %bitcast.32), custom_call_target="tpu_custom_call" | custom-call | flops 335544320 | bytes 3932160 | tf_op jit(solution)/shard_map/pallas_call | solution.py:95
  143.6 4.9 %collective-permute-start.21 = (bf16[512,512]{1,0:T(8,128)(2,1)}, bf16[512,512]{1,0:T(8,128)(2,1)}, u32[]{:S(2)}, u32[]{:S(2)}) collective-permute-start(bf16[512,512]{1,0:T(8,128)(2,1)} %get-tuple-element.106), channel_id=1, source_target_pairs={{0,1},{1,0},{2,3},{3,2},{4,5},{5,4},{6,7},{7,6},{8,9},{9,8},{10,11... | collective-permute-start | bytes 1572872 | tf_op jit(solution)/shard_map/ppermute | solution.py:54
  148.5 3.7 %all-to-all-start.5 = ((bf16[4,128,1024]{2,1,0:T(8,128)(2,1)}), bf16[4,128,1024]{2,1,0:T(8,128)(2,1)S(1)}, u32[]{:S(2)}, u32[]{:S(2)}) async-start(bf16[4,128,1024]{2,1,0:T(8,128)(2,1)} %bitcast.34), calls=%async_computation.5 | async-start | bytes 2097152 | tf_op jit(solution)/shard_map/all_to_all | solution.py:658
  155.3 5.1 %shard_map.256 = (bf16[4,256,512]{2,1,0:T(8,128)(2,1)S(1)}, bf16[4,256,512]{2,1,0:T(8,128)(2,1)}, bf16[512,1024]{1,0:T(8,128)(2,1)S(1)}, f32[4,16,512]{2,1,0:T(8,128)S(1)}) custom-call(bf16[512,256]{1,0:T(8,128)(2,1)S(1)} %copy-done.35, f32[512,512]{1,0:T(8,128)S(1)} %copy-done.23, bf16[512,512]{1,0:T(8,128)(2,1)} %collective-permute-done.21.far_grad, ...), custom_call_target="tpu_custom_call" | custom-call | flops 38654705664 | bytes 250085376 | tf_op jit(solution)/shard_map/pallas_call | solution.py:95
  165.1 3.5 %all-to-all-start.6 = ((bf16[4,128,1024]{2,1,0:T(8,128)(2,1)}), bf16[4,128,1024]{2,1,0:T(8,128)(2,1)S(1)}, u32[]{:S(2)}, u32[]{:S(2)}) async-start(bf16[4,128,1024]{2,1,0:T(8,128)(2,1)} %bitcast.35), calls=%async_computation.6 | async-start | bytes 2097152 | tf_op jit(solution)/shard_map/all_to_all | solution.py:696
  173.0 2.4 %collective-permute-start.24 = (bf16[272,512]{1,0:T(8,128)(2,1)}, bf16[272,512]{1,0:T(8,128)(2,1)}, u32[]{:S(2)}, u32[]{:S(2)}) collective-permute-start(bf16[272,512]{1,0:T(8,128)(2,1)} %get-tuple-element.122), channel_id=1, source_target_pairs={{0,4},{2,6},{4,0},{6,2},{1,5},{3,7},{5,1},{7,3},{8,12},{10,14},{12... | collective-permute-start | bytes 835592 | tf_op jit(solution)/shard_map/ppermute | solution.py:54
  182.9 4.0 %collective-permute-done.24 = bf16[272,512]{1,0:T(8,128)(2,1)} collective-permute-done((bf16[272,512]{1,0:T(8,128)(2,1)}, bf16[272,512]{1,0:T(8,128)(2,1)}, u32[]{:S(2)}, u32[]{:S(2)}) %collective-permute-start.24) | collective-permute-done | bytes 278560 | tf_op jit(solution)/shard_map/ppermute | solution.py:54
  186.9 12.0 %collective-permute-done.25 = bf16[272,512]{1,0:T(8,128)(2,1)} collective-permute-done((bf16[272,512]{1,0:T(8,128)(2,1)}, bf16[272,512]{1,0:T(8,128)(2,1)}, u32[]{:S(2)}, u32[]{:S(2)}) %collective-permute-start.25) | collective-permute-done | bytes 278560 | tf_op jit(solution)/shard_map/ppermute | solution.py:54
  200.1 2.7 %collective-permute-start.32 = (bf16[2,128,1024]{2,1,0:T(8,128)(2,1)}, bf16[2,128,1024]{2,1,0:T(8,128)(2,1)S(1)}, u32[]{:S(2)}, u32[]{:S(2)}) collective-permute-start(bf16[2,128,1024]{2,1,0:T(8,128)(2,1)} %reduce-scatter.2.cloned.1.call-done.p0), channel_id=1, source_target_pairs={{0,1},{1,0},{2,3},{3,2},{4,5},{5,4},{6,7},{7,6},{8,9},{9,8},{10,11... | collective-permute-start | bytes 1572872 | tf_op jit(solution)/shard_map/ppermute | solution.py:54
  211.0 5.0 %shard_map.259 = (f32[1024,1024]{1,0:T(8,128)}, f32[1024,1024]{1,0:T(8,128)}) custom-call(bf16[2,128,1024]{2,1,0:T(8,128)(2,1)S(1)} %copy-done.13, bf16[2,128,1024]{2,1,0:T(8,128)(2,1)S(1)} %collective-permute-done.29.p1, bf16[2,128,1024]{2,1,0:T(8,128)(2,1)S(1)} %collective-permute-done.30.p2, bf16[2,128,1024]{2,1,0:T(8,128)(2,1)} %collective-permute-done.31.p3, ...), custom_call_target="tpu_custom_call" | custom-call | bytes 301989888 | tf_op jit(solution)/shard_map/pallas_call | solution.py:95
  217.3 4.0 %collective-permute-done.27.p2 = bf16[272,512]{1,0:T(8,128)(2,1)S(1)} collective-permute-done((bf16[272,512]{1,0:T(8,128)(2,1)S(1)}, bf16[272,512]{1,0:T(8,128)(2,1)S(1)}, u32[]{:S(2)}, u32[]{:S(2)}) %collective-permute-start.27) | collective-permute-done | bytes 278560 | tf_op jit(solution)/shard_map/ppermute | solution.py:54
  223.9 2.5 %shard_map.260 = (f32[256,3072]{1,0:T(8,128)}, f32[256,1024]{1,0:T(8,128)}, f32[16,256]{1,0:T(8,128)S(1)}) custom-call(bf16[272,512]{1,0:T(8,128)(2,1)S(1)} %add_convert_fusion.p0, bf16[272,512]{1,0:T(8,128)(2,1)S(1)} %collective-permute-done.26.p1, bf16[272,512]{1,0:T(8,128)(2,1)S(1)} %collective-permute-done.27.p2, ...), custom_call_target="tpu_custom_call" | custom-call | bytes 154533888 | tf_op jit(solution)/shard_map/pallas_call | solution.py:95
  (192 shorter events, 75.5 us)
Async XLA Ops:
  9.8 30.7 %all-to-all-start = ((bf16[4,128,1024]{2,1,0:T(8,128)(2,1)}), bf16[4,128,1024]{2,1,0:T(8,128)(2,1)S(1)}, u32[]{:S(2)}, u32[]{:S(2)}) async-start(bf16[4,128,1024]{2,1,0:T(8,128)(2,1)} %bitcast.46), calls=%async_computation | async-start | bytes 2097152 | tf_op jit(solution)/shard_map/all_to_all | solution.py:565
  13.5 77.8 %all-gather.3.cloned.1.call-start = ((), (), s32[]{:S(2)}) async-start(), calls=%async_computation.9 | async-start | bytes 4718592 | tf_op jit(solution)/shard_map/all_gather | solution.py:577
  13.5 18.3 %collective-permute-start.15 = (bf16[128,1024]{1,0:T(8,128)(2,1)S(1)}, bf16[128,1024]{1,0:T(8,128)(2,1)S(1)}, u32[]{:S(2)}, u32[]{:S(2)}) collective-permute-start(bf16[128,1024]{1,0:T(8,128)(2,1)S(1)} %copy-done.25), channel_id=1, source_target_pairs={{0,8},{8,0},{16,24},{24,16},{1,9},{9,1},{17,25},{25,17},{2,10},{10... | collective-permute-start | bytes 786440 | tf_op jit(solution)/shard_map/ppermute | solution.py:54
  14.9 23.9 %collective-permute-start = (bf16[272,512]{1,0:T(8,128)(2,1)S(1)}, bf16[272,512]{1,0:T(8,128)(2,1)S(1)}, u32[]{:S(2)}, u32[]{:S(2)}) collective-permute-start(bf16[272,512]{1,0:T(8,128)(2,1)S(1)} %copy-done.24), channel_id=1, source_target_pairs={{0,2},{2,0},{4,6},{6,4},{1,3},{3,1},{5,7},{7,5},{8,10},{10,8},{12,... | collective-permute-start | bytes 835592 | tf_op jit(solution)/shard_map/ppermute | solution.py:54
  15.0 23.8 %collective-permute-start.1 = (bf16[272,512]{1,0:T(8,128)(2,1)S(1)}, bf16[272,512]{1,0:T(8,128)(2,1)S(1)}, u32[]{:S(2)}, u32[]{:S(2)}) collective-permute-start(bf16[272,512]{1,0:T(8,128)(2,1)S(1)} %copy-done.24), channel_id=1, source_target_pairs={{0,4},{2,6},{4,0},{6,2},{1,5},{3,7},{5,1},{7,3},{8,12},{10,14},{12... | collective-permute-start | bytes 835592 | tf_op jit(solution)/shard_map/ppermute | solution.py:54
  17.4 23.1 %collective-permute-start.2 = (bf16[272,512]{1,0:T(8,128)(2,1)S(1)}, bf16[272,512]{1,0:T(8,128)(2,1)S(1)}, u32[]{:S(2)}, u32[]{:S(2)}) collective-permute-start(bf16[272,512]{1,0:T(8,128)(2,1)S(1)} %copy-done.24), channel_id=1, source_target_pairs={{0,6},{2,4},{4,2},{6,0},{1,7},{3,5},{5,3},{7,1},{8,14},{10,12},{12... | collective-permute-start | bytes 835592 | tf_op jit(solution)/shard_map/ppermute | solution.py:54
  17.6 17.4 %collective-permute-start.16 = (bf16[128,1024]{1,0:T(8,128)(2,1)S(1)}, bf16[128,1024]{1,0:T(8,128)(2,1)S(1)}, u32[]{:S(2)}, u32[]{:S(2)}) collective-permute-start(bf16[128,1024]{1,0:T(8,128)(2,1)S(1)} %copy-done.25), channel_id=1, source_target_pairs={{0,16},{8,24},{16,0},{24,8},{1,17},{9,25},{17,1},{25,9},{2,18},{10... | collective-permute-start | bytes 786440 | tf_op jit(solution)/shard_map/ppermute | solution.py:54
  40.5 135.1 %reduce-scatter.2.cloned.1.call-start = ((), (), s32[]{:S(2)}) async-start(), calls=%async_computation.8 | async-start | bytes 4718592 | tf_op jit(solution)/shard_map/reduce_scatter | solution.py:648
  49.6 17.5 %collective-permute-start.10 = (bf16[1024,128]{1,0:T(8,128)(2,1)S(1)}, bf16[1024,128]{1,0:T(8,128)(2,1)S(1)}, u32[]{:S(2)}, u32[]{:S(2)}) collective-permute-start(bf16[1024,128]{1,0:T(8,128)(2,1)S(1)} %get-tuple-element.83.p0), channel_id=1, source_target_pairs={{0,24},{8,16},{16,8},{24,0},{1,25},{9,17},{17,9},{25,1},{2,26},{10... | collective-permute-start | bytes 786440 | tf_op jit(solution)/shard_map/ppermute | solution.py:54
  50.8 16.9 %collective-permute-start.9 = (bf16[1024,128]{1,0:T(8,128)(2,1)S(1)}, bf16[1024,128]{1,0:T(8,128)(2,1)S(1)}, u32[]{:S(2)}, u32[]{:S(2)}) collective-permute-start(bf16[1024,128]{1,0:T(8,128)(2,1)S(1)} %get-tuple-element.83.p0), channel_id=1, source_target_pairs={{0,16},{8,24},{16,0},{24,8},{1,17},{9,25},{17,1},{25,9},{2,18},{10... | collective-permute-start | bytes 786440 | tf_op jit(solution)/shard_map/ppermute | solution.py:54
  51.0 16.8 %collective-permute-start.8 = (bf16[1024,128]{1,0:T(8,128)(2,1)S(1)}, bf16[1024,128]{1,0:T(8,128)(2,1)S(1)}, u32[]{:S(2)}, u32[]{:S(2)}) collective-permute-start(bf16[1024,128]{1,0:T(8,128)(2,1)S(1)} %get-tuple-element.83.p0), channel_id=1, source_target_pairs={{0,8},{8,0},{16,24},{24,16},{1,9},{9,1},{17,25},{25,17},{2,10},{10... | collective-permute-start | bytes 786440 | tf_op jit(solution)/shard_map/ppermute | solution.py:54
  88.7 13.4 %collective-permute-start.18 = (bf16[512,256]{1,0:T(8,128)(2,1)S(1)}, bf16[512,256]{1,0:T(8,128)(2,1)}, u32[]{:S(2)}, u32[]{:S(2)}) collective-permute-start(bf16[512,256]{1,0:T(8,128)(2,1)S(1)} %get-tuple-element.91.a0), channel_id=1, source_target_pairs={{0,8},{8,0},{16,24},{24,16},{1,9},{9,1},{17,25},{25,17},{2,10},{10... | collective-permute-start | bytes 786440 | tf_op jit(solution)/shard_map/ppermute | solution.py:54
  89.6 12.5 %collective-permute-start.19 = (bf16[512,256]{1,0:T(8,128)(2,1)S(1)}, bf16[512,256]{1,0:T(8,128)(2,1)}, u32[]{:S(2)}, u32[]{:S(2)}) collective-permute-start(bf16[512,256]{1,0:T(8,128)(2,1)S(1)} %get-tuple-element.91.a0), channel_id=1, source_target_pairs={{0,16},{8,24},{16,0},{24,8},{1,17},{9,25},{17,1},{25,9},{2,18},{10... | collective-permute-start | bytes 786440 | tf_op jit(solution)/shard_map/ppermute | solution.py:54
  90.0 12.1 %collective-permute-start.20 = (bf16[512,256]{1,0:T(8,128)(2,1)S(1)}, bf16[512,256]{1,0:T(8,128)(2,1)}, u32[]{:S(2)}, u32[]{:S(2)}) collective-permute-start(bf16[512,256]{1,0:T(8,128)(2,1)S(1)} %get-tuple-element.91.a0), channel_id=1, source_target_pairs={{0,24},{8,16},{16,8},{24,0},{1,25},{9,17},{17,9},{25,1},{2,26},{10... | collective-permute-start | bytes 786440 | tf_op jit(solution)/shard_map/ppermute | solution.py:54
  143.6 10.5 %collective-permute-start.21 = (bf16[512,512]{1,0:T(8,128)(2,1)}, bf16[512,512]{1,0:T(8,128)(2,1)}, u32[]{:S(2)}, u32[]{:S(2)}) collective-permute-start(bf16[512,512]{1,0:T(8,128)(2,1)} %get-tuple-element.106), channel_id=1, source_target_pairs={{0,1},{1,0},{2,3},{3,2},{4,5},{5,4},{6,7},{7,6},{8,9},{9,8},{10,11... | collective-permute-start | bytes 1572872 | tf_op jit(solution)/shard_map/ppermute | solution.py:54
  148.5 16.6 %all-to-all-start.5 = ((bf16[4,128,1024]{2,1,0:T(8,128)(2,1)}), bf16[4,128,1024]{2,1,0:T(8,128)(2,1)S(1)}, u32[]{:S(2)}, u32[]{:S(2)}) async-start(bf16[4,128,1024]{2,1,0:T(8,128)(2,1)} %bitcast.34), calls=%async_computation.5 | async-start | bytes 2097152 | tf_op jit(solution)/shard_map/all_to_all | solution.py:658
  165.1 16.7 %all-to-all-start.6 = ((bf16[4,128,1024]{2,1,0:T(8,128)(2,1)}), bf16[4,128,1024]{2,1,0:T(8,128)(2,1)S(1)}, u32[]{:S(2)}, u32[]{:S(2)}) async-start(bf16[4,128,1024]{2,1,0:T(8,128)(2,1)} %bitcast.35), calls=%async_computation.6 | async-start | bytes 2097152 | tf_op jit(solution)/shard_map/all_to_all | solution.py:696
  173.0 13.9 %collective-permute-start.24 = (bf16[272,512]{1,0:T(8,128)(2,1)}, bf16[272,512]{1,0:T(8,128)(2,1)}, u32[]{:S(2)}, u32[]{:S(2)}) collective-permute-start(bf16[272,512]{1,0:T(8,128)(2,1)} %get-tuple-element.122), channel_id=1, source_target_pairs={{0,4},{2,6},{4,0},{6,2},{1,5},{3,7},{5,1},{7,3},{8,12},{10,14},{12... | collective-permute-start | bytes 835592 | tf_op jit(solution)/shard_map/ppermute | solution.py:54
  175.3 23.5 %collective-permute-start.25 = (bf16[272,512]{1,0:T(8,128)(2,1)}, bf16[272,512]{1,0:T(8,128)(2,1)}, u32[]{:S(2)}, u32[]{:S(2)}) collective-permute-start(bf16[272,512]{1,0:T(8,128)(2,1)} %get-tuple-element.123), channel_id=1, source_target_pairs={{0,6},{2,4},{4,2},{6,0},{1,7},{3,5},{5,3},{7,1},{8,14},{10,12},{12... | collective-permute-start | bytes 835592 | tf_op jit(solution)/shard_map/ppermute | solution.py:54
  175.6 27.2 %collective-permute-start.31 = (bf16[2,128,1024]{2,1,0:T(8,128)(2,1)}, bf16[2,128,1024]{2,1,0:T(8,128)(2,1)}, u32[]{:S(2)}, u32[]{:S(2)}) collective-permute-start(bf16[2,128,1024]{2,1,0:T(8,128)(2,1)} %reduce-scatter.2.cloned.1.call-done.p0), channel_id=1, source_target_pairs={{0,24},{8,16},{16,8},{24,0},{1,25},{9,17},{17,9},{25,1},{2,26},{10... | collective-permute-start | bytes 1572872 | tf_op jit(solution)/shard_map/ppermute | solution.py:54
  181.8 23.3 %collective-permute-start.30 = (bf16[2,128,1024]{2,1,0:T(8,128)(2,1)}, bf16[2,128,1024]{2,1,0:T(8,128)(2,1)S(1)}, u32[]{:S(2)}, u32[]{:S(2)}) collective-permute-start(bf16[2,128,1024]{2,1,0:T(8,128)(2,1)} %reduce-scatter.2.cloned.1.call-done.p0), channel_id=1, source_target_pairs={{0,16},{8,24},{16,0},{24,8},{1,17},{9,25},{17,1},{25,9},{2,18},{10... | collective-permute-start | bytes 1572872 | tf_op jit(solution)/shard_map/ppermute | solution.py:54
  182.2 24.0 %collective-permute-start.29 = (bf16[2,128,1024]{2,1,0:T(8,128)(2,1)}, bf16[2,128,1024]{2,1,0:T(8,128)(2,1)S(1)}, u32[]{:S(2)}, u32[]{:S(2)}) collective-permute-start(bf16[2,128,1024]{2,1,0:T(8,128)(2,1)} %reduce-scatter.2.cloned.1.call-done.p0), channel_id=1, source_target_pairs={{0,8},{8,0},{16,24},{24,16},{1,9},{9,1},{17,25},{25,17},{2,10},{10... | collective-permute-start | bytes 1572872 | tf_op jit(solution)/shard_map/ppermute | solution.py:54
  206.9 14.4 %collective-permute-start.27 = (bf16[272,512]{1,0:T(8,128)(2,1)S(1)}, bf16[272,512]{1,0:T(8,128)(2,1)S(1)}, u32[]{:S(2)}, u32[]{:S(2)}) collective-permute-start(bf16[272,512]{1,0:T(8,128)(2,1)S(1)} %add_convert_fusion.p0), channel_id=1, source_target_pairs={{0,16},{8,24},{16,0},{24,8},{1,17},{9,25},{17,1},{25,9},{2,18},{10... | collective-permute-start | bytes 835592 | tf_op jit(solution)/shard_map/ppermute | solution.py:54
  208.0 13.9 %collective-permute-start.26 = (bf16[272,512]{1,0:T(8,128)(2,1)S(1)}, bf16[272,512]{1,0:T(8,128)(2,1)S(1)}, u32[]{:S(2)}, u32[]{:S(2)}) collective-permute-start(bf16[272,512]{1,0:T(8,128)(2,1)S(1)} %add_convert_fusion.p0), channel_id=1, source_target_pairs={{0,8},{8,0},{16,24},{24,16},{1,9},{9,1},{17,25},{25,17},{2,10},{10... | collective-permute-start | bytes 835592 | tf_op jit(solution)/shard_map/ppermute | solution.py:54
  (69 other events, 357.2 us)
Sparse Core Ops, SparseCore 0:
  40.6 47.1 all-gather.2
  110.8 49.1 reduce-scatter.1

commit v5 on v4

--- a/solution.py
+++ b/solution.py
@@ -435,8 +435,8 @@
         far[k, :, TRIPLE:] = proj_far[k]
     gain = jnp.zeros((1, WIDTH), f32)
     shift = jnp.zeros((1, WIDTH), f32)
-    for k in range(REPS):
-        at = pl.ds(k * ROWS, ROWS)
+    for k in range(2):
+        at = pl.ds(k * 2 * ROWS, 2 * ROWS)
         back = dot_rows(mixed[at, :], weight[...])
         joined[at, :] = back.astype(bf16)
         gain = gain + jnp.sum(back * unit[at, :], 0, keepdims=True)

time: 236 us -> 236 us (level)
  no operation moved by 1% of the time
where the time goes in v5:
time: 236 us; the launch traced here: 235 us
  waiting for transfers between devices  48.8 us (21%)
  starting transfers between devices  48.3 us (20%)
  Pallas kernels  47.6 us (20%)
  blocking collectives  47.2 us (20%)
  local copies, waits for them, and re-layouts  26.6 us (11%)
  between operations  14.5 us (6%)
    pallas_call x16, Pallas kernels, vmem_call(): pl.pallas_call(body if staged else kernel, out_shape=[jax.ShapeDtypeStruc...  47.6 us
    ppermute x40, waiting for transfers between devices, swap(): return lax.ppermute(value, axis, [(i, i ^ offset) for i in range(size)])  44.3 us
    ppermute x40, starting transfers between devices, swap(): return lax.ppermute(value, axis, [(i, i ^ offset) for i in range(size)])  37.3 us
    unnamed x100, local copies, waits for them, and re-layouts  25 us
    all_to_all x1, blocking collectives, tiled_body(): normed_two = lax.all_to_all(normed_two, 'rep', 0, 0, tiled=True)  15.8 us
    all_to_all x1, blocking collectives, tiled_body(): back = lax.all_to_all(back, 'rep', 0, 0, tiled=True)  13.9 us
    all_to_all x1, blocking collectives, tiled_body(): mine = lax.all_to_all(attended, 'rep', 0, 0, tiled=True)  9.15 us
    all_to_all x1, blocking collectives, tiled_body(): pairs = lax.all_to_all(pairs, 'rep', 0, 0, tiled=True)  8.38 us
  transfers between devices with their start and end apart: 45, of which 17 were waited for; matrix products, arithmetic and copies ran while one was open for 1% of the time, Pallas kernels for 16%

profile of v5, /device:TPU:9, one launch (start us, length us, event | category | flops | bytes accessed | tf_op | source)
XLA Modules:
  0.0 235.0 jit_solution(2329835582395591619)
XLA Ops:
  7.2 2.6 %shard_map.245 = (bf16[272,512]{1,0:T(8,128)(2,1)}, bf16[512,1024]{1,0:T(8,128)(2,1)}) custom-call(bf16[256,3072]{1,0:T(8,128)(2,1)} %refs_0_.1, bf16[256,1024]{1,0:T(8,128)(2,1)} %refs_1_.1, bf16[128,1024]{1,0:T(8,128)(2,1)} %x.1, bf16[256]{0:T(256)(128)(2,1)} %refs_3_.1, bf16[256]{0:T(256)(128)(2,1)} %refs_4_.1, bf16[512]{0:T(512)(128)(2,1)} %refs_5_.1, ...), custom_call_target="tpu_custom_call" | custom-call | bytes 88621056 | tf_op jit(solution)/shard_map/pallas_call | solution.py:95
  9.8 3.7 %all-to-all-start = ((bf16[4,128,1024]{2,1,0:T(8,128)(2,1)}), bf16[4,128,1024]{2,1,0:T(8,128)(2,1)S(1)}, u32[]{:S(2)}, u32[]{:S(2)}) async-start(bf16[4,128,1024]{2,1,0:T(8,128)(2,1)} %bitcast.46), calls=%async_computation | async-start | bytes 2097152 | tf_op jit(solution)/shard_map/all_to_all | solution.py:565
  18.8 13.1 %collective-permute-done.15.c1 = bf16[128,1024]{1,0:T(8,128)(2,1)S(1)} collective-permute-done((bf16[128,1024]{1,0:T(8,128)(2,1)S(1)}, bf16[128,1024]{1,0:T(8,128)(2,1)S(1)}, u32[]{:S(2)}, u32[]{:S(2)}) %collective-permute-start.15) | collective-permute-done | bytes 262176 | tf_op jit(solution)/shard_map/ppermute | solution.py:54
  34.9 3.9 %collective-permute-done.17.c3 = bf16[128,1024]{1,0:T(8,128)(2,1)S(1)} collective-permute-done((bf16[128,1024]{1,0:T(8,128)(2,1)S(1)}, bf16[128,1024]{1,0:T(8,128)(2,1)S(1)}, u32[]{:S(2)}, u32[]{:S(2)}) %collective-permute-start.17) | collective-permute-done | bytes 262176 | tf_op jit(solution)/shard_map/ppermute | solution.py:54
  40.6 2.7 %collective-permute-start.3 = (bf16[272,512]{1,0:T(8,128)(2,1)S(1)}, bf16[272,512]{1,0:T(8,128)(2,1)S(1)}, u32[]{:S(2)}, u32[]{:S(2)}) collective-permute-start(bf16[272,512]{1,0:T(8,128)(2,1)S(1)} %copy-done.24), channel_id=1, source_target_pairs={{0,1},{1,0},{2,3},{3,2},{4,5},{5,4},{6,7},{7,6},{8,9},{9,8},{10,11... | collective-permute-start | bytes 835592 | tf_op jit(solution)/shard_map/ppermute | solution.py:54
  52.3 5.6 %shard_map.248 = (bf16[512,256]{1,0:T(8,128)(2,1)S(1)}, f32[512,128]{1,0:T(8,128)S(1)}) custom-call(bf16[512,768]{1,0:T(8,128)(2,1)S(1)} %get-tuple-element.79.qkv, bf16[512,512]{1,0:T(8,128)(2,1)S(1)} %collective-permute-done.7.far), custom_call_target="tpu_custom_call" | custom-call | flops 3221225472 | bytes 44040192 | tf_op jit(solution)/shard_map/pallas_call | solution.py:95
  58.0 9.2 %all_to_all.77 = bf16[4,128,256]{2,1,0:T(8,128)(2,1)S(1)} all-to-all(bf16[4,128,256]{2,1,0:T(8,128)(2,1)S(1)} %bitcast.42), channel_id=1, replica_groups=mesh['rep'=4,'fsdp'=4,'seq'=2] {'rep'}, dimensions={0} | all-to-all | bytes 524288 | tf_op jit(solution)/shard_map/all_to_all | solution.py:601
  72.8 15.8 %all_to_all.78 = bf16[4,128,1024]{2,1,0:T(8,128)(2,1)S(1)} all-to-all(bf16[4,128,1024]{2,1,0:T(8,128)(2,1)S(1)} %bitcast.39), channel_id=1, replica_groups=mesh['rep'=4,'fsdp'=4,'seq'=2] {'rep'}, dimensions={0} | all-to-all | bytes 2097152 | tf_op jit(solution)/shard_map/all_to_all | solution.py:618
  97.3 4.8 %shard_map.250 = (bf16[512,1024]{1,0:T(8,128)(2,1)S(1)}, bf16[512,1024]{1,0:T(8,128)(2,1)S(1)}, bf16[512,1024]{1,0:T(8,128)(2,1)S(1)}, bf16[512,1024]{1,0:T(8,128)(2,1)S(1)}) custom-call(bf16[512,1024]{1,0:T(8,128)(2,1)S(1)} %bitcast.36, bf16[128,1024]{1,0:T(8,128)(2,1)S(1)} %copy-done.26, bf16[128,1024]{1,0:T(8,128)(2,1)S(1)} %copy-done.29, ...), custom_call_target="tpu_custom_call" | custom-call | flops 77309411328 | bytes 253231104 | tf_op jit(solution)/shard_map/pallas_call | solution.py:95
  102.1 4.9 %shard_map.251 = (bf16[512,1024]{1,0:T(8,128)(2,1)S(1)}, bf16[16,128,1024]{2,1,0:T(8,128)(2,1)S(1)}, f32[8,1024]{1,0:T(8,128)S(1)}) custom-call(bf16[512,1024]{1,0:T(8,128)(2,1)S(1)} %get-tuple-element.92.hidden, bf16[512,1024]{1,0:T(8,128)(2,1)S(1)} %get-tuple-element.93.pre_grad, bf16[512,1024]{1,0:T(8,128)(2,1)S(1)} %bitcast.37, ...), custom_call_target="tpu_custom_call" | custom-call | flops 77309411328 | bytes 327942144 | tf_op jit(solution)/shard_map/pallas_call | solution.py:95
  110.7 13.9 %all_to_all.79 = bf16[4,128,1024]{2,1,0:T(8,128)(2,1)S(1)} all-to-all(bf16[4,128,1024]{2,1,0:T(8,128)(2,1)S(1)} %bitcast.38), channel_id=1, replica_groups=mesh['rep'=4,'fsdp'=4,'seq'=2] {'rep'}, dimensions={0} | all-to-all | bytes 2097152 | tf_op jit(solution)/shard_map/all_to_all | solution.py:632
  127.5 8.4 %all_to_all.80 = bf16[4,128,512]{2,1,0:T(8,128)(2,1)S(1)} all-to-all(bf16[4,128,512]{2,1,0:T(8,128)(2,1)S(1)} %bitcast.41), channel_id=1, replica_groups=mesh['rep'=4,'fsdp'=4,'seq'=2] {'rep'}, dimensions={0} | all-to-all | bytes 1048576 | tf_op jit(solution)/shard_map/all_to_all | solution.py:657
  135.9 6.7 %shard_map.254 = (bf16[512,256]{1,0:T(8,128)(2,1)S(1)}, f32[512,512]{1,0:T(8,128)S(1)}, bf16[512,512]{1,0:T(8,128)(2,1)}) custom-call(bf16[512,768]{1,0:T(8,128)(2,1)S(1)} %copy-done.6, bf16[512,512]{1,0:T(8,128)(2,1)S(1)} %copy-done.12, f32[512,128]{1,0:T(8,128)S(1)} %copy-done.16, bf16[512,512]{1,0:T(8,128)(2,1)S(1)} %bitcast.32), custom_call_target="tpu_custom_call" | custom-call | flops 335544320 | bytes 3932160 | tf_op jit(solution)/shard_map/pallas_call | solution.py:95
  143.6 4.9 %collective-permute-start.21 = (bf16[512,512]{1,0:T(8,128)(2,1)}, bf16[512,512]{1,0:T(8,128)(2,1)}, u32[]{:S(2)}, u32[]{:S(2)}) collective-permute-start(bf16[512,512]{1,0:T(8,128)(2,1)} %get-tuple-element.106), channel_id=1, source_target_pairs={{0,1},{1,0},{2,3},{3,2},{4,5},{5,4},{6,7},{7,6},{8,9},{9,8},{10,11... | collective-permute-start | bytes 1572872 | tf_op jit(solution)/shard_map/ppermute | solution.py:54
  148.5 3.7 %all-to-all-start.5 = ((bf16[4,128,1024]{2,1,0:T(8,128)(2,1)}), bf16[4,128,1024]{2,1,0:T(8,128)(2,1)S(1)}, u32[]{:S(2)}, u32[]{:S(2)}) async-start(bf16[4,128,1024]{2,1,0:T(8,128)(2,1)} %bitcast.34), calls=%async_computation.5 | async-start | bytes 2097152 | tf_op jit(solution)/shard_map/all_to_all | solution.py:658
  155.3 4.0 %shard_map.256 = (bf16[4,256,512]{2,1,0:T(8,128)(2,1)S(1)}, bf16[4,256,512]{2,1,0:T(8,128)(2,1)}, bf16[512,1024]{1,0:T(8,128)(2,1)S(1)}, f32[4,16,512]{2,1,0:T(8,128)S(1)}) custom-call(bf16[512,256]{1,0:T(8,128)(2,1)S(1)} %copy-done.35, f32[512,512]{1,0:T(8,128)S(1)} %copy-done.23, bf16[512,512]{1,0:T(8,128)(2,1)} %collective-permute-done.21.far_grad, ...), custom_call_target="tpu_custom_call" | custom-call | flops 38654705664 | bytes 250085376 | tf_op jit(solution)/shard_map/pallas_call | solution.py:95
  162.6 2.5 %all-to-all-done.5 = bf16[4,128,1024]{2,1,0:T(8,128)(2,1)S(1)} async-done(((bf16[4,128,1024]{2,1,0:T(8,128)(2,1)}), bf16[4,128,1024]{2,1,0:T(8,128)(2,1)S(1)}, u32[]{:S(2)}, u32[]{:S(2)}) %all-to-all-start.5) | async-done | bytes 1048608 | tf_op jit(solution)/shard_map/all_to_all | solution.py:658
  165.1 3.5 %all-to-all-start.6 = ((bf16[4,128,1024]{2,1,0:T(8,128)(2,1)}), bf16[4,128,1024]{2,1,0:T(8,128)(2,1)S(1)}, u32[]{:S(2)}, u32[]{:S(2)}) async-start(bf16[4,128,1024]{2,1,0:T(8,128)(2,1)} %bitcast.35), calls=%async_computation.6 | async-start | bytes 2097152 | tf_op jit(solution)/shard_map/all_to_all | solution.py:696
  182.9 4.0 %collective-permute-done.24 = bf16[272,512]{1,0:T(8,128)(2,1)} collective-permute-done((bf16[272,512]{1,0:T(8,128)(2,1)}, bf16[272,512]{1,0:T(8,128)(2,1)}, u32[]{:S(2)}, u32[]{:S(2)}) %collective-permute-start.24) | collective-permute-done | bytes 278560 | tf_op jit(solution)/shard_map/ppermute | solution.py:54
  186.9 12.0 %collective-permute-done.25 = bf16[272,512]{1,0:T(8,128)(2,1)} collective-permute-done((bf16[272,512]{1,0:T(8,128)(2,1)}, bf16[272,512]{1,0:T(8,128)(2,1)}, u32[]{:S(2)}, u32[]{:S(2)}) %collective-permute-start.25) | collective-permute-done | bytes 278560 | tf_op jit(solution)/shard_map/ppermute | solution.py:54
  200.1 2.7 %collective-permute-start.32 = (bf16[2,128,1024]{2,1,0:T(8,128)(2,1)}, bf16[2,128,1024]{2,1,0:T(8,128)(2,1)S(1)}, u32[]{:S(2)}, u32[]{:S(2)}) collective-permute-start(bf16[2,128,1024]{2,1,0:T(8,128)(2,1)} %reduce-scatter.2.cloned.1.call-done.p0), channel_id=1, source_target_pairs={{0,1},{1,0},{2,3},{3,2},{4,5},{5,4},{6,7},{7,6},{8,9},{9,8},{10,11... | collective-permute-start | bytes 1572872 | tf_op jit(solution)/shard_map/ppermute | solution.py:54
  211.0 5.0 %shard_map.259 = (f32[1024,1024]{1,0:T(8,128)}, f32[1024,1024]{1,0:T(8,128)}) custom-call(bf16[2,128,1024]{2,1,0:T(8,128)(2,1)S(1)} %copy-done.13, bf16[2,128,1024]{2,1,0:T(8,128)(2,1)S(1)} %collective-permute-done.29.p1, bf16[2,128,1024]{2,1,0:T(8,128)(2,1)S(1)} %collective-permute-done.30.p2, bf16[2,128,1024]{2,1,0:T(8,128)(2,1)} %collective-permute-done.31.p3, ...), custom_call_target="tpu_custom_call" | custom-call | bytes 301989888 | tf_op jit(solution)/shard_map/pallas_call | solution.py:95
  217.3 4.0 %collective-permute-done.27.p2 = bf16[272,512]{1,0:T(8,128)(2,1)S(1)} collective-permute-done((bf16[272,512]{1,0:T(8,128)(2,1)S(1)}, bf16[272,512]{1,0:T(8,128)(2,1)S(1)}, u32[]{:S(2)}, u32[]{:S(2)}) %collective-permute-start.27) | collective-permute-done | bytes 278560 | tf_op jit(solution)/shard_map/ppermute | solution.py:54
  223.9 2.5 %shard_map.260 = (f32[256,3072]{1,0:T(8,128)}, f32[256,1024]{1,0:T(8,128)}, f32[16,256]{1,0:T(8,128)S(1)}) custom-call(bf16[272,512]{1,0:T(8,128)(2,1)S(1)} %add_convert_fusion.p0, bf16[272,512]{1,0:T(8,128)(2,1)S(1)} %collective-permute-done.26.p1, bf16[272,512]{1,0:T(8,128)(2,1)S(1)} %collective-permute-done.27.p2, ...), custom_call_target="tpu_custom_call" | custom-call | bytes 154533888 | tf_op jit(solution)/shard_map/pallas_call | solution.py:95
  (192 shorter events, 76.5 us)
Async XLA Ops:
  9.8 30.7 %all-to-all-start = ((bf16[4,128,1024]{2,1,0:T(8,128)(2,1)}), bf16[4,128,1024]{2,1,0:T(8,128)(2,1)S(1)}, u32[]{:S(2)}, u32[]{:S(2)}) async-start(bf16[4,128,1024]{2,1,0:T(8,128)(2,1)} %bitcast.46), calls=%async_computation | async-start | bytes 2097152 | tf_op jit(solution)/shard_map/all_to_all | solution.py:565
  13.5 77.8 %all-gather.3.cloned.1.call-start = ((), (), s32[]{:S(2)}) async-start(), calls=%async_computation.9 | async-start | bytes 4718592 | tf_op jit(solution)/shard_map/all_gather | solution.py:577
  13.5 18.3 %collective-permute-start.15 = (bf16[128,1024]{1,0:T(8,128)(2,1)S(1)}, bf16[128,1024]{1,0:T(8,128)(2,1)S(1)}, u32[]{:S(2)}, u32[]{:S(2)}) collective-permute-start(bf16[128,1024]{1,0:T(8,128)(2,1)S(1)} %copy-done.25), channel_id=1, source_target_pairs={{0,8},{8,0},{16,24},{24,16},{1,9},{9,1},{17,25},{25,17},{2,10},{10... | collective-permute-start | bytes 786440 | tf_op jit(solution)/shard_map/ppermute | solution.py:54
  14.9 23.9 %collective-permute-start = (bf16[272,512]{1,0:T(8,128)(2,1)S(1)}, bf16[272,512]{1,0:T(8,128)(2,1)S(1)}, u32[]{:S(2)}, u32[]{:S(2)}) collective-permute-start(bf16[272,512]{1,0:T(8,128)(2,1)S(1)} %copy-done.24), channel_id=1, source_target_pairs={{0,2},{2,0},{4,6},{6,4},{1,3},{3,1},{5,7},{7,5},{8,10},{10,8},{12,... | collective-permute-start | bytes 835592 | tf_op jit(solution)/shard_map/ppermute | solution.py:54
  15.0 23.8 %collective-permute-start.1 = (bf16[272,512]{1,0:T(8,128)(2,1)S(1)}, bf16[272,512]{1,0:T(8,128)(2,1)S(1)}, u32[]{:S(2)}, u32[]{:S(2)}) collective-permute-start(bf16[272,512]{1,0:T(8,128)(2,1)S(1)} %copy-done.24), channel_id=1, source_target_pairs={{0,4},{2,6},{4,0},{6,2},{1,5},{3,7},{5,1},{7,3},{8,12},{10,14},{12... | collective-permute-start | bytes 835592 | tf_op jit(solution)/shard_map/ppermute | solution.py:54
  17.4 23.1 %collective-permute-start.2 = (bf16[272,512]{1,0:T(8,128)(2,1)S(1)}, bf16[272,512]{1,0:T(8,128)(2,1)S(1)}, u32[]{:S(2)}, u32[]{:S(2)}) collective-permute-start(bf16[272,512]{1,0:T(8,128)(2,1)S(1)} %copy-done.24), channel_id=1, source_target_pairs={{0,6},{2,4},{4,2},{6,0},{1,7},{3,5},{5,3},{7,1},{8,14},{10,12},{12... | collective-permute-start | bytes 835592 | tf_op jit(solution)/shard_map/ppermute | solution.py:54
  17.6 17.4 %collective-permute-start.16 = (bf16[128,1024]{1,0:T(8,128)(2,1)S(1)}, bf16[128,1024]{1,0:T(8,128)(2,1)S(1)}, u32[]{:S(2)}, u32[]{:S(2)}) collective-permute-start(bf16[128,1024]{1,0:T(8,128)(2,1)S(1)} %copy-done.25), channel_id=1, source_target_pairs={{0,16},{8,24},{16,0},{24,8},{1,17},{9,25},{17,1},{25,9},{2,18},{10... | collective-permute-start | bytes 786440 | tf_op jit(solution)/shard_map/ppermute | solution.py:54
  40.5 135.1 %reduce-scatter.2.cloned.1.call-start = ((), (), s32[]{:S(2)}) async-start(), calls=%async_computation.8 | async-start | bytes 4718592 | tf_op jit(solution)/shard_map/reduce_scatter | solution.py:648
  49.6 17.5 %collective-permute-start.10 = (bf16[1024,128]{1,0:T(8,128)(2,1)S(1)}, bf16[1024,128]{1,0:T(8,128)(2,1)S(1)}, u32[]{:S(2)}, u32[]{:S(2)}) collective-permute-start(bf16[1024,128]{1,0:T(8,128)(2,1)S(1)} %get-tuple-element.83.p0), channel_id=1, source_target_pairs={{0,24},{8,16},{16,8},{24,0},{1,25},{9,17},{17,9},{25,1},{2,26},{10... | collective-permute-start | bytes 786440 | tf_op jit(solution)/shard_map/ppermute | solution.py:54
  50.8 16.9 %collective-permute-start.9 = (bf16[1024,128]{1,0:T(8,128)(2,1)S(1)}, bf16[1024,128]{1,0:T(8,128)(2,1)S(1)}, u32[]{:S(2)}, u32[]{:S(2)}) collective-permute-start(bf16[1024,128]{1,0:T(8,128)(2,1)S(1)} %get-tuple-element.83.p0), channel_id=1, source_target_pairs={{0,16},{8,24},{16,0},{24,8},{1,17},{9,25},{17,1},{25,9},{2,18},{10... | collective-permute-start | bytes 786440 | tf_op jit(solution)/shard_map/ppermute | solution.py:54
  51.0 16.8 %collective-permute-start.8 = (bf16[1024,128]{1,0:T(8,128)(2,1)S(1)}, bf16[1024,128]{1,0:T(8,128)(2,1)S(1)}, u32[]{:S(2)}, u32[]{:S(2)}) collective-permute-start(bf16[1024,128]{1,0:T(8,128)(2,1)S(1)} %get-tuple-element.83.p0), channel_id=1, source_target_pairs={{0,8},{8,0},{16,24},{24,16},{1,9},{9,1},{17,25},{25,17},{2,10},{10... | collective-permute-start | bytes 786440 | tf_op jit(solution)/shard_map/ppermute | solution.py:54
  88.7 13.4 %collective-permute-start.18 = (bf16[512,256]{1,0:T(8,128)(2,1)S(1)}, bf16[512,256]{1,0:T(8,128)(2,1)}, u32[]{:S(2)}, u32[]{:S(2)}) collective-permute-start(bf16[512,256]{1,0:T(8,128)(2,1)S(1)} %get-tuple-element.91.a0), channel_id=1, source_target_pairs={{0,8},{8,0},{16,24},{24,16},{1,9},{9,1},{17,25},{25,17},{2,10},{10... | collective-permute-start | bytes 786440 | tf_op jit(solution)/shard_map/ppermute | solution.py:54
  89.6 12.5 %collective-permute-start.19 = (bf16[512,256]{1,0:T(8,128)(2,1)S(1)}, bf16[512,256]{1,0:T(8,128)(2,1)}, u32[]{:S(2)}, u32[]{:S(2)}) collective-permute-start(bf16[512,256]{1,0:T(8,128)(2,1)S(1)} %get-tuple-element.91.a0), channel_id=1, source_target_pairs={{0,16},{8,24},{16,0},{24,8},{1,17},{9,25},{17,1},{25,9},{2,18},{10... | collective-permute-start | bytes 786440 | tf_op jit(solution)/shard_map/ppermute | solution.py:54
  90.0 12.1 %collective-permute-start.20 = (bf16[512,256]{1,0:T(8,128)(2,1)S(1)}, bf16[512,256]{1,0:T(8,128)(2,1)}, u32[]{:S(2)}, u32[]{:S(2)}) collective-permute-start(bf16[512,256]{1,0:T(8,128)(2,1)S(1)} %get-tuple-element.91.a0), channel_id=1, source_target_pairs={{0,24},{8,16},{16,8},{24,0},{1,25},{9,17},{17,9},{25,1},{2,26},{10... | collective-permute-start | bytes 786440 | tf_op jit(solution)/shard_map/ppermute | solution.py:54
  143.6 10.5 %collective-permute-start.21 = (bf16[512,512]{1,0:T(8,128)(2,1)}, bf16[512,512]{1,0:T(8,128)(2,1)}, u32[]{:S(2)}, u32[]{:S(2)}) collective-permute-start(bf16[512,512]{1,0:T(8,128)(2,1)} %get-tuple-element.106), channel_id=1, source_target_pairs={{0,1},{1,0},{2,3},{3,2},{4,5},{5,4},{6,7},{7,6},{8,9},{9,8},{10,11... | collective-permute-start | bytes 1572872 | tf_op jit(solution)/shard_map/ppermute | solution.py:54
  148.5 16.6 %all-to-all-start.5 = ((bf16[4,128,1024]{2,1,0:T(8,128)(2,1)}), bf16[4,128,1024]{2,1,0:T(8,128)(2,1)S(1)}, u32[]{:S(2)}, u32[]{:S(2)}) async-start(bf16[4,128,1024]{2,1,0:T(8,128)(2,1)} %bitcast.34), calls=%async_computation.5 | async-start | bytes 2097152 | tf_op jit(solution)/shard_map/all_to_all | solution.py:658
  165.1 16.7 %all-to-all-start.6 = ((bf16[4,128,1024]{2,1,0:T(8,128)(2,1)}), bf16[4,128,1024]{2,1,0:T(8,128)(2,1)S(1)}, u32[]{:S(2)}, u32[]{:S(2)}) async-start(bf16[4,128,1024]{2,1,0:T(8,128)(2,1)} %bitcast.35), calls=%async_computation.6 | async-start | bytes 2097152 | tf_op jit(solution)/shard_map/all_to_all | solution.py:696
  173.0 13.9 %collective-permute-start.24 = (bf16[272,512]{1,0:T(8,128)(2,1)}, bf16[272,512]{1,0:T(8,128)(2,1)}, u32[]{:S(2)}, u32[]{:S(2)}) collective-permute-start(bf16[272,512]{1,0:T(8,128)(2,1)} %get-tuple-element.122), channel_id=1, source_target_pairs={{0,4},{2,6},{4,0},{6,2},{1,5},{3,7},{5,1},{7,3},{8,12},{10,14},{12... | collective-permute-start | bytes 835592 | tf_op jit(solution)/shard_map/ppermute | solution.py:54
  175.3 23.5 %collective-permute-start.25 = (bf16[272,512]{1,0:T(8,128)(2,1)}, bf16[272,512]{1,0:T(8,128)(2,1)}, u32[]{:S(2)}, u32[]{:S(2)}) collective-permute-start(bf16[272,512]{1,0:T(8,128)(2,1)} %get-tuple-element.123), channel_id=1, source_target_pairs={{0,6},{2,4},{4,2},{6,0},{1,7},{3,5},{5,3},{7,1},{8,14},{10,12},{12... | collective-permute-start | bytes 835592 | tf_op jit(solution)/shard_map/ppermute | solution.py:54
  175.6 27.2 %collective-permute-start.31 = (bf16[2,128,1024]{2,1,0:T(8,128)(2,1)}, bf16[2,128,1024]{2,1,0:T(8,128)(2,1)}, u32[]{:S(2)}, u32[]{:S(2)}) collective-permute-start(bf16[2,128,1024]{2,1,0:T(8,128)(2,1)} %reduce-scatter.2.cloned.1.call-done.p0), channel_id=1, source_target_pairs={{0,24},{8,16},{16,8},{24,0},{1,25},{9,17},{17,9},{25,1},{2,26},{10... | collective-permute-start | bytes 1572872 | tf_op jit(solution)/shard_map/ppermute | solution.py:54
  181.8 23.3 %collective-permute-start.30 = (bf16[2,128,1024]{2,1,0:T(8,128)(2,1)}, bf16[2,128,1024]{2,1,0:T(8,128)(2,1)S(1)}, u32[]{:S(2)}, u32[]{:S(2)}) collective-permute-start(bf16[2,128,1024]{2,1,0:T(8,128)(2,1)} %reduce-scatter.2.cloned.1.call-done.p0), channel_id=1, source_target_pairs={{0,16},{8,24},{16,0},{24,8},{1,17},{9,25},{17,1},{25,9},{2,18},{10... | collective-permute-start | bytes 1572872 | tf_op jit(solution)/shard_map/ppermute | solution.py:54
  182.2 24.0 %collective-permute-start.29 = (bf16[2,128,1024]{2,1,0:T(8,128)(2,1)}, bf16[2,128,1024]{2,1,0:T(8,128)(2,1)S(1)}, u32[]{:S(2)}, u32[]{:S(2)}) collective-permute-start(bf16[2,128,1024]{2,1,0:T(8,128)(2,1)} %reduce-scatter.2.cloned.1.call-done.p0), channel_id=1, source_target_pairs={{0,8},{8,0},{16,24},{24,16},{1,9},{9,1},{17,25},{25,17},{2,10},{10... | collective-permute-start | bytes 1572872 | tf_op jit(solution)/shard_map/ppermute | solution.py:54
  206.9 14.4 %collective-permute-start.27 = (bf16[272,512]{1,0:T(8,128)(2,1)S(1)}, bf16[272,512]{1,0:T(8,128)(2,1)S(1)}, u32[]{:S(2)}, u32[]{:S(2)}) collective-permute-start(bf16[272,512]{1,0:T(8,128)(2,1)S(1)} %add_convert_fusion.p0), channel_id=1, source_target_pairs={{0,16},{8,24},{16,0},{24,8},{1,17},{9,25},{17,1},{25,9},{2,18},{10... | collective-permute-start | bytes 835592 | tf_op jit(solution)/shard_map/ppermute | solution.py:54
  208.0 13.9 %collective-permute-start.26 = (bf16[272,512]{1,0:T(8,128)(2,1)S(1)}, bf16[272,512]{1,0:T(8,128)(2,1)S(1)}, u32[]{:S(2)}, u32[]{:S(2)}) collective-permute-start(bf16[272,512]{1,0:T(8,128)(2,1)S(1)} %add_convert_fusion.p0), channel_id=1, source_target_pairs={{0,8},{8,0},{16,24},{24,16},{1,9},{9,1},{17,25},{25,17},{2,10},{10... | collective-permute-start | bytes 835592 | tf_op jit(solution)/shard_map/ppermute | solution.py:54
  (69 other events, 358.3 us)
Sparse Core Ops, SparseCore 0:
  40.6 47.1 all-gather.2
  110.8 49.1 reduce-scatter.1
